TPU v7x, 128 devices: a whole 4x4x4 slice. The times are simulated.
128 devices in a mesh: space: 4 (over x), kx: 4 (over y_hi, core), ky: 8 (over y_lo, z).
Axes of the slice: x: 4, y: 4 (y_hi: 2, y_lo: 2; y = y_hi * 2 + y_lo), z: 4, core: 2. Of those that a mesh axis runs over, the one named last changes fastest.
Arguments:
- action: float32 [64, 64, 64, 256], P('kx', 'ky', 'space'), may hold values from 0.05 to 2
- depth_cm: int32 [64, 256], P('space'), may hold values from 120 to 599
- inflow_mask: int32 [64, 256], P('space'), may hold values 0 or 1
- inflow: float32 [64, 64], replicated, may hold values from 0.05 to 2
Outputs:
- action_next: float32 [64, 64, 64, 256], P('kx', 'ky', 'space')
All inputs are finite; a program needn't handle non-finite values. No bound on the sum of `inflow_mask` on one device may be relied on, other than what follows from the above.
Results may differ from a plain program's by a relative error of at most 0.035.
Values sent between devices are 32-bit elements; how exact they have to be, the bound alone decides.
No kernel may reach another device: no remote copies, remote signals or barrier semaphores. Data moves between devices by JAX's collectives and lax.ppermute only.
A program may use at most 128 MiB of HBM per device.

v0:
```python
import jax
import jax.numpy as jnp
from jax import lax
from jax.sharding import PartitionSpec as P

NKX = 64
NKY = 64


gravity = 9.81
spacing = 4.0
k_step = 0.04
time_step = 0.2


def padded_2(cells, sides, width):
    for axis, dim in sides:
        count = lax.axis_size(axis)
        ends = count - 1
        head = lax.slice_in_dim(cells, 0, width, axis=dim)
        tail = lax.slice_in_dim(cells, cells.shape[dim] - width, cells.shape[dim], axis=dim)
        cells = jnp.concatenate(
            [
                lax.ppermute(tail, axis, [(i, (i + 1) % count) for i in range(ends)]),
                cells,
                lax.ppermute(head, axis, [((i + 1) % count, i) for i in range(ends)]),
            ],
            axis=dim,
        )
    return cells


def group_speed(kx_value, ky_value, depth_m):
    modulus = jnp.sqrt(kx_value * kx_value + ky_value * ky_value)
    tangent = jnp.tanh(modulus * depth_m)
    frequency = jnp.sqrt(gravity * modulus * tangent)
    damping = 1.0 - tangent * tangent
    return gravity * (tangent + modulus * depth_m * damping) / (2.0 * frequency * modulus)


def refraction(kx_value, ky_value, depth_m):
    modulus = jnp.sqrt(kx_value * kx_value + ky_value * ky_value)
    tangent = jnp.tanh(modulus * depth_m)
    frequency = jnp.sqrt(gravity * modulus * tangent)
    damping = 1.0 - tangent * tangent
    return gravity * modulus * modulus * damping / (2.0 * frequency)


def centred(extended, kept_dim):
    for dimension in range(4):
        if dimension != kept_dim:
            extended = lax.slice_in_dim(extended, 2, extended.shape[dimension] - 2, axis=dimension)
    return extended


def upwind(padded, velocity, along_dim):
    extent = padded.shape[along_dim] - 4

    def section(first_cell, cell_count):
        return lax.slice_in_dim(padded, first_cell, first_cell + cell_count, axis=along_dim)

    left_side = 1.5 * section(1, extent + 1) - 0.5 * section(0, extent + 1)
    right_side = 1.5 * section(2, extent + 1) - 0.5 * section(3, extent + 1)
    face_flux = jnp.maximum(velocity, 0.0) * left_side + jnp.minimum(velocity, 0.0) * right_side
    return lax.slice_in_dim(face_flux, 1, extent + 1, axis=along_dim) - lax.slice_in_dim(
        face_flux, 0, extent, axis=along_dim
    )


def tendency(padded, depth_pad, kx_first, ky_first):
    extended = jnp.pad(padded, ((0, 0), (0, 0), (0, 0), (2, 2)))
    kx_rows = padded.shape[0] - 4
    ky_rows = padded.shape[1] - 4
    kx_centre = (
        (kx_first + jnp.arange(kx_rows, dtype=jnp.int32) - NKX // 2).astype(jnp.float32) + 0.5
    ) * k_step
    kx_face = (kx_first + jnp.arange(kx_rows + 1, dtype=jnp.int32) - NKX // 2).astype(
        jnp.float32
    ) * k_step
    ky_centre = (
        (ky_first + jnp.arange(ky_rows, dtype=jnp.int32) - NKY // 2).astype(jnp.float32) + 0.5
    ) * k_step
    ky_face = (ky_first + jnp.arange(ky_rows + 1, dtype=jnp.int32) - NKY // 2).astype(
        jnp.float32
    ) * k_step
    kx_centre = kx_centre.reshape(-1, 1, 1, 1)
    kx_face = kx_face.reshape(-1, 1, 1, 1)
    ky_centre = ky_centre.reshape(1, -1, 1, 1)
    ky_face = ky_face.reshape(1, -1, 1, 1)
    depth_centre = depth_pad[1:-1, 1:-1][None, None]
    depth_xface = (0.5 * (depth_pad[:-1, 1:-1] + depth_pad[1:, 1:-1]))[None, None]
    depth_yface = (0.5 * (depth_pad[1:-1, :-1] + depth_pad[1:-1, 1:]))[None, None]
    slope_x = ((depth_pad[2:, 1:-1] - depth_pad[:-2, 1:-1]) / (2.0 * spacing))[None, None]
    slope_y = ((depth_pad[1:-1, 2:] - depth_pad[1:-1, :-2]) / (2.0 * spacing))[None, None]
    speed_x = group_speed(kx_centre, ky_centre, depth_xface) * kx_centre
    speed_y = group_speed(kx_centre, ky_centre, depth_yface) * ky_centre
    speed_kx = -refraction(kx_face, ky_centre, depth_centre) * slope_x
    speed_ky = -refraction(kx_centre, ky_face, depth_centre) * slope_y
    total = upwind(centred(extended, 2), speed_x, 2) / spacing
    total = total + upwind(centred(extended, 3), speed_y, 3) / spacing
    total = total + upwind(centred(extended, 0), speed_kx, 0) / k_step
    total = total + upwind(centred(extended, 1), speed_ky, 1) / k_step
    return -total


def hold(values, mask_rows, spectrum):
    return jnp.where(mask_rows[None, None] == 1, spectrum[:, :, None, None], values)


def extend(values, rim_width):
    return padded_2(values, (("space", 2), ("kx", 0), ("ky", 1)), rim_width)


def bed_levels(rim_depth, x_start, x_total, rim_width):
    heights = rim_depth.astype(jnp.float32) * 0.01
    row_index = jnp.clip(
        x_start - rim_width + jnp.arange(heights.shape[0], dtype=jnp.int32), 0, x_total - 1
    ) - (x_start - rim_width)
    heights = jnp.take(heights, row_index, axis=0)
    return jnp.pad(heights, ((0, 0), (1, 1)), mode="edge")


def per_device(action, depth_cm, inflow_mask, inflow):
    kx_rows, ky_rows, x_rows, y_rows = action.shape
    kx_start = lax.axis_index("kx") * kx_rows
    ky_start = lax.axis_index("ky") * ky_rows
    x_start = lax.axis_index("space") * x_rows
    x_total = x_rows * lax.axis_size("space")
    local_spectrum = lax.dynamic_slice(inflow, (kx_start, ky_start), (kx_rows, ky_rows))
    rim_depth = padded_2(depth_cm, (("space", 0),), 1)
    depth_pad = bed_levels(rim_depth, x_start, x_total, 1)
    segment_one = hold(
        action + time_step * tendency(extend(action, 2), depth_pad, kx_start, ky_start),
        inflow_mask,
        local_spectrum,
    )
    second = tendency(extend(segment_one, 2), depth_pad, kx_start, ky_start)
    return hold(0.5 * (action + segment_one + time_step * second), inflow_mask, local_spectrum)


def solution(mesh):
    in_specs = (P("kx", "ky", "space", None), P("space", None), P("space", None), P())
    out_specs = P("kx", "ky", "space", None)
    return jax.shard_map(
        per_device, mesh=mesh, in_specs=in_specs, out_specs=out_specs, check_vma=False
    )
```

profile of v0, /device:TPU:15, one launch (start us, length us, event | category | flops | bytes accessed | tf_op | source)
XLA Modules:
  0.0 161.8 jit_solution(3804408822375373076)
XLA Ops:
  0.0 1.9 %fusion.106 = (f32[16,8,2,256]{3,2,1,0:T(2,128)S(1)}, f32[16,8,2,256]{3,2,1,0:T(2,128)S(1)}) fusion(f32[16,8,16,256]{3,2,1,0:T(8,128)} %param.4), kind=kLoop, calls=%fused_computation.227 | loop fusion | bytes 1048576 | tf_op jit(solution)/shard_map/slice | solution.py:21
  1.9 2.5 %collective-permute-start.3 = (f32[16,8,2,256]{3,1,2,0:T(8,128)S(1)}, f32[16,8,2,256]{3,1,2,0:T(8,128)S(1)}, u32[]{:S(2)}, u32[]{:S(2)}) collective-permute-start(f32[16,8,2,256]{3,1,2,0:T(8,128)S(1)} %copy.26), channel_id=1, source_target_pairs={{32,0},{64,32},{96,64},{33,1},{65,33},{97,65},{34,2},{66,34},{98,6... | collective-permute-start | bytes 786440 | tf_op jit(solution)/shard_map/ppermute | solution.py:26
  4.5 1.3 collective-permute-start.2
  5.8 0.7 fusion.108
  6.5 4.0 %collective-permute-start.1 = (s32[1,256]{1,0:T(1,128)S(1)}, s32[1,256]{1,0:T(1,128)S(1)}, u32[]{:S(2)}, u32[]{:S(2)}) collective-permute-start(s32[1,256]{1,0:T(1,128)S(1)} %get-tuple-element.29), channel_id=1, source_target_pairs={{32,0},{64,32},{96,64},{33,1},{65,33},{97,65},{34,2},{66,34},{98,6... | collective-permute-start | bytes 3080 | tf_op jit(solution)/shard_map/ppermute | solution.py:26
  10.5 1.3 collective-permute-start
  11.8 1.7 %constant_dynamic-update-slice_fusion.1 = f32[16,8,18,256]{3,2,1,0:T(8,128)} fusion(f32[16,8,16,256]{3,2,1,0:T(8,128)S(1)} %copy-done), kind=kLoop, calls=%fused_computation.215 | loop fusion | bytes 4194304
  13.8 0.8 dynamic_slice.3
  14.6 0.2 collective-permute-done
  14.8 0.6 gather_fusion
  15.7 0.1 copy.14
  15.9 1.0 constant_dynamic-update-slice_fusion
  17.0 4.8 %collective-permute-start.5 = (f32[2,8,20,256]{3,2,1,0:T(8,128)S(1)}, f32[2,8,20,256]{3,2,1,0:T(8,128)S(1)}, u32[]{:S(2)}, u32[]{:S(2)}) collective-permute-start(f32[2,8,20,256]{3,2,1,0:T(8,128)S(1)} %get-tuple-element.16), channel_id=1, source_target_pairs={{8,0},{16,8},{24,16},{9,1},{17,9},{25,17},{10,2},{18,10},{26,18},{... | collective-permute-start | bytes 983048 | tf_op jit(solution)/shard_map/ppermute | solution.py:26
  21.8 3.8 %collective-permute-start.4 = (f32[2,8,20,256]{3,2,1,0:T(8,128)S(1)}, f32[2,8,20,256]{3,2,1,0:T(8,128)S(1)}, u32[]{:S(2)}, u32[]{:S(2)}) collective-permute-start(f32[2,8,20,256]{3,2,1,0:T(8,128)S(1)} %get-tuple-element.15), channel_id=1, source_target_pairs={{0,8},{8,16},{16,24},{1,9},{9,17},{17,25},{2,10},{10,18},{18,26},{... | collective-permute-start | bytes 983048 | tf_op jit(solution)/shard_map/ppermute | solution.py:24
  25.6 4.4 %fusion.38 = f32[16,8,17,256]{3,2,1,0:T(8,128)S(1)} fusion(f32[16,8,18,256]{3,2,1,0:T(8,128)S(1)} %copy-done.1, f32[16,8,16,256]{3,2,1,0:T(8,128)S(1)} %copy-done, f32[16,8,2,256]{3,2,1,0:T(2,128)S(1)} %copy.14, f32[16]{0:T(128)S(1)} %add_multiply_fusion.1, f32[16,8]{1,0:T(8,128)S(1)} %get-tuple-element.31, f32[16,8]{1,0:T(8,128)S(1)} %get-tuple-element.32, ...), kind=kLoop, calls=%fused_computation.74 | loop fusion | flops 12812288 | bytes 9062976 | tf_op jit(solution)/shard_map/add | solution.py:64
  30.0 0.3 collective-permute-done.4
  30.3 0.3 pad_maximum_fusion.34
  30.7 6.5 %collective-permute-start.7 = (f32[20,2,20,256]{3,2,1,0:T(8,128)S(1)}, f32[20,2,20,256]{3,2,1,0:T(8,128)S(1)}, u32[]{:S(2)}, u32[]{:S(2)}) collective-permute-start(f32[20,2,20,256]{3,2,1,0:T(8,128)S(1)} %get-tuple-element.8), channel_id=1, source_target_pairs={{1,0},{2,1},{3,2},{4,3},{5,4},{6,5},{7,6},{9,8},{10,9},{11,10},{12... | collective-permute-start | bytes 2457608 | tf_op jit(solution)/shard_map/ppermute | solution.py:26
  37.1 1.9 %collective-permute-start.6 = (f32[20,2,20,256]{3,2,1,0:T(8,128)S(1)}, f32[20,2,20,256]{3,2,1,0:T(8,128)S(1)}, u32[]{:S(2)}, u32[]{:S(2)}) collective-permute-start(f32[20,2,20,256]{3,2,1,0:T(8,128)S(1)} %get-tuple-element.7), channel_id=1, source_target_pairs={{0,1},{1,2},{2,3},{3,4},{4,5},{5,6},{6,7},{8,9},{9,10},{10,11},{11... | collective-permute-start | bytes 2457608 | tf_op jit(solution)/shard_map/ppermute | solution.py:24
  39.1 1.4 maximum_maximum_fusion
  40.5 3.9 %fusion.63 = f32[17,8,16,256]{3,2,1,0:T(8,128)S(1)} fusion(f32[18,8,20,256]{3,2,1,0:T(8,128)S(1)} %get-tuple-element.14, f32[18,8,20,256]{3,2,1,0:T(8,128)S(1)} %get-tuple-element.13, f32[16,256]{1,0:T(8,128)S(1)} %get-tuple-element.23, f32[17,8]{1,0:T(8,128)S(1)} %get-tuple-element.34, f32[16,256]{1,0:T(8,128)S(1)} %get-tuple-element.24, ...), kind=kLoop, calls=%fused_computation.132 | loop fusion | flops 11141120 | bytes 11175520 | tf_op jit(solution)/shard_map/add | solution.py:64
  44.4 12.2 %collective-permute-done.7 = f32[20,2,20,256]{3,2,1,0:T(8,128)S(1)} collective-permute-done((f32[20,2,20,256]{3,2,1,0:T(8,128)S(1)}, f32[20,2,20,256]{3,2,1,0:T(8,128)S(1)}, u32[]{:S(2)}, u32[]{:S(2)}) %collective-permute-start.7) | collective-permute-done | bytes 819232 | tf_op jit(solution)/shard_map/ppermute | solution.py:26
  56.6 6.2 %collective-permute-done.6 = f32[20,2,20,256]{3,2,1,0:T(8,128)S(1)} collective-permute-done((f32[20,2,20,256]{3,2,1,0:T(8,128)S(1)}, f32[20,2,20,256]{3,2,1,0:T(8,128)S(1)}, u32[]{:S(2)}, u32[]{:S(2)}) %collective-permute-start.6) | collective-permute-done | bytes 819232 | tf_op jit(solution)/shard_map/ppermute | solution.py:24
  62.8 9.8 %select_maximum_fusion.6 = f32[20,12,20,260]{3,2,1,0:T(8,128)S(1)} fusion(f32[20,2,20,256]{3,2,1,0:T(8,128)S(1)} %collective-permute-done.7, f32[20,2,20,256]{3,2,1,0:T(8,128)S(1)} %collective-permute-done.6, f32[2,8,20,256]{3,2,1,0:T(8,128)S(1)} %collective-permute-done.5, f32[2,8,20,256]{3,2,1,0:T(8,128)S(1)} %collective-permute-done.4, ...), kind=kLoop, calls=%fused_computation.9 | loop fusion | flops 19968000 | bytes 9907200 | tf_op jit(solution)/shard_map/concatenate | solution.py:22
  72.6 4.3 %fusion.33 = f32[16,8,16,257]{3,2,1,0:T(8,128)S(1)} fusion(f32[20,12,20,260]{3,2,1,0:T(8,128)S(1)} %select_maximum_fusion.6, f32[8]{0:T(128)S(1)} %add_multiply_fusion, f32[16,8]{1,0:T(8,128)S(1)} %get-tuple-element.31, f32[16,8]{1,0:T(8,128)S(1)} %get-tuple-element.32, f32[16,257]{1,0:T(8,128)S(1)} %fusion.89, f32[16,8]{1,0:T(8,128)S(1)} %get-tuple-element.30), kind=kLoop, calls=%fused_computation.65 | loop fusion | flops 11053056 | bytes 10544736 | tf_op jit(solution)/shard_map/add | solution.py:64
  76.9 6.0 %fusion.52 = f32[16,9,16,256]{3,2,1,0:T(8,128)S(1)} fusion(f32[20,2,20,256]{3,2,1,0:T(8,128)S(1)} %collective-permute-done.7, f32[2,8,20,256]{3,2,1,0:T(8,128)S(1)} %collective-permute-done.5, f32[2,8,20,256]{3,2,1,0:T(8,128)S(1)} %collective-permute-done.4, f32[16,8,2,256]{3,2,1,0:T(2,128)S(1)} %get-tuple-element.22, f32[16,8,16,256]{3,2,1,0:T(8,128)S(1)} %copy-done, ...), kind=kLoop, calls=%fused_computation.104 | loop fusion | flops 23592960 | bytes 7308992 | tf_op jit(solution)/shard_map/add | solution.py:64
  82.9 2.4 %fusion.82 = f32[16,8,16,256]{3,2,1,0:T(8,128)S(1)} fusion(f32[16,8,16,256]{3,2,1,0:T(8,128)S(1)} %copy-done, f32[16,9,16,256]{3,2,1,0:T(8,128)S(1)} %fusion.52, f32[17,8,16,256]{3,2,1,0:T(8,128)S(1)} %fusion.63, f32[16,8,16,257]{3,2,1,0:T(8,128)S(1)} %fusion.33, f32[16,8,17,256]{3,2,1,0:T(8,128)S(1)} %fusion.38, f32[16,8]{1,0:T(8,128)S(1)} %dynamic_slice.3, ...), kind=kLoop, calls=%fused_computation.160 | loop fusion | flops 7340032 | bytes 20976128 | tf_op jit(solution)/shard_map/jit(_where)/select_n | solution.py:107
  85.3 0.3 fusion.105
  85.6 3.0 %collective-permute-start.9 = (f32[16,8,2,256]{3,1,2,0:T(8,128)S(1)}, f32[16,8,2,256]{3,1,2,0:T(8,128)S(1)}, u32[]{:S(2)}, u32[]{:S(2)}) collective-permute-start(f32[16,8,2,256]{3,1,2,0:T(8,128)S(1)} %copy.21), channel_id=1, source_target_pairs={{32,0},{64,32},{96,64},{33,1},{65,33},{97,65},{34,2},{66,34},{98,6... | collective-permute-start | bytes 786440 | tf_op jit(solution)/shard_map/ppermute | solution.py:26
  88.6 1.5 collective-permute-start.8
  90.1 3.8 %collective-permute-done.9 = f32[16,8,2,256]{3,1,2,0:T(8,128)S(1)} collective-permute-done((f32[16,8,2,256]{3,1,2,0:T(8,128)S(1)}, f32[16,8,2,256]{3,1,2,0:T(8,128)S(1)}, u32[]{:S(2)}, u32[]{:S(2)}) %collective-permute-start.9) | collective-permute-done | bytes 262176 | tf_op jit(solution)/shard_map/ppermute | solution.py:26
  94.0 0.1 copy.22
  94.1 4.0 %collective-permute-done.8 = f32[16,8,2,256]{3,1,2,0:T(8,128)S(1)} collective-permute-done((f32[16,8,2,256]{3,1,2,0:T(8,128)S(1)}, f32[16,8,2,256]{3,1,2,0:T(8,128)S(1)}, u32[]{:S(2)}, u32[]{:S(2)}) %collective-permute-start.8) | collective-permute-done | bytes 262176 | tf_op jit(solution)/shard_map/ppermute | solution.py:24
  98.4 2.2 %collective-permute-start.11 = (f32[2,8,20,256]{3,2,1,0:T(8,128)S(1)}, f32[2,8,20,256]{3,2,1,0:T(8,128)S(1)}, u32[]{:S(2)}, u32[]{:S(2)}) collective-permute-start(f32[2,8,20,256]{3,2,1,0:T(8,128)S(1)} %get-tuple-element.12), channel_id=1, source_target_pairs={{8,0},{16,8},{24,16},{9,1},{17,9},{25,17},{10,2},{18,10},{26,18},{... | collective-permute-start | bytes 983048 | tf_op jit(solution)/shard_map/ppermute | solution.py:26
  100.6 4.9 %collective-permute-start.10 = (f32[2,8,20,256]{3,2,1,0:T(8,128)S(1)}, f32[2,8,20,256]{3,2,1,0:T(8,128)S(1)}, u32[]{:S(2)}, u32[]{:S(2)}) collective-permute-start(f32[2,8,20,256]{3,2,1,0:T(8,128)S(1)} %get-tuple-element.11), channel_id=1, source_target_pairs={{0,8},{8,16},{16,24},{1,9},{9,17},{17,25},{2,10},{10,18},{18,26},{... | collective-permute-start | bytes 983048 | tf_op jit(solution)/shard_map/ppermute | solution.py:24
  105.5 4.5 %fusion.27 = f32[16,8,17,256]{3,2,1,0:T(8,128)S(1)} fusion(f32[16,8,2,256]{3,2,1,0:T(2,128)S(1)} %copy.22, f32[16,8,16,256]{3,2,1,0:T(8,128)S(1)} %fusion.82, f32[16,8,2,256]{3,2,1,0:T(2,128)S(1)} %copy.20, f32[16]{0:T(128)S(1)} %add_multiply_fusion.1, f32[16,8]{1,0:T(8,128)S(1)} %get-tuple-element.31, f32[16,8]{1,0:T(8,128)S(1)} %get-tuple-element.32, ...), kind=kLoop, calls=%fused_computation.55 | loop fusion | flops 13926400 | bytes 4868672 | tf_op jit(solution)/shard_map/add | solution.py:64
  110.0 0.1 collective-permute-done.10
  110.2 0.3 pad_maximum_fusion.29
  110.5 1.9 %collective-permute-start.13 = (f32[20,2,20,256]{3,2,1,0:T(8,128)S(1)}, f32[20,2,20,256]{3,2,1,0:T(8,128)S(1)}, u32[]{:S(2)}, u32[]{:S(2)}) collective-permute-start(f32[20,2,20,256]{3,2,1,0:T(8,128)S(1)} %get-tuple-element.6), channel_id=1, source_target_pairs={{1,0},{2,1},{3,2},{4,3},{5,4},{6,5},{7,6},{9,8},{10,9},{11,10},{12... | collective-permute-start | bytes 2457608 | tf_op jit(solution)/shard_map/ppermute | solution.py:26
  112.4 3.4 %collective-permute-start.12 = (f32[20,2,20,256]{3,2,1,0:T(8,128)S(1)}, f32[20,2,20,256]{3,2,1,0:T(8,128)S(1)}, u32[]{:S(2)}, u32[]{:S(2)}) collective-permute-start(f32[20,2,20,256]{3,2,1,0:T(8,128)S(1)} %get-tuple-element.5), channel_id=1, source_target_pairs={{0,1},{1,2},{2,3},{3,4},{4,5},{5,6},{6,7},{8,9},{9,10},{10,11},{11... | collective-permute-start | bytes 2457608 | tf_op jit(solution)/shard_map/ppermute | solution.py:24
  115.8 1.3 maximum_maximum_fusion.1
  117.1 3.9 %fusion.58 = f32[17,8,16,256]{3,2,1,0:T(8,128)S(1)} fusion(f32[18,8,20,256]{3,2,1,0:T(8,128)S(1)} %get-tuple-element.10, f32[18,8,20,256]{3,2,1,0:T(8,128)S(1)} %get-tuple-element.9, f32[16,256]{1,0:T(8,128)S(1)} %get-tuple-element.23, f32[17,8]{1,0:T(8,128)S(1)} %get-tuple-element.34, f32[16,256]{1,0:T(8,128)S(1)} %get-tuple-element.24, ...), kind=kLoop, calls=%fused_computation.123 | loop fusion | flops 11141120 | bytes 11175520 | tf_op jit(solution)/shard_map/add | solution.py:64
  121.0 13.0 %collective-permute-done.13 = f32[20,2,20,256]{3,2,1,0:T(8,128)S(1)} collective-permute-done((f32[20,2,20,256]{3,2,1,0:T(8,128)S(1)}, f32[20,2,20,256]{3,2,1,0:T(8,128)S(1)}, u32[]{:S(2)}, u32[]{:S(2)}) %collective-permute-start.13) | collective-permute-done | bytes 819232 | tf_op jit(solution)/shard_map/ppermute | solution.py:26
  134.1 3.7 %collective-permute-done.12 = f32[20,2,20,256]{3,2,1,0:T(8,128)S(1)} collective-permute-done((f32[20,2,20,256]{3,2,1,0:T(8,128)S(1)}, f32[20,2,20,256]{3,2,1,0:T(8,128)S(1)}, u32[]{:S(2)}, u32[]{:S(2)}) %collective-permute-start.12) | collective-permute-done | bytes 819232 | tf_op jit(solution)/shard_map/ppermute | solution.py:24
  137.8 9.8 %select_maximum_fusion = f32[20,12,20,260]{3,2,1,0:T(8,128)S(1)} fusion(f32[20,2,20,256]{3,2,1,0:T(8,128)S(1)} %collective-permute-done.13, f32[20,2,20,256]{3,2,1,0:T(8,128)S(1)} %collective-permute-done.12, f32[2,8,20,256]{3,2,1,0:T(8,128)S(1)} %collective-permute-done.11, f32[2,8,20,256]{3,2,1,0:T(8,128)S(1)} %collective-permute-done.10, ...), kind=kLoop, calls=%fused_computation.3 | loop fusion | flops 19968000 | bytes 9907200 | tf_op jit(solution)/shard_map/concatenate | solution.py:22
  147.6 4.3 %fusion.21 = f32[16,8,16,257]{3,2,1,0:T(8,128)S(1)} fusion(f32[20,12,20,260]{3,2,1,0:T(8,128)S(1)} %select_maximum_fusion, f32[8]{0:T(128)S(1)} %add_multiply_fusion, f32[16,8]{1,0:T(8,128)S(1)} %get-tuple-element.31, f32[16,8]{1,0:T(8,128)S(1)} %get-tuple-element.32, f32[16,257]{1,0:T(8,128)S(1)} %fusion.89, f32[16,8]{1,0:T(8,128)S(1)} %get-tuple-element.30), kind=kLoop, calls=%fused_computation.45 | loop fusion | flops 11053056 | bytes 10544736 | tf_op jit(solution)/shard_map/add | solution.py:64
  152.0 6.1 %fusion.45 = f32[16,9,16,256]{3,2,1,0:T(8,128)S(1)} fusion(f32[20,2,20,256]{3,2,1,0:T(8,128)S(1)} %collective-permute-done.13, f32[2,8,20,256]{3,2,1,0:T(8,128)S(1)} %collective-permute-done.11, f32[2,8,20,256]{3,2,1,0:T(8,128)S(1)} %collective-permute-done.10, f32[16,8,2,256]{3,2,1,0:T(2,128)S(1)} %copy.22, f32[16,8,16,256]{3,2,1,0:T(8,128)S(1)} %fusion.82, ...), kind=kLoop, calls=%fused_computation.85 | loop fusion | flops 23592960 | bytes 7308992 | tf_op jit(solution)/shard_map/add | solution.py:64
  158.0 3.8 %fusion.72 = f32[16,8,16,256]{3,2,1,0:T(8,128)} fusion(f32[16,9,16,256]{3,2,1,0:T(8,128)S(1)} %fusion.45, f32[17,8,16,256]{3,2,1,0:T(8,128)S(1)} %fusion.58, f32[16,8,16,257]{3,2,1,0:T(8,128)S(1)} %fusion.21, f32[16,8,17,256]{3,2,1,0:T(8,128)S(1)} %fusion.27, f32[16,8,16,256]{3,2,1,0:T(8,128)S(1)} %copy-done, f32[16,8,16,256]{3,2,1,0:T(8,128)S(1)} %fusion.82, ...), kind=kLoop, calls=%fused_computation.146 | loop fusion | flops 8388608 | bytes 23073280 | tf_op jit(solution)/shard_map/jit(_where)/select_n | solution.py:107
  (39 shorter events, 1.2 us)
Async XLA Ops:
  0.0 11.8 %copy-start = (f32[16,8,16,256]{3,2,1,0:T(8,128)S(1)}, f32[16,8,16,256]{3,2,1,0:T(8,128)}, u32[]{:S(2)}) copy-start(f32[16,8,16,256]{3,2,1,0:T(8,128)} %param.4) | copy-start | bytes 6291460
  1.9 13.9 %collective-permute-start.3 = (f32[16,8,2,256]{3,1,2,0:T(8,128)S(1)}, f32[16,8,2,256]{3,1,2,0:T(8,128)S(1)}, u32[]{:S(2)}, u32[]{:S(2)}) collective-permute-start(f32[16,8,2,256]{3,1,2,0:T(8,128)S(1)} %copy.26), channel_id=1, source_target_pairs={{32,0},{64,32},{96,64},{33,1},{65,33},{97,65},{34,2},{66,34},{98,6... | collective-permute-start | bytes 786440 | tf_op jit(solution)/shard_map/ppermute | solution.py:26
  4.4 9.4 %copy-start.3 = (s32[16,256]{1,0:T(8,128)S(1)}, s32[16,256]{1,0:T(8,128)}, u32[]{:S(2)}) copy-start(s32[16,256]{1,0:T(8,128)} %param.6) | copy-start | bytes 49156
  4.4 10.4 %copy-start.2 = (s32[16,256]{1,0:T(8,128)S(1)}, s32[16,256]{1,0:T(8,128)}, u32[]{:S(2)}) copy-start(s32[16,256]{1,0:T(8,128)} %param.5) | copy-start | bytes 49156
  4.5 11.2 %collective-permute-start.2 = (f32[16,8,2,256]{3,1,2,0:T(8,128)S(1)}, f32[16,8,2,256]{3,1,2,0:T(8,128)S(1)}, u32[]{:S(2)}, u32[]{:S(2)}) collective-permute-start(f32[16,8,2,256]{3,1,2,0:T(8,128)S(1)} %copy.25), channel_id=1, source_target_pairs={{0,32},{32,64},{64,96},{1,33},{33,65},{65,97},{2,34},{34,66},{66,9... | collective-permute-start | bytes 786440 | tf_op jit(solution)/shard_map/ppermute | solution.py:24
  6.5 8.1 %collective-permute-start.1 = (s32[1,256]{1,0:T(1,128)S(1)}, s32[1,256]{1,0:T(1,128)S(1)}, u32[]{:S(2)}, u32[]{:S(2)}) collective-permute-start(s32[1,256]{1,0:T(1,128)S(1)} %get-tuple-element.29), channel_id=1, source_target_pairs={{32,0},{64,32},{96,64},{33,1},{65,33},{97,65},{34,2},{66,34},{98,6... | collective-permute-start | bytes 3080 | tf_op jit(solution)/shard_map/ppermute | solution.py:26
  10.5 4.3 %collective-permute-start = (s32[1,256]{1,0:T(1,128)S(1)}, s32[1,256]{1,0:T(1,128)S(1)}, u32[]{:S(2)}, u32[]{:S(2)}) collective-permute-start(s32[1,256]{1,0:T(1,128)S(1)} %get-tuple-element.28), channel_id=1, source_target_pairs={{0,32},{32,64},{64,96},{1,33},{33,65},{65,97},{2,34},{34,66},{66,9... | collective-permute-start | bytes 3080 | tf_op jit(solution)/shard_map/ppermute | solution.py:24
  16.8 8.8 %copy-start.1 = (f32[16,8,18,256]{3,2,1,0:T(8,128)S(1)}, f32[16,8,18,256]{3,2,1,0:T(8,128)}, u32[]{:S(2)}) copy-start(f32[16,8,18,256]{3,2,1,0:T(8,128)} %get-tuple-element.21) | copy-start | bytes 7077892
  17.0 13.1 %collective-permute-start.5 = (f32[2,8,20,256]{3,2,1,0:T(8,128)S(1)}, f32[2,8,20,256]{3,2,1,0:T(8,128)S(1)}, u32[]{:S(2)}, u32[]{:S(2)}) collective-permute-start(f32[2,8,20,256]{3,2,1,0:T(8,128)S(1)} %get-tuple-element.16), channel_id=1, source_target_pairs={{8,0},{16,8},{24,16},{9,1},{17,9},{25,17},{10,2},{18,10},{26,18},{... | collective-permute-start | bytes 983048 | tf_op jit(solution)/shard_map/ppermute | solution.py:26
  21.8 8.5 %collective-permute-start.4 = (f32[2,8,20,256]{3,2,1,0:T(8,128)S(1)}, f32[2,8,20,256]{3,2,1,0:T(8,128)S(1)}, u32[]{:S(2)}, u32[]{:S(2)}) collective-permute-start(f32[2,8,20,256]{3,2,1,0:T(8,128)S(1)} %get-tuple-element.15), channel_id=1, source_target_pairs={{0,8},{8,16},{16,24},{1,9},{9,17},{17,25},{2,10},{10,18},{18,26},{... | collective-permute-start | bytes 983048 | tf_op jit(solution)/shard_map/ppermute | solution.py:24
  30.7 25.9 %collective-permute-start.7 = (f32[20,2,20,256]{3,2,1,0:T(8,128)S(1)}, f32[20,2,20,256]{3,2,1,0:T(8,128)S(1)}, u32[]{:S(2)}, u32[]{:S(2)}) collective-permute-start(f32[20,2,20,256]{3,2,1,0:T(8,128)S(1)} %get-tuple-element.8), channel_id=1, source_target_pairs={{1,0},{2,1},{3,2},{4,3},{5,4},{6,5},{7,6},{9,8},{10,9},{11,10},{12... | collective-permute-start | bytes 2457608 | tf_op jit(solution)/shard_map/ppermute | solution.py:26
  37.1 25.7 %collective-permute-start.6 = (f32[20,2,20,256]{3,2,1,0:T(8,128)S(1)}, f32[20,2,20,256]{3,2,1,0:T(8,128)S(1)}, u32[]{:S(2)}, u32[]{:S(2)}) collective-permute-start(f32[20,2,20,256]{3,2,1,0:T(8,128)S(1)} %get-tuple-element.7), channel_id=1, source_target_pairs={{0,1},{1,2},{2,3},{3,4},{4,5},{5,6},{6,7},{8,9},{9,10},{10,11},{11... | collective-permute-start | bytes 2457608 | tf_op jit(solution)/shard_map/ppermute | solution.py:24
  85.6 8.4 %collective-permute-start.9 = (f32[16,8,2,256]{3,1,2,0:T(8,128)S(1)}, f32[16,8,2,256]{3,1,2,0:T(8,128)S(1)}, u32[]{:S(2)}, u32[]{:S(2)}) collective-permute-start(f32[16,8,2,256]{3,1,2,0:T(8,128)S(1)} %copy.21), channel_id=1, source_target_pairs={{32,0},{64,32},{96,64},{33,1},{65,33},{97,65},{34,2},{66,34},{98,6... | collective-permute-start | bytes 786440 | tf_op jit(solution)/shard_map/ppermute | solution.py:26
  88.6 9.5 %collective-permute-start.8 = (f32[16,8,2,256]{3,1,2,0:T(8,128)S(1)}, f32[16,8,2,256]{3,1,2,0:T(8,128)S(1)}, u32[]{:S(2)}, u32[]{:S(2)}) collective-permute-start(f32[16,8,2,256]{3,1,2,0:T(8,128)S(1)} %copy.19), channel_id=1, source_target_pairs={{0,32},{32,64},{64,96},{1,33},{33,65},{65,97},{2,34},{34,66},{66,9... | collective-permute-start | bytes 786440 | tf_op jit(solution)/shard_map/ppermute | solution.py:24
  98.4 11.6 %collective-permute-start.11 = (f32[2,8,20,256]{3,2,1,0:T(8,128)S(1)}, f32[2,8,20,256]{3,2,1,0:T(8,128)S(1)}, u32[]{:S(2)}, u32[]{:S(2)}) collective-permute-start(f32[2,8,20,256]{3,2,1,0:T(8,128)S(1)} %get-tuple-element.12), channel_id=1, source_target_pairs={{8,0},{16,8},{24,16},{9,1},{17,9},{25,17},{10,2},{18,10},{26,18},{... | collective-permute-start | bytes 983048 | tf_op jit(solution)/shard_map/ppermute | solution.py:26
  100.6 9.6 %collective-permute-start.10 = (f32[2,8,20,256]{3,2,1,0:T(8,128)S(1)}, f32[2,8,20,256]{3,2,1,0:T(8,128)S(1)}, u32[]{:S(2)}, u32[]{:S(2)}) collective-permute-start(f32[2,8,20,256]{3,2,1,0:T(8,128)S(1)} %get-tuple-element.11), channel_id=1, source_target_pairs={{0,8},{8,16},{16,24},{1,9},{9,17},{17,25},{2,10},{10,18},{18,26},{... | collective-permute-start | bytes 983048 | tf_op jit(solution)/shard_map/ppermute | solution.py:24
  110.5 23.6 %collective-permute-start.13 = (f32[20,2,20,256]{3,2,1,0:T(8,128)S(1)}, f32[20,2,20,256]{3,2,1,0:T(8,128)S(1)}, u32[]{:S(2)}, u32[]{:S(2)}) collective-permute-start(f32[20,2,20,256]{3,2,1,0:T(8,128)S(1)} %get-tuple-element.6), channel_id=1, source_target_pairs={{1,0},{2,1},{3,2},{4,3},{5,4},{6,5},{7,6},{9,8},{10,9},{11,10},{12... | collective-permute-start | bytes 2457608 | tf_op jit(solution)/shard_map/ppermute | solution.py:26
  112.4 25.4 %collective-permute-start.12 = (f32[20,2,20,256]{3,2,1,0:T(8,128)S(1)}, f32[20,2,20,256]{3,2,1,0:T(8,128)S(1)}, u32[]{:S(2)}, u32[]{:S(2)}) collective-permute-start(f32[20,2,20,256]{3,2,1,0:T(8,128)S(1)} %get-tuple-element.5), channel_id=1, source_target_pairs={{0,1},{1,2},{2,3},{3,4},{4,5},{5,6},{6,7},{8,9},{9,10},{10,11},{11... | collective-permute-start | bytes 2457608 | tf_op jit(solution)/shard_map/ppermute | solution.py:24
where the time goes:
time: 162 us
  other arithmetic  67.4 us (42%)
  waiting for transfers between devices  43.6 us (27%)
  starting transfers between devices  42.9 us (26%)
  local copies, waits for them, and re-layouts  7.45 us (5%)
    add x8, other arithmetic, upwind(): jnp.maximum(velocity, 0.0) * left_side  37.4 us
    ppermute x7, waiting for transfers between devices, padded_2(): lax.ppermute(head, axis, [((i + 1) % count, i) for i in range(ends)])  29.1 us
    ppermute x7, starting transfers between devices, padded_2(): lax.ppermute(head, axis, [((i + 1) % count, i) for i in range(ends)])  24.9 us
    concatenate x4, other arithmetic, padded_2(): jnp.concatenate([lax.ppermute(tail, axis, [(i, (i + 1) % count) for i in...  22.3 us
    ppermute x7, starting transfers between devices, padded_2(): lax.ppermute(tail, axis, [(i, (i + 1) % count) for i in range(ends)])  18 us
    ppermute x7, waiting for transfers between devices, padded_2(): lax.ppermute(tail, axis, [(i, (i + 1) % count) for i in range(ends)])  14.5 us
    select_n x2, other arithmetic, hold(): jnp.where(mask_rows[None, None] == 1, spectrum[:, :, None, None], values)  6.18 us
  transfers between devices with their start and end apart: 14, of which 9 were waited for; matrix products, arithmetic and copies ran while one was open for 15% of the time, Pallas kernels for 0%

commit v1 on v0

v1 whole, which is shorter than its diff:
```python
import functools

import jax
import jax.numpy as jnp
from jax import lax
from jax.experimental import pallas as pl
from jax.experimental.pallas import tpu as pltpu
from jax.sharding import PartitionSpec as P

NKX = 64
NKY = 64

gravity = 9.81
spacing = 4.0
k_step = 0.04
time_step = 0.2

BX, BY, BS, NY = 16, 8, 16, 256
SLAB = BS
f32 = jnp.float32
VMEM = pltpu.VMEM
LIMIT = 48 * 2**20

X_SCALE = time_step / spacing * 0.5
K_SCALE = time_step / k_step * 0.5


def even_pairs(count):
    return [(i, i ^ 1) for i in range(count)]


def odd_pairs(count):
    pairs = []
    for i in range(1, count, 2):
        pairs += [(i, (i + 1) % count), ((i + 1) % count, i)]
    return pairs


def place():
    s, i, j = lax.axis_index("space"), lax.axis_index("kx"), lax.axis_index("ky")
    return s, i, j, i >= lax.axis_size("kx") // 2, j >= lax.axis_size("ky") // 2


def edge_rows(rows, base, x_up, refs):
    def one_kx(i, carry):
        for at, r in ((0, jnp.where(x_up, BS - 1, 0)), (BX * BY, jnp.where(x_up, BS - 2, 1))):
            for j in range(BY):
                slab = i * BY + j
                row = rows[pl.ds(base + slab * BS + r, 1), :]
                for ref in refs:
                    ref[pl.ds(at + slab, 1), :] = row
        return carry

    lax.fori_loop(0, BX, one_kx, 0)


def first_messages(a, depth, np_ref, ky_od, ky_ev, kx_od, kx_ev, x_od, x_ev, sems):
    s, i, j, x_up, _ = place()
    copies = []

    def copy(src, dst):
        c = pltpu.make_async_copy(src, dst, sems.at[len(copies)])
        c.start()
        copies.append(c)

    ky_even, kx_even, s_even = j % 2 == 0, i % 2 == 0, s % 2 == 0
    copy(a.at[:, pl.ds(jnp.where(ky_even, 0, BY - 2), 2)], ky_od)
    copy(a.at[:, pl.ds(jnp.where(ky_even, BY - 2, 0), 2)], ky_ev)
    copy(a, np_ref.at[pl.ds(2, BX)])
    copy(a.at[pl.ds(jnp.where(kx_even, 0, BX - 2), 2)], kx_od)
    copy(a.at[pl.ds(jnp.where(kx_even, BX - 2, 0), 2)], kx_ev)
    copies[2].wait()
    rows = np_ref.reshape((BX + 4) * BY * BS, NY)
    base = 2 * BY * BS
    edge_rows(rows, base, x_up, (x_od, x_ev))
    low = jnp.broadcast_to(depth[0:1, :].astype(f32), (8, NY))
    high = jnp.broadcast_to(depth[BS - 1 : BS, :].astype(f32), (8, NY))
    for ref, above in ((x_od, jnp.logical_not(s_even)), (x_ev, s_even)):
        ref[pl.ds(256, 8), :] = jnp.where(above, high, low)
    for c in (copies[0], copies[1], copies[3], copies[4]):
        c.wait()


def shifted(h, axis, up):
    size = h.shape[axis]
    place_of = lax.broadcasted_iota(jnp.int32, h.shape, axis)
    if up:
        return jnp.where(place_of == size - 1, h, pltpu.roll(h, size - 1, axis))
    return jnp.where(place_of == 0, h, pltpu.roll(h, 1, axis))


def group(k, c, h):
    kh = k * h
    t = jnp.tanh(kh)
    return c * ((t + kh * (1.0 - t * t)) * lax.rsqrt(t))


def refract(k, c, h):
    t = jnp.tanh(k * h)
    return c * ((1.0 - t * t) * lax.rsqrt(t))


def speeds(tab, depth, ax, ay, rkx, aky, gy, geo):
    _, _, _, x_up, y_up = place()
    h = depth[...].astype(f32) * 0.01
    hx = 0.5 * (h + jnp.where(x_up, shifted(h, 0, True), shifted(h, 0, False)))
    y_next, y_last = shifted(h, 1, True), shifted(h, 1, False)
    hy = 0.5 * (h + jnp.where(y_up, y_next, y_last))
    slope = (y_last - y_next) * (1.0 / (2.0 * spacing))
    gy[...] = slope
    geo[0] = h
    geo[1] = hx
    geo[2] = hy

    def one_kx(i, carry):
        for j in range(BY):
            n = i * BY + j
            r = pl.ds(pl.multiple_of(n * BS, BS), BS)
            k = tab[0, n]
            ax[r, :] = group(k, tab[1, n], geo[1])
            ay[r, :] = group(k, tab[2, n], geo[2])
            rkx[r, :] = refract(tab[3, n], tab[4, n], geo[0])
        for j in range(BY + 1):
            n = i * (BY + 1) + j
            r = pl.ds(pl.multiple_of(n * BS, BS), BS)
            aky[r, :] = refract(tab[5, n], tab[6, n], geo[0]) * gy[...]
        return carry

    lax.fori_loop(0, BX, one_kx, 0)
    for j in range(BY):
        n = BX * BY + j
        rkx[pl.ds(n * BS, BS), :] = refract(tab[3, n], tab[4, n], geo[0])


class Flow:
    def __init__(self, x_up, y_up):
        x0 = jnp.where(x_up, 0, 8)
        y0 = jnp.where(y_up, 0, 128)
        self.x = (pl.multiple_of(x0, 8), pl.multiple_of(8 - x0, 8))
        self.y = (pl.multiple_of(y0, 128), pl.multiple_of(128 - y0, 128))
        self.x_roll = jnp.where(x_up, 1, 7)
        self.y_roll = jnp.where(y_up, 1, 127)
        rows = lax.broadcasted_iota(jnp.int32, (8, 128), 0)
        lanes = lax.broadcasted_iota(jnp.int32, (8, 128), 1)
        self.x_first = rows == jnp.where(x_up, 0, 7)
        self.x_last = rows == jnp.where(x_up, 7, 0)
        self.y_first = lanes == jnp.where(y_up, 0, 127)

    def load(self, ref, slab):
        r = slab * BS
        return [
            [ref[pl.ds(pl.multiple_of(r + self.x[a], 8), 8), pl.ds(self.y[b], 128)] for b in range(2)]
            for a in range(2)
        ]

    def store(self, ref, slab, tiles):
        r = slab * BS
        for a in range(2):
            for b in range(2):
                ref[pl.ds(pl.multiple_of(r + self.x[a], 8), 8), pl.ds(self.y[b], 128)] = tiles[a][b]

    def row(self, ref, first, j, b):
        tile = ref[pl.ds(pl.multiple_of(first, 8), 8), pl.ds(self.y[b], 128)]
        return jnp.broadcast_to(tile[j : j + 1, :], (8, 128))

    def before_x(self, tiles, b, halo):
        first, second = (pltpu.roll(tiles[a][b], self.x_roll, 0) for a in range(2))
        return [jnp.where(self.x_first, halo, first), jnp.where(self.x_first, first, second)]

    def before_y(self, tiles, a):
        first, second = (pltpu.roll(tiles[a][b], self.y_roll, 1) for b in range(2))
        return [jnp.where(self.y_first, 0.0, first), jnp.where(self.y_first, first, second)]


def each(fn, *grids):
    return [[fn(*(g[a][b] for g in grids)) for b in range(2)] for a in range(2)]


def space_change(flow, n3, n, ax_ref, ay_ref, i, j, edge, halo_row, halo_flux):
    slab, first = i * BY + j, i * BY
    ax = flow.load(ax_ref, slab)
    ay = flow.load(ay_ref, slab)
    total = [[None, None], [None, None]]
    for b in range(2):
        ax[1][b] = jnp.where(flow.x_last, flow.row(edge, first, j, b), ax[1][b])
        before = flow.before_x(n, b, flow.row(halo_row, first, j, b))
        out = [[ax[a][b] * (n3[a][b] - before[a])] * 2 for a in range(2)]
        into = flow.before_x(out, b, flow.row(halo_flux, first, j, b))
        for a in range(2):
            total[a][b] = out[a][b] - into[a]
    for a in range(2):
        before = flow.before_y(n, a)
        out = [ay[a][b] * (n3[a][b] - before[b]) for b in range(2)]
        into = flow.before_y([out, out], 0)
        for b in range(2):
            total[a][b] = total[a][b] + (out[b] - into[b])
    return total


def face(up, speed, n_2, n_1, n1, n2):
    near = jnp.where(up, n_1, n1)
    far = jnp.where(up, n_2, n2)
    return speed * (3.0 * near - far)


def times3(tiles):
    return each(lambda v: 3.0 * v, tiles)


def edge_speeds(flow, kcol, ccol, h_row, out, i):
    for b in range(2):
        y = pl.ds(flow.y[b], 128)
        r = pl.ds(pl.multiple_of(i * BY, BY), BY)
        out[r, y] = group(kcol[r, :], ccol[r, :], flow.row(h_row, 0, 0, b))


def stage_one_space(
    np_in, ax, ay, rkx, aky, gy, geo, depth, mask, spec, kcol, ccol, kx_od, kx_ev, x_od, x_ev,
    np_ref, p_ref, gx, edge, halo_speed, ky2_od, ky2_ev, fk, hrow, xnear, xflux, sems,
):
    s, i, j, x_up, y_up = place()
    flow = Flow(x_up, y_up)
    s_count, kx_count = lax.axis_size("space"), lax.axis_size("kx")
    s_even, kx_even, ky_even = s % 2 == 0, i % 2 == 0, j % 2 == 0
    cells = BY * BS
    below = jnp.where(kx_even, kx_od[...], kx_ev[...])
    np_ref[pl.ds(0, 2 * cells), :] = jnp.where(i == 0, 0.0, below)
    above = jnp.where(kx_even, kx_ev[...], kx_od[...])
    np_ref[pl.ds((BX + 2) * cells, 2 * cells), :] = jnp.where(i == kx_count - 1, 0.0, above)
    h = geo[0]
    h_low = jnp.where(s_even, x_od[pl.ds(256, 1), :], x_ev[pl.ds(256, 1), :]) * 0.01
    h_low = jnp.where(s == 0, h[0:1, :], h_low)
    h_high = jnp.where(s_even, x_ev[pl.ds(256, 1), :], x_od[pl.ds(256, 1), :]) * 0.01
    h_high = jnp.where(s == s_count - 1, h[BS - 1 : BS, :], h_high)
    place_of = lax.broadcasted_iota(jnp.int32, (BS, NY), 0)
    before = jnp.where(place_of == 0, h_low, pltpu.roll(h, 1, 0))
    after = jnp.where(place_of == BS - 1, h_high, pltpu.roll(h, BS - 1, 0))
    gx[...] = (before - after) * (1.0 / (2.0 * spacing))
    face_low = 0.5 * (h_low + h[0:1, :])
    face_high = 0.5 * (h_high + h[BS - 1 : BS, :])
    hrow[0:1, :] = jnp.where(x_up, face_high, face_low)
    hrow[8:9, :] = jnp.where(x_up, face_low, face_high)
    none = jnp.logical_or(jnp.logical_and(x_up, s == 0), jnp.logical_and(jnp.logical_not(x_up), s == s_count - 1))
    use_od = s_even == x_up
    near = jnp.where(use_od, x_od[pl.ds(0, 128), :], x_ev[pl.ds(0, 128), :])
    far = jnp.where(use_od, x_od[pl.ds(128, 128), :], x_ev[pl.ds(128, 128), :])
    near = jnp.where(none, 0.0, near)
    xnear[...] = near
    xflux[...] = 3.0 * near - jnp.where(none, 0.0, far)
    out_row, in_row = hrow.at[pl.ds(0, 8)], hrow.at[pl.ds(8, 8)]

    def edges(i, carry):
        edge_speeds(flow, kcol, ccol, out_row, edge, i)
        edge_speeds(flow, kcol, ccol, in_row, halo_speed, i)
        r = pl.ds(pl.multiple_of(i * BY, BY), BY)
        xflux[r, :] = xflux[r, :] * halo_speed[r, :]
        return carry

    lax.fori_loop(0, BX, edges, 0)

    tgx = flow.load(gx, 0)

    def kx_flux(i, j):
        n = [flow.load(np_ref, (i + d) * BY + j) for d in range(4)]
        r = flow.load(rkx, i * BY + j)
        return each(lambda g, r, *n: face(g > 0, r * g, *n), tgx, r, *n)

    for j in range(BY):
        flow.store(fk, j, kx_flux(0, j))

    def one_kx(i, carry):
        hold = each(lambda m: m == 1, flow.load(mask, 0))
        layer = [flow.load(np_ref, (i + 2) * BY + j) for j in range(BY)]
        part = {}
        for j in range(BY):
            slab = i * BY + j
            n = layer[j]
            total = space_change(flow, times3(n), n, ax, ay, i, j, edge, xnear, xflux)
            upper = kx_flux(i + 1, j)
            lower = flow.load(fk, j)
            flow.store(fk, j, upper)
            p = each(lambda n, t, u, v: n - (t + (u - v)), n, total, upper, lower)
            flow.store(p_ref, slab, p)
            if j in (0, 1, BY - 2, BY - 1):
                part[j] = p

        def own(f, a, b):
            w = flow.load(aky, i * (BY + 1) + f)
            return each(lambda w, a, b: w * (3.0 * a - b), w, layer[a], layer[b])

        def send(j, low, high, ref, l):
            v = each(
                lambda m, p, u, v: jnp.where(m, spec[i * BY + j], p - (u - v)), hold, part[j], high, low
            )
            flow.store(ref, i * 2 + l, v)

        f = [own(0, 0, 1), own(1, 1, 2), own(2, 2, 3)]
        down = [(0, f[0], f[1]), (1, f[1], f[2])]
        g = [own(BY - 2, BY - 3, BY - 4), own(BY - 1, BY - 2, BY - 3), own(BY, BY - 1, BY - 2)]
        up = [(BY - 2, g[0], g[1]), (BY - 1, g[1], g[2])]

        @pl.when(ky_even)
        def _():
            for l in range(2):
                send(*down[l], ky2_od, l)
                send(*up[l], ky2_ev, l)

        @pl.when(jnp.logical_not(ky_even))
        def _():
            for l in range(2):
                send(*down[l], ky2_ev, l)
                send(*up[l], ky2_od, l)

        return carry

    lax.fori_loop(0, BX, one_kx, 0)


def ky_halos(od, ev, low, high):
    j = lax.axis_index("ky")
    last = lax.axis_size("ky") - 1
    even = j % 2 == 0

    def fill(ref, first, second, empty):
        @pl.when(empty)
        def _():
            ref[...] = jnp.zeros(ref.shape, f32)

        @pl.when(jnp.logical_and(even, jnp.logical_not(empty)))
        def _():
            ref[...] = first[...]

        @pl.when(jnp.logical_and(jnp.logical_not(even), jnp.logical_not(empty)))
        def _():
            ref[...] = second[...]

    fill(low, od, ev, j == 0)
    fill(high, ev, od, j == last)


def ky_column(flow, n_ref, low, high, i):
    layers = [flow.load(low, i * 2 + l) for l in range(2)]
    layers += [flow.load(n_ref, (i + 2) * BY + j) for j in range(BY)]
    return layers + [flow.load(high, i * 2 + l) for l in range(2)]


def ky_flux(flow, aky, tgy, layers, i, f):
    w = flow.load(aky, i * (BY + 1) + f)
    return each(lambda g, w, *n: face(g > 0, w, *n), tgy, w, *layers[f : f + 4])


def stage_one_ky(np_ref, p_ref, aky, gy, mask, spec, ky_od, ky_ev, sp_ref, kx2_od, kx2_ev, x2, low, high):
    s, i, j, x_up, y_up = place()
    flow = Flow(x_up, y_up)
    ky_halos(ky_od, ky_ev, low, high)
    tgy = flow.load(gy, 0)

    def one_kx(i, carry):
        hold = each(lambda m: m == 1, flow.load(mask, 0))
        layers = ky_column(flow, np_ref, low, high, i)
        lower = ky_flux(flow, aky, tgy, layers, i, 0)
        for j in range(BY):
            upper = ky_flux(flow, aky, tgy, layers, i, j + 1)
            slab = i * BY + j
            p = flow.load(p_ref, slab)
            v = each(lambda m, p, u, v: jnp.where(m, spec[slab], p - (u - v)), hold, p, upper, lower)
            flow.store(sp_ref, slab + 2 * BY, v)
            lower = upper
        return carry

    lax.fori_loop(0, BX, one_kx, 0)
    cells = BY * BS
    base = 2 * cells
    low_rows, high_rows = pl.ds(base, base), pl.ds(base + (BX - 2) * cells, base)
    kx_even = i % 2 == 0

    @pl.when(kx_even)
    def _():
        kx2_od[...] = sp_ref[low_rows, :]
        kx2_ev[...] = sp_ref[high_rows, :]

    @pl.when(jnp.logical_not(kx_even))
    def _():
        kx2_od[...] = sp_ref[high_rows, :]
        kx2_ev[...] = sp_ref[low_rows, :]

    edge_rows(sp_ref, base, x_up, (x2,))


def stage_two(
    np_ref, sp_in, ax, ay, rkx, aky, gx, gy, edge, halo_speed, mask, spec, ky_od, ky_ev, kx_od, kx_ev, x2,
    out, sp_ref, fk, xnear, xflux, low, high, sem,
):
    s, i, j, x_up, y_up = place()
    flow = Flow(x_up, y_up)
    s_count, kx_count = lax.axis_size("space"), lax.axis_size("kx")
    kx_even = i % 2 == 0
    cells = BY * BS
    inner = pl.ds(2 * cells, BX * cells)
    copy = pltpu.make_async_copy(sp_in.at[inner], sp_ref.at[inner], sem)
    copy.start()
    ky_halos(ky_od, ky_ev, low, high)
    below = jnp.where(kx_even, kx_od[...], kx_ev[...])
    sp_ref[pl.ds(0, 2 * cells), :] = jnp.where(i == 0, 0.0, below)
    above = jnp.where(kx_even, kx_ev[...], kx_od[...])
    sp_ref[pl.ds((BX + 2) * cells, 2 * cells), :] = jnp.where(i == kx_count - 1, 0.0, above)
    none = jnp.logical_or(jnp.logical_and(x_up, s == 0), jnp.logical_and(jnp.logical_not(x_up), s == s_count - 1))
    near = jnp.where(none, 0.0, x2[pl.ds(0, 128), :])
    far = jnp.where(none, 0.0, x2[pl.ds(128, 128), :])
    xnear[...] = near
    xflux[...] = (3.0 * near - far) * halo_speed[...]
    copy.wait()

    tgx = flow.load(gx, 0)
    tgy = flow.load(gy, 0)

    def kx_flux(i, j):
        n = [flow.load(sp_ref, (i + d) * BY + j) for d in range(4)]
        r = flow.load(rkx, i * BY + j)
        return each(lambda g, r, *n: face(g > 0, r * g, *n), tgx, r, *n)

    for j in range(BY):
        flow.store(fk, j, kx_flux(0, j))

    def one_kx(i, carry):
        hold = each(lambda m: m == 1, flow.load(mask, 0))
        layers = ky_column(flow, sp_ref, low, high, i)
        lower_y = ky_flux(flow, aky, tgy, layers, i, 0)
        for j in range(BY):
            slab = i * BY + j
            n = layers[j + 2]
            total = space_change(flow, times3(n), n, ax, ay, i, j, edge, xnear, xflux)
            upper = kx_flux(i + 1, j)
            lower = flow.load(fk, j)
            flow.store(fk, j, upper)
            upper_y = ky_flux(flow, aky, tgy, layers, i, j + 1)
            first = flow.load(np_ref, slab + 2 * BY)
            v = each(
                lambda m, a, n, t, u, v, p, q: jnp.where(
                    m, spec[slab], 0.5 * ((a + n) - ((t + (u - v)) + (p - q)))
                ),
                hold, first, n, total, upper, lower, upper_y, lower_y,
            )
            flow.store(out, slab, v)
            lower_y = upper_y
        return carry

    lax.fori_loop(0, BX, one_kx, 0)


def call(kernel, outs, operands, spaces, scratch=(), alias=None, flops=0):
    whole = {
        "v": pl.BlockSpec(memory_space=pltpu.VMEM),
        "s": pl.BlockSpec(memory_space=pltpu.SMEM),
        "h": pl.BlockSpec(memory_space=pltpu.HBM),
    }
    return pl.pallas_call(
        kernel,
        out_shape=outs,
        in_specs=[whole[c] for c in spaces],
        out_specs=jax.tree.map(lambda _: whole["v"], outs),
        scratch_shapes=list(scratch),
        input_output_aliases=alias or {},
        compiler_params=pltpu.CompilerParams(vmem_limit_bytes=LIMIT),
        cost_estimate=pl.CostEstimate(flops=flops, bytes_accessed=0, transcendentals=0),
        name=kernel.__name__,
    )(*operands)


def wave_tables(kx_first, ky_first):
    kx = ((kx_first + jnp.arange(BX) - NKX // 2).astype(f32) + 0.5) * k_step
    kxf = (kx_first + jnp.arange(BX + 1) - NKX // 2).astype(f32) * k_step
    ky = ((ky_first + jnp.arange(BY) - NKY // 2).astype(f32) + 0.5) * k_step
    kyf = (ky_first + jnp.arange(BY + 1) - NKY // 2).astype(f32) * k_step

    def modulus(a, b):
        return jnp.sqrt(a[:, None] * a[:, None] + b[None, :] * b[None, :])

    k = modulus(kx, ky)
    c = (0.5 * X_SCALE) * jnp.sqrt(gravity / k) / k
    cx = c * jnp.abs(kx)[:, None]
    cy = c * jnp.abs(ky)[None, :]
    kf = modulus(kxf, ky)
    kg = modulus(kx, kyf)
    rows = [k, cx, cy, kf, (0.5 * K_SCALE) * jnp.sqrt(gravity * kf) * kf, kg, (0.5 * K_SCALE) * jnp.sqrt(gravity * kg) * kg]
    flat = [jnp.pad(r.reshape(-1), (0, 144 - r.size)) for r in rows]
    column = [jnp.broadcast_to(r.reshape(-1, 1), (BX * BY, 128)) for r in (k, cx)]
    return jnp.stack(flat), column[0], column[1]


def per_device(action, depth_cm, inflow_mask, inflow):
    kx_first = lax.axis_index("kx") * BX
    ky_first = lax.axis_index("ky") * BY
    spec = lax.dynamic_slice(inflow, (kx_first, ky_first), (BX, BY)).reshape(-1)
    tab, kcol, ccol = wave_tables(kx_first, ky_first)
    rows = BX * BY * BS
    padded = (BX + 4) * BY * BS
    ky_rows, kx_rows = BX * 2 * BS, 2 * BY * BS

    def v(*shape):
        return pltpu.VMEM(shape, f32)

    def swap(od, ev, axis):
        n = lax.axis_size(axis)
        return lax.ppermute(od, axis, odd_pairs(n)), lax.ppermute(ev, axis, even_pairs(n))

    np4, ky_od, ky_ev, kx_od, kx_ev, x_od, x_ev = call(
        first_messages,
        (v(BX + 4, BY, BS, NY), v(BX, 2, BS, NY), v(BX, 2, BS, NY), v(2, BY, BS, NY), v(2, BY, BS, NY), v(264, NY), v(264, NY)),
        (action, depth_cm),
        "hv",
        [pltpu.SemaphoreType.DMA((5,))],
    )
    ky_od, ky_ev = swap(ky_od, ky_ev, "ky")
    kx_od, kx_ev = swap(kx_od, kx_ev, "kx")
    x_od, x_ev = swap(x_od, x_ev, "space")
    ax, ay, rkx, aky, gy, geo = call(
        speeds,
        (v(rows, NY), v(rows, NY), v((BX + 1) * BY * BS, NY), v(BX * (BY + 1) * BS, NY), v(BS, NY), v(3, BS, NY)),
        (tab, depth_cm),
        "sv",
        flops=10_000_000,
    )
    np2 = np4.reshape(padded, NY)
    np2, part, gx, edge, halo_speed, ky2_od, ky2_ev = call(
        stage_one_space,
        (v(padded, NY), v(rows, NY), v(BS, NY), v(BX * BY, NY), v(BX * BY, NY), v(ky_rows, NY), v(ky_rows, NY)),
        (np2, ax, ay, rkx, aky, gy, geo, depth_cm, inflow_mask, spec, kcol, ccol,
         kx_od.reshape(kx_rows, NY), kx_ev.reshape(kx_rows, NY), x_od, x_ev),
        "vvvvvvvvvsvvvvvv",
        [v(BY * BS, NY), v(16, NY), v(BX * BY, NY), v(BX * BY, NY), pltpu.SemaphoreType.DMA((2,))],
        alias={0: 0},
    )
    ky2_od, ky2_ev = swap(ky2_od, ky2_ev, "ky")
    sp, kx2_od, kx2_ev, x2 = call(
        stage_one_ky,
        (v(padded, NY), v(kx_rows, NY), v(kx_rows, NY), v(256, NY)),
        (np2, part, aky, gy, inflow_mask, spec, ky_od.reshape(ky_rows, NY), ky_ev.reshape(ky_rows, NY)),
        "vvvvvsvv",
        [v(ky_rows, NY), v(ky_rows, NY)],
    )
    kx2_od, kx2_ev = swap(kx2_od, kx2_ev, "kx")
    n_space, n_kx = lax.axis_size("space"), lax.axis_size("kx")
    ring = []
    for a in range(n_space):
        for b in range(n_kx):
            to = (a + (1 if b >= n_kx // 2 else -1)) % n_space
            ring.append((a * n_kx + b, to * n_kx + b))
    x2 = lax.ppermute(x2, ("space", "kx"), ring)
    out = call(
        stage_two,
        jax.ShapeDtypeStruct((rows, NY), f32),
        (np2, sp, ax, ay, rkx, aky, gx, gy, edge, halo_speed, inflow_mask, spec,
         ky2_od, ky2_ev, kx2_od, kx2_ev, x2),
        "vvvvvvvvvvvsvvvvv",
        [v(padded, NY), v(BY * BS, NY), v(BX * BY, NY), v(BX * BY, NY), v(ky_rows, NY), v(ky_rows, NY), pltpu.SemaphoreType.DMA],
    )
    return out.reshape(BX, BY, BS, NY)


def solution(mesh):
    in_specs = (P("kx", "ky", "space", None), P("space", None), P("space", None), P())
    out_specs = P("kx", "ky", "space", None)
    return jax.shard_map(
        per_device, mesh=mesh, in_specs=in_specs, out_specs=out_specs, check_vma=False
    )
```

time: 162 us -> 84.9 us (0.52)
  the two profiles are of different devices: /device:TPU:15 before, /device:TPU:6 now
where the time goes in v1:
time: 84.9 us; the launch traced here: 84.6 us
  Pallas kernels  42 us (49%)
  starting transfers between devices  18.6 us (22%)
  local copies, waits for them, and re-layouts  14.2 us (17%)
  waiting for transfers between devices  9.39 us (11%)
    pallas_call x5, Pallas kernels, call(): pl.pallas_call(kernel, out_shape=outs, in_specs=[whole[c] for c in spaces...  42 us
    ppermute x5, starting transfers between devices, swap(): lax.ppermute(od, axis, odd_pairs(n))  13.1 us
    unnamed x24, local copies, waits for them, and re-layouts  11.4 us
    ppermute x5, waiting for transfers between devices, swap(): lax.ppermute(od, axis, odd_pairs(n))  6.68 us
    ppermute x5, starting transfers between devices, swap(): lax.ppermute(ev, axis, even_pairs(n))  4.64 us
    ppermute x1, waiting for transfers between devices, per_device(): x2 = lax.ppermute(x2, ('space', 'kx'), ring)  2.7 us
  transfers between devices with their start and end apart: 11, of which 3 were waited for; matrix products, arithmetic and copies ran while one was open for 4% of the time, Pallas kernels for 29%

profile of v1, /device:TPU:6, one launch (start us, length us, event | category | flops | bytes accessed | tf_op | source)
XLA Modules:
  0.0 84.6 jit_solution(1987338486086284744)
XLA Ops:
  0.0 0.7 copy-done.9
  0.7 4.1 %first_messages.1 = (f32[20,8,16,256]{3,2,1,0:T(8,128)S(1)}, f32[16,2,16,256]{3,2,1,0:T(8,128)}, f32[16,2,16,256]{3,2,1,0:T(8,128)S(1)}, f32[2,8,16,256]{3,2,1,0...) custom-call(f32[16,8,16,256]{3,2,1,0:T(8,128)} %a.1, s32[16,256]{1,0:T(8,128)S(1)} %copy-done.9), custom_call_target="tpu_custom_call" | custom-call | tf_op jit(solution)/shard_map/first_messages/pallas_call | solution.py:457
  4.8 0.8 copy-done.11
  5.6 2.6 %collective-permute-start = (f32[2,8,16,256]{3,2,1,0:T(8,128)}, f32[2,8,16,256]{3,2,1,0:T(8,128)}, u32[]{:S(2)}, u32[]{:S(2)}) collective-permute-start(f32[2,8,16,256]{3,2,1,0:T(8,128)} %get-tuple-element.36), channel_id=1, source_target_pairs={{8,16},{16,8},{24,0},{0,24},{9,17},{17,9},{25,1},{1,25},{10,18},{1... | collective-permute-start | bytes 786440 | tf_op jit(solution)/shard_map/ppermute | solution.py:505
  8.2 0.7 collective-permute-start.1
  8.9 0.5 collective-permute-start.2
  9.4 0.9 %collective-permute-start.3 = (f32[264,256]{1,0:T(8,128)S(1)}, f32[264,256]{1,0:T(8,128)}, u32[]{:S(2)}, u32[]{:S(2)}) collective-permute-start(f32[264,256]{1,0:T(8,128)S(1)} %get-tuple-element.39), channel_id=1, source_target_pairs={{0,32},{32,0},{64,96},{96,64},{1,33},{33,1},{65,97},{97,65},{2,34}... | collective-permute-start | bytes 811016 | tf_op jit(solution)/shard_map/ppermute | solution.py:505
  10.3 4.2 %collective-permute-start.4 = (f32[16,2,16,256]{3,2,1,0:T(8,128)}, f32[16,2,16,256]{3,2,1,0:T(8,128)S(1)}, u32[]{:S(2)}, u32[]{:S(2)}) collective-permute-start(f32[16,2,16,256]{3,2,1,0:T(8,128)} %get-tuple-element.42), channel_id=1, source_target_pairs={{1,2},{2,1},{3,4},{4,3},{5,6},{6,5},{7,0},{0,7},{9,10},{10,9},{11,... | collective-permute-start | bytes 1572872 | tf_op jit(solution)/shard_map/ppermute | solution.py:505
  14.5 0.1 add_sqrt_fusion.2
  14.5 0.1 add_sqrt_fusion
  14.6 0.1 sqrt.68
  14.8 0.1 sqrt.65
  14.8 0.1 mul.178
  14.9 0.1 add_sqrt_fusion.1
  15.0 0.8 collective-permute-done
  15.8 1.9 %collective-permute-start.5 = (f32[16,2,16,256]{3,2,1,0:T(8,128)}, f32[16,2,16,256]{3,2,1,0:T(8,128)}, u32[]{:S(2)}, u32[]{:S(2)}) collective-permute-start(f32[16,2,16,256]{3,2,1,0:T(8,128)} %copy-done.11), channel_id=1, source_target_pairs={{0,1},{1,0},{2,3},{3,2},{4,5},{5,4},{6,7},{7,6},{8,9},{9,8},{10,11... | collective-permute-start | bytes 1572872 | tf_op jit(solution)/shard_map/ppermute | solution.py:505
  17.7 0.8 dynamic_slice.3
  18.5 0.1 reshape.178.spec
  18.6 0.1 mul.174
  18.7 0.1 mul.175
  18.8 0.1 sqrt.71
  18.9 0.6 stack.25.tab
  19.6 3.8 %speeds.1 = (f32[2048,256]{1,0:T(8,128)S(1)}, f32[2048,256]{1,0:T(8,128)S(1)}, f32[2176,256]{1,0:T(8,128)S(1)}, f32[2304,256]{1,0:T(8,128)S(1)}, f32[16,256]{1,0:T(8,128)S(1)}, /*index=5*/f32[3,16,256]{2,1,0:T(8,128)S(1)}) custom-call(f32[7,144]{1,0:T(8,128)} %stack.25.tab, s32[16,256]{1,0:T(8,128)} %depth.5), custom_call_target="tpu_custom_call" | custom-call | flops 10000000 | tf_op jit(solution)/shard_map/speeds/pallas_call | solution.py:457
  23.4 1.4 %copy-done.1 = f32[2304,256]{1,0:T(8,128)} copy-done((f32[2304,256]{1,0:T(8,128)}, f32[2304,256]{1,0:T(8,128)S(1)}, u32[]{:S(2)}) %copy-start.1) | copy-done | bytes 2359320
  24.8 1.4 %copy-done.2 = f32[2176,256]{1,0:T(8,128)} copy-done((f32[2176,256]{1,0:T(8,128)}, f32[2176,256]{1,0:T(8,128)S(1)}, u32[]{:S(2)}) %copy-start.2) | copy-done | bytes 2228248
  26.2 1.3 %copy-done.3 = f32[2048,256]{1,0:T(8,128)} copy-done((f32[2048,256]{1,0:T(8,128)}, f32[2048,256]{1,0:T(8,128)S(1)}, u32[]{:S(2)}) %copy-start.3) | copy-done | bytes 2097176
  27.6 1.3 %copy-done.5 = f32[2048,256]{1,0:T(8,128)} copy-done((f32[2048,256]{1,0:T(8,128)}, f32[2048,256]{1,0:T(8,128)S(1)}, u32[]{:S(2)}) %copy-start.5) | copy-done | bytes 2097176
  28.8 0.0 collective-permute-done.2.x_od
  28.9 0.0 collective-permute-done.3.x_ev
  28.9 0.7 broadcast_in_dim.5.ccol
  29.6 0.1 broadcast_in_dim.4.kcol
  29.7 11.9 %stage_one_space.1 = (f32[2560,256]{1,0:T(8,128)S(1)}, f32[2048,256]{1,0:T(8,128)S(1)}, f32[16,256]{1,0:T(8,128)S(1)}, f32[128,256]{1,0:T(8,128)S(1)}, f32[128,2...) custom-call(f32[2560,256]{1,0:T(8,128)S(1)} %bitcast.11, ...), custom_call_target="tpu_custom_call", output_to_operand_aliasing={{0}: (0, {})} | custom-call | tf_op jit(solution)/shard_map/stage_one_space/pallas_call | solution.py:457
  41.6 1.5 %copy-done = f32[2560,256]{1,0:T(8,128)} copy-done((f32[2560,256]{1,0:T(8,128)}, f32[2560,256]{1,0:T(8,128)S(1)}, u32[]{:S(2)}) %copy-start) | copy-done | bytes 2621464
  43.1 1.4 %copy-done.7 = f32[2048,256]{1,0:T(8,128)} copy-done((f32[2048,256]{1,0:T(8,128)}, f32[2048,256]{1,0:T(8,128)S(1)}, u32[]{:S(2)}) %copy-start.7) | copy-done | bytes 2097176
  44.5 3.7 %collective-permute-start.6 = (f32[512,256]{1,0:T(8,128)S(1)}, f32[512,256]{1,0:T(8,128)S(1)}, u32[]{:S(2)}, u32[]{:S(2)}) collective-permute-start(f32[512,256]{1,0:T(8,128)S(1)} %get-tuple-element.48), channel_id=1, source_target_pairs={{1,2},{2,1},{3,4},{4,3},{5,6},{6,5},{7,0},{0,7},{9,10},{10,9},{11,... | collective-permute-start | bytes 1572872 | tf_op jit(solution)/shard_map/ppermute | solution.py:505
  48.2 0.0 collective-permute-start.7
  48.2 0.0 collective-permute-done.4
  48.2 0.0 collective-permute-done.5
  48.2 0.0 copy-start.4
  48.2 8.5 %stage_one_ky.1 = (f32[2560,256]{1,0:T(8,128)S(1)}, f32[256,256]{1,0:T(8,128)S(1)}, f32[256,256]{1,0:T(8,128)S(1)}, f32[256,256]{1,0:T(8,128)S(1)}) custom-call(f32[2560,256]{1,0:T(8,128)} %copy-done, f32[2048,256]{1,0:T(8,128)} %copy-done.7, f32[2304,256]{1,0:T(8,128)} %copy-done.1, f32[16,256]{1,0:T(8,128)S(1)} %get-tuple-element.34.gy, ...), custom_call_target="tpu_custom_call" | custom-call | tf_op jit(solution)/shard_map/stage_one_ky/pallas_call | solution.py:457
  56.7 1.5 %copy-done.6 = f32[2560,256]{1,0:T(8,128)} copy-done((f32[2560,256]{1,0:T(8,128)}, f32[2560,256]{1,0:T(8,128)S(1)}, u32[]{:S(2)}) %copy-start.6) | copy-done | bytes 2621464
  58.2 2.1 %collective-permute-start.8 = (f32[256,256]{1,0:T(8,128)S(1)}, f32[256,256]{1,0:T(8,128)S(1)}, u32[]{:S(2)}, u32[]{:S(2)}) collective-permute-start(f32[256,256]{1,0:T(8,128)S(1)} %get-tuple-element.50), channel_id=1, source_target_pairs={{8,16},{16,8},{24,0},{0,24},{9,17},{17,9},{25,1},{1,25},{10,18},{1... | collective-permute-start | bytes 786440 | tf_op jit(solution)/shard_map/ppermute | solution.py:505
  60.4 1.2 %collective-permute-start.9 = (f32[256,256]{1,0:T(8,128)S(1)}, f32[256,256]{1,0:T(8,128)S(1)}, u32[]{:S(2)}, u32[]{:S(2)}) collective-permute-start(f32[256,256]{1,0:T(8,128)S(1)} %get-tuple-element.51), channel_id=1, source_target_pairs={{0,8},{8,0},{16,24},{24,16},{1,9},{9,1},{17,25},{25,17},{2,10},{10... | collective-permute-start | bytes 786440 | tf_op jit(solution)/shard_map/ppermute | solution.py:505
  61.5 0.8 collective-permute-start.10
  62.3 5.9 %collective-permute-done.8.kx_od = f32[256,256]{1,0:T(8,128)S(1)} collective-permute-done((f32[256,256]{1,0:T(8,128)S(1)}, f32[256,256]{1,0:T(8,128)S(1)}, u32[]{:S(2)}, u32[]{:S(2)}) %collective-permute-start.8) | collective-permute-done | bytes 262176 | tf_op jit(solution)/shard_map/ppermute | solution.py:505
  68.2 0.0 collective-permute-done.9.kx_ev
  68.2 2.7 %collective-permute-done.10.x2 = f32[256,256]{1,0:T(8,128)S(1)} collective-permute-done((f32[256,256]{1,0:T(8,128)S(1)}, f32[256,256]{1,0:T(8,128)S(1)}, u32[]{:S(2)}, u32[]{:S(2)}) %collective-permute-start.10) | collective-permute-done | bytes 262176 | tf_op jit(solution)/shard_map/ppermute | solution.py:549
  71.0 13.7 %stage_two.1 = f32[2048,256]{1,0:T(8,128)} custom-call(f32[2560,256]{1,0:T(8,128)} %copy-done, f32[2560,256]{1,0:T(8,128)} %copy-done.6, f32[2048,256]{1,0:T(8,128)S(1)} %copy-done.4, f32[2048,256]{1,0:T(8,128)} %copy-done.5, f32[2176,256]{1,0:T(8,128)} %copy-done.2, f32[2304,256]{1,0:T(8,128)} %copy-done.1, f32[16,256]{1,0:T(8,128)S(1)} %get-tuple-element.45.gx, ...), custom_call_target="tpu_custom_call" | custom-call | tf_op jit(solution)/shard_map/stage_two/pallas_call | solution.py:457
  (31 shorter events, 0.1 us)
Async XLA Ops:
  0.0 0.7 copy-start.9
  0.7 28.9 %copy-start.8 = (s32[16,256]{1,0:T(8,128)S(1)}, s32[16,256]{1,0:T(8,128)}, u32[]{:S(2)}) copy-start(s32[16,256]{1,0:T(8,128)} %mask.5) | copy-start | bytes 49156
  0.7 28.9 %copy-start.10 = (s32[16,256]{1,0:T(8,128)S(1)}, s32[16,256]{1,0:T(8,128)}, u32[]{:S(2)}) copy-start(s32[16,256]{1,0:T(8,128)} %depth.5) | copy-start | bytes 49156
  4.8 0.8 copy-start.11
  5.6 10.2 %collective-permute-start = (f32[2,8,16,256]{3,2,1,0:T(8,128)}, f32[2,8,16,256]{3,2,1,0:T(8,128)}, u32[]{:S(2)}, u32[]{:S(2)}) collective-permute-start(f32[2,8,16,256]{3,2,1,0:T(8,128)} %get-tuple-element.36), channel_id=1, source_target_pairs={{8,16},{16,8},{24,0},{0,24},{9,17},{17,9},{25,1},{1,25},{10,18},{1... | collective-permute-start | bytes 786440 | tf_op jit(solution)/shard_map/ppermute | solution.py:505
  8.2 20.6 %collective-permute-start.1 = (f32[2,8,16,256]{3,2,1,0:T(8,128)}, f32[2,8,16,256]{3,2,1,0:T(8,128)}, u32[]{:S(2)}, u32[]{:S(2)}) collective-permute-start(f32[2,8,16,256]{3,2,1,0:T(8,128)} %get-tuple-element.37), channel_id=1, source_target_pairs={{0,8},{8,0},{16,24},{24,16},{1,9},{9,1},{17,25},{25,17},{2,10},{10... | collective-permute-start | bytes 786440 | tf_op jit(solution)/shard_map/ppermute | solution.py:505
  8.9 19.9 %collective-permute-start.2 = (f32[264,256]{1,0:T(8,128)}, f32[264,256]{1,0:T(8,128)}, u32[]{:S(2)}, u32[]{:S(2)}) collective-permute-start(f32[264,256]{1,0:T(8,128)} %get-tuple-element.38), channel_id=1, source_target_pairs={{32,64},{64,32},{96,0},{0,96},{33,65},{65,33},{97,1},{1,97},{34,66... | collective-permute-start | bytes 811016 | tf_op jit(solution)/shard_map/ppermute | solution.py:505
  9.4 19.5 %collective-permute-start.3 = (f32[264,256]{1,0:T(8,128)S(1)}, f32[264,256]{1,0:T(8,128)}, u32[]{:S(2)}, u32[]{:S(2)}) collective-permute-start(f32[264,256]{1,0:T(8,128)S(1)} %get-tuple-element.39), channel_id=1, source_target_pairs={{0,32},{32,0},{64,96},{96,64},{1,33},{33,1},{65,97},{97,65},{2,34}... | collective-permute-start | bytes 811016 | tf_op jit(solution)/shard_map/ppermute | solution.py:505
  10.3 37.9 %collective-permute-start.4 = (f32[16,2,16,256]{3,2,1,0:T(8,128)}, f32[16,2,16,256]{3,2,1,0:T(8,128)S(1)}, u32[]{:S(2)}, u32[]{:S(2)}) collective-permute-start(f32[16,2,16,256]{3,2,1,0:T(8,128)} %get-tuple-element.42), channel_id=1, source_target_pairs={{1,2},{2,1},{3,4},{4,3},{5,6},{6,5},{7,0},{0,7},{9,10},{10,9},{11,... | collective-permute-start | bytes 1572872 | tf_op jit(solution)/shard_map/ppermute | solution.py:505
  15.8 32.4 %collective-permute-start.5 = (f32[16,2,16,256]{3,2,1,0:T(8,128)}, f32[16,2,16,256]{3,2,1,0:T(8,128)}, u32[]{:S(2)}, u32[]{:S(2)}) collective-permute-start(f32[16,2,16,256]{3,2,1,0:T(8,128)} %copy-done.11), channel_id=1, source_target_pairs={{0,1},{1,0},{2,3},{3,2},{4,5},{5,4},{6,7},{7,6},{8,9},{9,8},{10,11... | collective-permute-start | bytes 1572872 | tf_op jit(solution)/shard_map/ppermute | solution.py:505
  23.4 1.4 %copy-start.1 = (f32[2304,256]{1,0:T(8,128)}, f32[2304,256]{1,0:T(8,128)S(1)}, u32[]{:S(2)}) copy-start(f32[2304,256]{1,0:T(8,128)S(1)} %get-tuple-element.33.aky) | copy-start | bytes 7077892
  24.8 1.4 %copy-start.2 = (f32[2176,256]{1,0:T(8,128)}, f32[2176,256]{1,0:T(8,128)S(1)}, u32[]{:S(2)}) copy-start(f32[2176,256]{1,0:T(8,128)S(1)} %get-tuple-element.32.rkx) | copy-start | bytes 6684676
  26.2 1.3 %copy-start.3 = (f32[2048,256]{1,0:T(8,128)}, f32[2048,256]{1,0:T(8,128)S(1)}, u32[]{:S(2)}) copy-start(f32[2048,256]{1,0:T(8,128)S(1)} %get-tuple-element.30.ax) | copy-start | bytes 6291460
  27.6 1.3 %copy-start.5 = (f32[2048,256]{1,0:T(8,128)}, f32[2048,256]{1,0:T(8,128)S(1)}, u32[]{:S(2)}) copy-start(f32[2048,256]{1,0:T(8,128)S(1)} %get-tuple-element.31.ay) | copy-start | bytes 6291460
  41.6 1.5 %copy-start = (f32[2560,256]{1,0:T(8,128)}, f32[2560,256]{1,0:T(8,128)S(1)}, u32[]{:S(2)}) copy-start(f32[2560,256]{1,0:T(8,128)S(1)} %get-tuple-element.40.np_ref) | copy-start | bytes 7864324
  43.1 1.4 %copy-start.7 = (f32[2048,256]{1,0:T(8,128)}, f32[2048,256]{1,0:T(8,128)S(1)}, u32[]{:S(2)}) copy-start(f32[2048,256]{1,0:T(8,128)S(1)} %get-tuple-element.41.p_ref) | copy-start | bytes 6291460
  44.5 26.5 %collective-permute-start.6 = (f32[512,256]{1,0:T(8,128)S(1)}, f32[512,256]{1,0:T(8,128)S(1)}, u32[]{:S(2)}, u32[]{:S(2)}) collective-permute-start(f32[512,256]{1,0:T(8,128)S(1)} %get-tuple-element.48), channel_id=1, source_target_pairs={{1,2},{2,1},{3,4},{4,3},{5,6},{6,5},{7,0},{0,7},{9,10},{10,9},{11,... | collective-permute-start | bytes 1572872 | tf_op jit(solution)/shard_map/ppermute | solution.py:505
  48.2 22.8 %collective-permute-start.7 = (f32[512,256]{1,0:T(8,128)S(1)}, f32[512,256]{1,0:T(8,128)S(1)}, u32[]{:S(2)}, u32[]{:S(2)}) collective-permute-start(f32[512,256]{1,0:T(8,128)S(1)} %get-tuple-element.49), channel_id=1, source_target_pairs={{0,1},{1,0},{2,3},{3,2},{4,5},{5,4},{6,7},{7,6},{8,9},{9,8},{10,11... | collective-permute-start | bytes 1572872 | tf_op jit(solution)/shard_map/ppermute | solution.py:505
  48.2 22.8 %copy-start.4 = (f32[2048,256]{1,0:T(8,128)S(1)}, f32[2048,256]{1,0:T(8,128)}, u32[]{:S(2)}) copy-start(f32[2048,256]{1,0:T(8,128)} %copy-done.3) | copy-start | bytes 6291460
  56.7 1.5 %copy-start.6 = (f32[2560,256]{1,0:T(8,128)}, f32[2560,256]{1,0:T(8,128)S(1)}, u32[]{:S(2)}) copy-start(f32[2560,256]{1,0:T(8,128)S(1)} %get-tuple-element.44.sp_in) | copy-start | bytes 7864324
  58.2 10.0 %collective-permute-start.8 = (f32[256,256]{1,0:T(8,128)S(1)}, f32[256,256]{1,0:T(8,128)S(1)}, u32[]{:S(2)}, u32[]{:S(2)}) collective-permute-start(f32[256,256]{1,0:T(8,128)S(1)} %get-tuple-element.50), channel_id=1, source_target_pairs={{8,16},{16,8},{24,0},{0,24},{9,17},{17,9},{25,1},{1,25},{10,18},{1... | collective-permute-start | bytes 786440 | tf_op jit(solution)/shard_map/ppermute | solution.py:505
  60.4 7.9 %collective-permute-start.9 = (f32[256,256]{1,0:T(8,128)S(1)}, f32[256,256]{1,0:T(8,128)S(1)}, u32[]{:S(2)}, u32[]{:S(2)}) collective-permute-start(f32[256,256]{1,0:T(8,128)S(1)} %get-tuple-element.51), channel_id=1, source_target_pairs={{0,8},{8,0},{16,24},{24,16},{1,9},{9,1},{17,25},{25,17},{2,10},{10... | collective-permute-start | bytes 786440 | tf_op jit(solution)/shard_map/ppermute | solution.py:505
  61.5 9.4 %collective-permute-start.10 = (f32[256,256]{1,0:T(8,128)S(1)}, f32[256,256]{1,0:T(8,128)S(1)}, u32[]{:S(2)}, u32[]{:S(2)}) collective-permute-start(f32[256,256]{1,0:T(8,128)S(1)} %get-tuple-element.52), channel_id=1, source_target_pairs={{0,96},{8,104},{16,48},{24,56},{32,0},{40,8},{48,80},{56,88},{64,3... | collective-permute-start | bytes 786440 | tf_op jit(solution)/shard_map/ppermute | solution.py:549

commit v2 on v0

v2 whole, which is shorter than its diff:
```python
import jax
import jax.numpy as jnp
from jax import lax
from jax.experimental import pallas as pl
from jax.experimental.pallas import tpu as pltpu
from jax.sharding import PartitionSpec as P

NKX = 64
NKY = 64

gravity = 9.81
spacing = 4.0
k_step = 0.04
time_step = 0.2

BX, BY, BS, NY = 16, 8, 16, 256
T = 4
f32 = jnp.float32
LIMIT = 8 * 2**20
EDGES = (0, 1, BY - 2, BY - 1)
MIDDLE = tuple(range(2, BY - 2))

X_SCALE = time_step / spacing * 0.5
K_SCALE = time_step / k_step * 0.5


def even_pairs(count):
    return [(i, i ^ 1) for i in range(count)]


def odd_pairs(count):
    pairs = []
    for i in range(1, count, 2):
        pairs += [(i, (i + 1) % count), ((i + 1) % count, i)]
    return pairs


def place():
    s, i, j = lax.axis_index("space"), lax.axis_index("kx"), lax.axis_index("ky")
    return s, i, j, i >= lax.axis_size("kx") // 2, j >= lax.axis_size("ky") // 2


def is_even(i):
    return i % 2 == 0


class Flow:
    def __init__(self):
        _, _, _, x_up, y_up = place()
        x0 = jnp.where(x_up, 0, 8)
        y0 = jnp.where(y_up, 0, 128)
        self.x_up = x_up
        self.x = (pl.multiple_of(x0, 8), pl.multiple_of(8 - x0, 8))
        self.y = (pl.multiple_of(y0, 128), pl.multiple_of(128 - y0, 128))
        self.x_roll = jnp.where(x_up, 1, 7)
        self.y_roll = jnp.where(y_up, 1, 127)
        self.rows = lax.broadcasted_iota(jnp.int32, (8, 128), 0)
        lanes = lax.broadcasted_iota(jnp.int32, (8, 128), 1)
        self.x_first = self.rows == jnp.where(x_up, 0, 7)
        self.x_last = self.rows == jnp.where(x_up, 7, 0)
        self.y_first = lanes == jnp.where(y_up, 0, 127)

    def natural(self, a, b):
        return pl.ds(self.x[a], 8), pl.ds(self.y[b], 128)

    def before_x(self, tiles, b, halo):
        first, second = (pltpu.roll(tiles[a][b], self.x_roll, 0) for a in range(2))
        return [jnp.where(self.x_first, halo, first), jnp.where(self.x_first, first, second)]

    def before_y(self, tiles, a):
        first, second = (pltpu.roll(tiles[a][b], self.y_roll, 1) for b in range(2))
        return [jnp.where(self.y_first, 0.0, first), jnp.where(self.y_first, first, second)]

    def edge_rows(self, tiles):
        out = []
        for up, down in ((7, 0), (6, 1)):
            rows = None
            for j in range(BY):
                shift = jnp.where(self.x_up, (j - up) % 8, (j - down) % 8)
                turned = pltpu.roll(tiles[j], shift, 0)
                rows = turned if rows is None else jnp.where(self.rows == j, turned, rows)
            out.append(rows)
        return out


def load(ref, slab):
    return [[ref[slab * T + 2 * a + b] for b in range(2)] for a in range(2)]


def store(ref, slab, tiles):
    for a in range(2):
        for b in range(2):
            ref[slab * T + 2 * a + b] = tiles[a][b]


def each(fn, *grids):
    return [[fn(*(g[a][b] for g in grids)) for b in range(2)] for a in range(2)]


def row(ref, i, j, b):
    return jnp.broadcast_to(ref[i * 2 + b][j : j + 1, :], (8, 128))


class Copies:
    def __init__(self, sems):
        self.sems, self.started = sems, []

    def start(self, src, dst):
        c = pltpu.make_async_copy(src, dst, self.sems.at[len(self.started)])
        c.start()
        self.started.append(c)

    def wait(self):
        for c in self.started:
            c.wait()


def first_messages(a_ref, depth, np_ref, ky_od, ky_ev, kx_od, kx_ev, x_od, x_ev, sems):
    s, i, j, x_up, _ = place()
    flow = Flow()
    copies = Copies(sems)
    tiles = [(a, b) for a in range(2) for b in range(2)]

    for a, b in tiles:
        x, y = flow.natural(a, b)
        copies.start(a_ref.at[:, pl.ds(jnp.where(is_even(j), 0, BY - 2), 2), x, y], ky_od.at[:, :, 2 * a + b])
        copies.start(a_ref.at[:, pl.ds(jnp.where(is_even(j), BY - 2, 0), 2), x, y], ky_ev.at[:, :, 2 * a + b])
    for a, b in tiles:
        x, y = flow.natural(a, b)
        copies.start(a_ref.at[:, :, x, y], np_ref.at[pl.ds(2, BX), :, 2 * a + b])
    for a, b in tiles:
        x, y = flow.natural(a, b)
        copies.start(a_ref.at[pl.ds(jnp.where(is_even(i), 0, BX - 2), 2), :, x, y], kx_od.at[:, :, 2 * a + b])
        copies.start(a_ref.at[pl.ds(jnp.where(is_even(i), BX - 2, 0), 2), :, x, y], kx_ev.at[:, :, 2 * a + b])
    for b in range(2):
        y = pl.ds(flow.y[b], 128)
        low = jnp.broadcast_to(depth[0:1, y].astype(f32), (8, 128))
        high = jnp.broadcast_to(depth[BS - 1 : BS, y].astype(f32), (8, 128))
        x_od[4 * BX + b] = jnp.where(is_even(s), low, high)
        x_ev[4 * BX + b] = jnp.where(is_even(s), high, low)
    copies.wait()

    def one_kx(i, carry):
        for b in range(2):
            rows = flow.edge_rows([np_ref[i + 2, j, 2 + b] for j in range(BY)])
            for l in range(2):
                x_od[l * 2 * BX + i * 2 + b] = rows[l]
                x_ev[l * 2 * BX + i * 2 + b] = rows[l]
        return carry

    lax.fori_loop(0, BX, one_kx, 0)


def shifted(h, axis, up):
    size = h.shape[axis]
    place_of = lax.broadcasted_iota(jnp.int32, h.shape, axis)
    if up:
        return jnp.where(place_of == size - 1, h, pltpu.roll(h, size - 1, axis))
    return jnp.where(place_of == 0, h, pltpu.roll(h, 1, axis))


def centre(first, i):
    return ((first + i - NKX // 2).astype(f32) + 0.5) * k_step


def lower_face(first, i):
    return (first + i - NKX // 2).astype(f32) * k_step


def wave(kx, ky):
    square = jnp.broadcast_to(kx * kx + ky * ky, (8, 128))
    inverse = lax.rsqrt(square)
    return square * inverse, inverse


def group_factor(k, inverse):
    return (0.5 * X_SCALE * gravity**0.5) * inverse * (inverse * jnp.sqrt(k))


def refract_factor(k):
    return (0.5 * K_SCALE * gravity**0.5) * k * jnp.sqrt(k)


def group(k, c, h):
    kh = k * h
    t = jnp.tanh(kh)
    return c * ((t + kh * (1.0 - t * t)) * lax.rsqrt(t))


def refract(k, c, h):
    t = jnp.tanh(k * h)
    return c * ((1.0 - t * t) * lax.rsqrt(t))


def speeds(depth, mask, ax, ay, rkx, aky, gy, heights, hold, geo):
    _, kx_place, ky_place, x_up, y_up = place()
    flow = Flow()
    kx_first, ky_first = kx_place * BX, ky_place * BY
    h = depth[...].astype(f32) * 0.01
    heights[...] = h
    y_next, y_last = shifted(h, 1, True), shifted(h, 1, False)
    hx = 0.5 * (h + jnp.where(x_up, shifted(h, 0, True), shifted(h, 0, False)))
    hy = 0.5 * (h + jnp.where(y_up, y_next, y_last))
    slope = (y_last - y_next) * (1.0 / (2.0 * spacing))
    x_flip, y_flip = jnp.where(x_up, 0, 1), jnp.where(y_up, 0, 1)
    for a in range(2):
        for b in range(2):
            at = (a ^ x_flip) * 2 + (b ^ y_flip)
            part = (slice(8 * a, 8 * a + 8), slice(128 * b, 128 * b + 128))
            gy[at] = slope[part]
            hold[at] = mask[part]
            geo[at] = h[part]
            geo[T + at] = hx[part]
            geo[2 * T + at] = hy[part]

    def kx_faces(i, j):
        k, _ = wave(lower_face(kx_first, i), centre(ky_first, j))
        c = refract_factor(k)
        store(rkx, i * BY + j, each(lambda h: refract(k, c, h), load(geo, 0)))

    def one_kx(i, carry):
        kx = centre(kx_first, i)
        for j in range(BY):
            ky = centre(ky_first, j)
            k, inverse = wave(kx, ky)
            c = group_factor(k, inverse)
            cx, cy = c * jnp.abs(kx), c * jnp.abs(ky)
            store(ax, i * BY + j, each(lambda h: group(k, cx, h), load(geo, 1)))
            store(ay, i * BY + j, each(lambda h: group(k, cy, h), load(geo, 2)))
            kx_faces(i, j)
        for j in range(BY + 1):
            k, _ = wave(kx, lower_face(ky_first, j))
            c = refract_factor(k)
            store(aky, i * (BY + 1) + j, each(lambda h, g: refract(k, c, h) * g, load(geo, 0), load(gy, 0)))
        return carry

    lax.fori_loop(0, BX, one_kx, 0)
    for j in range(BY):
        kx_faces(BX, j)


def space_change(flow, n, ax_ref, ay_ref, i, j, edge, halo_row, halo_flux):
    slab = i * BY + j
    ax, ay = load(ax_ref, slab), load(ay_ref, slab)
    n3 = each(lambda v: 3.0 * v, n)
    total = [[None, None], [None, None]]
    for b in range(2):
        ax[1][b] = jnp.where(flow.x_last, row(edge, i, j, b), ax[1][b])
        before = flow.before_x(n, b, row(halo_row, i, j, b))
        out = [[ax[a][b] * (n3[a][b] - before[a])] * 2 for a in range(2)]
        into = flow.before_x(out, b, row(halo_flux, i, j, b))
        for a in range(2):
            total[a][b] = out[a][b] - into[a]
    for a in range(2):
        before = flow.before_y(n, a)
        out = [ay[a][b] * (n3[a][b] - before[b]) for b in range(2)]
        into = flow.before_y([out, out], 0)
        for b in range(2):
            total[a][b] = total[a][b] + (out[b] - into[b])
    return total


def face(up, speed, n_2, n_1, n1, n2):
    near = jnp.where(up, n_1, n1)
    far = jnp.where(up, n_2, n2)
    return speed * (3.0 * near - far)


def kx_flux(gx, rkx, n_ref, i, j):
    n = [load(n_ref, (i + d) * BY + j) for d in range(4)]
    return each(lambda g, r, *n: face(g > 0, r * g, *n), gx, load(rkx, i * BY + j), *n)


def ky_flux(gy, aky, layers, i, f):
    return each(lambda g, w, *n: face(g > 0, w, *n), gy, load(aky, i * (BY + 1) + f), *layers[f : f + 4])


def halos(copies, od, ev, low, high, axis, flip):
    p, last = lax.axis_index(axis), lax.axis_size(axis) - 1
    middle = (last + 1) // 2
    todo = []
    for dst, src_even, src_odd, empty, turned in (
        (low, od, ev, p == 0, p == middle),
        (high, ev, od, p == last, p == middle - 1),
    ):
        full = jnp.logical_not(empty)

        @pl.when(empty)
        def _():
            dst[...] = jnp.zeros(dst.shape, f32)

        for t in range(T):
            at = jnp.where(turned, t ^ flip, t)
            sem = copies.sems.at[len(todo)]
            pair = [pltpu.make_async_copy(src.at[:, :, at], dst.at[:, :, t], sem) for src in (src_even, src_odd)]
            pl.when(jnp.logical_and(full, is_even(p)))(pair[0].start)
            pl.when(jnp.logical_and(full, jnp.logical_not(is_even(p))))(pair[1].start)
            todo.append((full, pair[0]))

    def wait():
        for full, c in todo:
            pl.when(full)(c.wait)

    return wait


def no_inflow(x_up):
    s = lax.axis_index("space")
    return s == jnp.where(x_up, 0, lax.axis_size("space") - 1)


def stage_one_edges(
    np_in, ax, ay, rkx, aky, heights, hold_ref, spec, kx_od, kx_ev, x_od, x_ev,
    np_ref, p_ref, gx, edge, halo_speed, xnear, xflux, ky2_od, ky2_ev, fk, hrow, sems,
):
    s, kx_place, ky_place, x_up, y_up = place()
    flow = Flow()
    slabs = (BX + 4) * BY
    kx_first, ky_first = kx_place * BX, ky_place * BY
    np5 = np_ref.reshape(BX + 4, BY, T, 8, 128)
    wait = halos(Copies(sems), kx_od, kx_ev, np5.at[pl.ds(0, 2)], np5.at[pl.ds(BX + 2, 2)], "kx", 2)
    h = heights[...]
    x_flip, y_flip = jnp.where(x_up, 0, 1), jnp.where(y_up, 0, 1)
    none = no_inflow(x_up)
    use_od = is_even(s) == x_up
    for b in range(2):
        y = b ^ y_flip
        at = 4 * BX + y
        mine = h[:, 128 * b : 128 * b + 128]
        od, ev = x_od[at][0:1, :] * 0.01, x_ev[at][0:1, :] * 0.01
        low = jnp.where(s == 0, mine[0:1, :], jnp.where(is_even(s), od, ev))
        high = jnp.where(s == lax.axis_size("space") - 1, mine[BS - 1 : BS, :], jnp.where(is_even(s), ev, od))
        place_of = lax.broadcasted_iota(jnp.int32, (BS, 128), 0)
        before = jnp.where(place_of == 0, low, pltpu.roll(mine, 1, 0))
        after = jnp.where(place_of == BS - 1, high, pltpu.roll(mine, BS - 1, 0))
        slope = (before - after) * (1.0 / (2.0 * spacing))
        for a in range(2):
            gx[(a ^ x_flip) * 2 + y] = slope[8 * a : 8 * a + 8, :]
        face_low = jnp.broadcast_to(0.5 * (low + mine[0:1, :]), (8, 128))
        face_high = jnp.broadcast_to(0.5 * (high + mine[BS - 1 : BS, :]), (8, 128))
        hrow[y] = jnp.where(x_up, face_high, face_low)
        hrow[2 + y] = jnp.where(x_up, face_low, face_high)
    ky = ((ky_first + flow.rows - NKY // 2).astype(f32) + 0.5) * k_step

    def edges(i, carry):
        kx = centre(kx_first, i)
        k, inverse = wave(kx, ky)
        c = group_factor(k, inverse) * jnp.abs(kx)
        for b in range(2):
            at = i * 2 + b
            near = jnp.where(use_od, x_od[at], x_ev[at])
            far = jnp.where(use_od, x_od[2 * BX + at], x_ev[2 * BX + at])
            edge[at] = group(k, c, hrow[b])
            speed = group(k, c, hrow[2 + b])
            halo_speed[at] = speed
            xnear[at] = jnp.where(none, 0.0, near)
            xflux[at] = jnp.where(none, 0.0, speed * (3.0 * near - far))
        return carry

    lax.fori_loop(0, BX, edges, 0)
    wait()

    g = load(gx, 0)
    for e, j in enumerate(EDGES):
        store(fk, e, kx_flux(g, rkx, np_ref, 0, j))

    def one_kx(i, carry):
        hold = each(lambda m: m == 1, load(hold_ref, 0))
        g = load(gx, 0)
        part = {}
        for e, j in enumerate(EDGES):
            n = load(np_ref, (i + 2) * BY + j)
            total = space_change(flow, n, ax, ay, i, j, edge, xnear, xflux)
            upper = kx_flux(g, rkx, np_ref, i + 1, j)
            lower = load(fk, e)
            store(fk, e, upper)
            part[j] = each(lambda n, t, u, v: n - (t + (u - v)), n, total, upper, lower)
            store(p_ref, i * len(EDGES) + e, part[j])

        def own(f, a, b):
            w = load(aky, i * (BY + 1) + f)
            a, b = (load(np_ref, (i + 2) * BY + j) for j in (a, b))
            return each(lambda w, a, b: w * (3.0 * a - b), w, a, b)

        def send(j, low, high, l, to):
            v = each(
                lambda m, p, u, v: jnp.where(m, spec[kx_first + i, ky_first + j], p - (u - v)), hold, part[j], high, low
            )
            for ref, here in ((ky2_od, to), (ky2_ev, jnp.logical_not(to))):
                @pl.when(here)
                def _():
                    store(ref, i * 2 + l, v)

        f = [own(0, 0, 1), own(1, 1, 2), own(2, 2, 3)]
        send(0, f[0], f[1], 0, is_even(ky_place))
        send(1, f[1], f[2], 1, is_even(ky_place))
        f = [own(BY - 2, BY - 3, BY - 4), own(BY - 1, BY - 2, BY - 3), own(BY, BY - 1, BY - 2)]
        send(BY - 2, f[0], f[1], 0, jnp.logical_not(is_even(ky_place)))
        send(BY - 1, f[1], f[2], 1, jnp.logical_not(is_even(ky_place)))
        return carry

    lax.fori_loop(0, BX, one_kx, 0)


def ky_column(n_ref, low, high, i):
    layers = [load(low, i * 2 + l) for l in range(2)]
    layers += [load(n_ref, (i + 2) * BY + j) for j in range(BY)]
    return layers + [load(high, i * 2 + l) for l in range(2)]


def stage_one_rest(
    np_ref, p_ref, ax, ay, rkx, aky, gx, gy, edge, xnear, xflux, hold_ref, spec, ky_od, ky_ev,
    sp_ref, kx2_od, kx2_ev, x2, fk, low, high, sems,
):
    s, kx_place, ky_place, x_up, y_up = place()
    flow = Flow()
    kx_first, ky_first = kx_place * BX, ky_place * BY
    wait = halos(
        Copies(sems), ky_od, ky_ev, low.reshape(BX, 2, T, 8, 128), high.reshape(BX, 2, T, 8, 128), "ky", 1
    )
    g = load(gx, 0)
    for e, j in enumerate(MIDDLE):
        store(fk, e, kx_flux(g, rkx, np_ref, 0, j))
    wait()

    def one_kx(i, carry):
        hold = each(lambda m: m == 1, load(hold_ref, 0))
        g, gk = load(gx, 0), load(gy, 0)
        layers = ky_column(np_ref, low, high, i)
        lower_y = ky_flux(gk, aky, layers, i, 0)
        last = [[], []]
        for j in range(BY):
            n = layers[j + 2]
            if j in EDGES:
                p = load(p_ref, i * len(EDGES) + EDGES.index(j))
            else:
                e = MIDDLE.index(j)
                total = space_change(flow, n, ax, ay, i, j, edge, xnear, xflux)
                upper = kx_flux(g, rkx, np_ref, i + 1, j)
                lower = load(fk, e)
                store(fk, e, upper)
                p = each(lambda n, t, u, v: n - (t + (u - v)), n, total, upper, lower)
            upper_y = ky_flux(gk, aky, layers, i, j + 1)
            v = each(
                lambda m, p, u, v: jnp.where(m, spec[kx_first + i, ky_first + j], p - (u - v)), hold, p, upper_y, lower_y
            )
            store(sp_ref, (i + 2) * BY + j, v)
            lower_y = upper_y
            for b in range(2):
                last[b].append(v[1][b])
        for b in range(2):
            rows = flow.edge_rows(last[b])
            for l in range(2):
                x2[l * 2 * BX + i * 2 + b] = rows[l]
        return carry

    lax.fori_loop(0, BX, one_kx, 0)
    size = 2 * BY * T
    copies = Copies(sems)
    copies.start(sp_ref.at[pl.ds(size + jnp.where(is_even(kx_place), 0, (BX - 2) * BY * T), size)], kx2_od)
    copies.start(sp_ref.at[pl.ds(size + jnp.where(is_even(kx_place), (BX - 2) * BY * T, 0), size)], kx2_ev)
    copies.wait()


def send_out(buffer, out, sems, i, layers, first):
    flow = Flow()
    todo = []
    for a in range(2):
        for b in range(2):
            x, y = flow.natural(a, b)
            t = 2 * a + b
            todo.append(
                pltpu.make_async_copy(
                    buffer.at[i, pl.ds(first, len(layers)), t],
                    out.at[i, pl.ds(layers[0], len(layers)), x, y],
                    sems.at[i, first, t],
                )
            )
    return todo


def stage_two_most(
    np_ref, sp_in, ax, ay, rkx, aky, gx, gy, edge, halo_speed, hold_ref, spec, kx_od, kx_ev, x2,
    sp_ref, q_ref, out, fk, xnear, xflux, done, sems, out_sems,
):
    s, kx_place, ky_place, x_up, y_up = place()
    flow = Flow()
    kx_first, ky_first = kx_place * BX, ky_place * BY
    sp5 = sp_ref.reshape(BX + 4, BY, T, 8, 128)
    wait = halos(Copies(sems), kx_od, kx_ev, sp5.at[pl.ds(0, 2)], sp5.at[pl.ds(BX + 2, 2)], "kx", 2)
    none = no_inflow(x_up)
    near = jnp.where(none, 0.0, x2[pl.ds(0, 2 * BX)])
    xnear[...] = near
    xflux[...] = (3.0 * near - jnp.where(none, 0.0, x2[pl.ds(2 * BX, 2 * BX)])) * halo_speed[...]
    wait()
    g = load(gx, 0)
    for j in range(BY):
        store(fk, j, kx_flux(g, rkx, sp_ref, 0, j))

    def one_kx(i, carry):
        hold = each(lambda m: m == 1, load(hold_ref, 0))
        g, gk = load(gx, 0), load(gy, 0)
        layers = [None, None] + [load(sp_ref, (i + 2) * BY + j) for j in range(BY)]
        lower_y = None
        for j in range(BY):
            n = layers[j + 2]
            total = space_change(flow, n, ax, ay, i, j, edge, xnear, xflux)
            upper = kx_flux(g, rkx, sp_ref, i + 1, j)
            lower = load(fk, j)
            store(fk, j, upper)
            first = load(np_ref, (i + 2) * BY + j)
            upper_y = ky_flux(gk, aky, layers, i, j + 1) if 2 <= j + 1 <= BY - 2 else None
            total = each(lambda t, u, v: t + (u - v), total, upper, lower)
            if upper_y is not None:
                total = each(lambda t, u: t + u, total, upper_y)
            if lower_y is not None:
                total = each(lambda t, u: t - u, total, lower_y)
            v = each(lambda a, n, t: 0.5 * ((a + n) - t), first, n, total)
            if j in EDGES:
                store(q_ref, i * len(EDGES) + EDGES.index(j), v)
            else:
                v = each(lambda m, v: jnp.where(m, spec[kx_first + i, ky_first + j], v), hold, v)
                for a in range(2):
                    for b in range(2):
                        done[i, MIDDLE.index(j), 2 * a + b] = v[a][b]
            lower_y = upper_y
        for c in send_out(done, out, out_sems, i, MIDDLE, 0):
            c.start()
        return carry

    lax.fori_loop(0, BX, one_kx, 0)

    def finish(i, carry):
        for c in send_out(done, out, out_sems, i, MIDDLE, 0):
            c.wait()
        return carry

    lax.fori_loop(0, BX, finish, 0)


def stage_two_edges(sp_ref, q_ref, aky, gy, hold_ref, spec, ky_od, ky_ev, out_in, out, low, high, done, sems, out_sems):
    s, kx_place, ky_place, x_up, y_up = place()
    kx_first, ky_first = kx_place * BX, ky_place * BY
    halos(
        Copies(sems), ky_od, ky_ev, low.reshape(BX, 2, T, 8, 128), high.reshape(BX, 2, T, 8, 128), "ky", 1
    )()
    parts = ((EDGES[:2], 0), (EDGES[2:], 2))

    def one_kx(i, carry):
        hold = each(lambda m: m == 1, load(hold_ref, 0))
        gk = load(gy, 0)
        layers = ky_column(sp_ref, low, high, i)
        flux = {f: ky_flux(gk, aky, layers, i, f) for f in (0, 1, BY - 1, BY)}
        for e, j in enumerate(EDGES):
            q = load(q_ref, i * len(EDGES) + e)
            if j in flux:
                q = each(lambda q, v: q + 0.5 * v, q, flux[j])
            if j + 1 in flux:
                q = each(lambda q, u: q - 0.5 * u, q, flux[j + 1])
            v = each(lambda m, v: jnp.where(m, spec[kx_first + i, ky_first + j], v), hold, q)
            for a in range(2):
                for b in range(2):
                    done[i, e, 2 * a + b] = v[a][b]
        for layers_of, first in parts:
            for c in send_out(done, out, out_sems, i, layers_of, first):
                c.start()
        return carry

    lax.fori_loop(0, BX, one_kx, 0)

    def finish(i, carry):
        for layers_of, first in parts:
            for c in send_out(done, out, out_sems, i, layers_of, first):
                c.wait()
        return carry

    lax.fori_loop(0, BX, finish, 0)


def call(kernel, outs, operands, spaces, out_spaces, scratch=(), alias=None, flops=0):
    whole = {
        "v": pl.BlockSpec(memory_space=pltpu.VMEM),
        "s": pl.BlockSpec(memory_space=pltpu.SMEM),
        "h": pl.BlockSpec(memory_space=pltpu.HBM),
    }
    return pl.pallas_call(
        kernel,
        out_shape=tuple(outs),
        in_specs=[whole[c] for c in spaces],
        out_specs=tuple(whole[c] for c in out_spaces),
        scratch_shapes=list(scratch),
        input_output_aliases=alias or {},
        compiler_params=pltpu.CompilerParams(vmem_limit_bytes=LIMIT),
        cost_estimate=pl.CostEstimate(flops=flops, bytes_accessed=0, transcendentals=0),
        name=kernel.__name__,
    )(*operands)


def per_device(action, depth_cm, inflow_mask, inflow):
    slabs, padded = BX * BY * T, (BX + 4) * BY * T
    edge_slabs = BX * len(EDGES) * T

    def v(*shape):
        return pltpu.VMEM(shape + (8, 128), f32)

    def swap(od, ev, axis):
        n = lax.axis_size(axis)
        return lax.ppermute(od, axis, odd_pairs(n)), lax.ppermute(ev, axis, even_pairs(n))

    sem = pltpu.SemaphoreType.DMA
    ky_shape, kx_shape = (BX, 2, T), (2, BY, T)
    np5, ky_od, ky_ev, kx_od, kx_ev, x_od, x_ev = call(
        first_messages,
        (v(BX + 4, BY, T), v(*ky_shape), v(*ky_shape), v(*kx_shape), v(*kx_shape), v(4 * BX + 2), v(4 * BX + 2)),
        (action, depth_cm),
        "hv",
        "v" * 7,
        [sem((20,))],
    )
    ky_od, ky_ev = swap(ky_od, ky_ev, "ky")
    kx_od, kx_ev = swap(kx_od, kx_ev, "kx")
    x_od, x_ev = swap(x_od, x_ev, "space")
    ax, ay, rkx, aky, gy, heights, hold = call(
        speeds,
        (v(slabs), v(slabs), v((BX + 1) * BY * T), v(BX * (BY + 1) * T), v(T), pltpu.VMEM((BS, NY), f32),
         pltpu.VMEM((T, 8, 128), jnp.int32)),
        (depth_cm, inflow_mask),
        "vv",
        "v" * 7,
        [v(3 * T)],
        flops=10_000_000,
    )
    np3 = np5.reshape(padded, 8, 128)
    np3, part, gx, edge, halo_speed, xnear, xflux, ky2_od, ky2_ev = call(
        stage_one_edges,
        (v(padded), v(edge_slabs), v(T), v(2 * BX), v(2 * BX), v(2 * BX), v(2 * BX), v(BX * 2 * T), v(BX * 2 * T)),
        (np3, ax, ay, rkx, aky, heights, hold, inflow, kx_od, kx_ev, x_od, x_ev),
        "vvvvvvvsvvvv",
        "v" * 9,
        [v(len(EDGES) * T), v(4), sem((2 * T,))],
        alias={0: 0},
    )
    ky2_od, ky2_ev = swap(ky2_od, ky2_ev, "ky")
    sp, kx2_od, kx2_ev, x2 = call(
        stage_one_rest,
        (v(padded), v(2 * BY * T), v(2 * BY * T), v(4 * BX)),
        (np3, part, ax, ay, rkx, aky, gx, gy, edge, xnear, xflux, hold, inflow, ky_od, ky_ev),
        "vvvvvvvvvvvvsvv",
        "v" * 4,
        [v(len(MIDDLE) * T), v(BX * 2 * T), v(BX * 2 * T), sem((2 * T,))],
    )
    kx2_od, kx2_ev = swap(kx2_od, kx2_ev, "kx")
    n_space, n_kx = lax.axis_size("space"), lax.axis_size("kx")
    ring = []
    for a in range(n_space):
        for b in range(n_kx):
            to = (a + (1 if b >= n_kx // 2 else -1)) % n_space
            ring.append((a * n_kx + b, to * n_kx + b))
    x2 = lax.ppermute(x2, ("space", "kx"), ring)
    sp, q, out = call(
        stage_two_most,
        (v(padded), v(edge_slabs), jax.ShapeDtypeStruct(action.shape, f32)),
        (np3, sp, ax, ay, rkx, aky, gx, gy, edge, halo_speed, hold, inflow,
         kx2_od.reshape(*kx_shape, 8, 128), kx2_ev.reshape(*kx_shape, 8, 128), x2),
        "vvvvvvvvvvvsvvv",
        "vvh",
        [v(BY * T), v(2 * BX), v(2 * BX), v(BX, len(MIDDLE), T), sem((2 * T,)), sem((BX, 1, T))],
        alias={1: 0},
    )
    (out,) = call(
        stage_two_edges,
        (jax.ShapeDtypeStruct(action.shape, f32),),
        (sp, q, aky, gy, hold, inflow, ky2_od.reshape(*ky_shape, 8, 128), ky2_ev.reshape(*ky_shape, 8, 128), out),
        "vvvvvsvvh",
        "h",
        [v(BX * 2 * T), v(BX * 2 * T), v(BX, len(EDGES), T), sem((2 * T,)), sem((BX, 4, T))],
        alias={8: 0},
    )
    return out


def solution(mesh):
    in_specs = (P("kx", "ky", "space", None), P("space", None), P("space", None), P())
    out_specs = P("kx", "ky", "space", None)
    return jax.shard_map(
        per_device, mesh=mesh, in_specs=in_specs, out_specs=out_specs, check_vma=False
    )
```

time: 162 us -> 62.8 us (0.39)
  the two profiles are of different devices: /device:TPU:15 before, /device:TPU:1 now
where the time goes in v2:
time: 62.8 us; the launch traced here: 62.5 us
  Pallas kernels  25.2 us (40%)
  starting transfers between devices  22 us (35%)
  waiting for transfers between devices  10.7 us (17%)
  local copies, waits for them, and re-layouts  4.49 us (7%)
    pallas_call x6, Pallas kernels, call(): pl.pallas_call(kernel, out_shape=tuple(outs), in_specs=[whole[c] for c in...  25.2 us
    ppermute x5, starting transfers between devices, swap(): lax.ppermute(od, axis, odd_pairs(n))  19 us
    ppermute x5, waiting for transfers between devices, swap(): lax.ppermute(od, axis, odd_pairs(n))  10.7 us
    unnamed x10, local copies, waits for them, and re-layouts  4.49 us
    ppermute x1, starting transfers between devices, per_device(): x2 = lax.ppermute(x2, ('space', 'kx'), ring)  2.48 us
  transfers between devices with their start and end apart: 11, of which 2 were waited for; matrix products, arithmetic and copies ran while one was open for 0% of the time, Pallas kernels for 31%

profile of v2, /device:TPU:1, one launch (start us, length us, event | category | flops | bytes accessed | tf_op | source)
XLA Modules:
  0.0 62.5 jit_solution(15939675652694930087)
XLA Ops:
  0.0 0.0 copy-start
  0.0 1.6 %copy-done = f32[16,8,16,256]{3,2,1,0:T(8,128)S(1)} copy-done((f32[16,8,16,256]{3,2,1,0:T(8,128)S(1)}, f32[16,8,16,256]{3,2,1,0:T(8,128)}, u32[]{:S(2)}) %copy-start) | copy-done | bytes 2097176
  1.6 0.0 copy-start.2
  1.6 0.7 %copy-done.2 = s32[16,256]{1,0:T(8,128)S(1)} copy-done((s32[16,256]{1,0:T(8,128)S(1)}, s32[16,256]{1,0:T(8,128)}, u32[]{:S(2)}) %copy-start.2) | copy-done | bytes 16408
  2.3 1.2 %first_messages.1 = (f32[20,8,4,8,128]{4,3,2,1,0:T(8,128)S(1)}, f32[16,2,4,8,128]{4,3,2,1,0:T(8,128)S(1)}, f32[16,2,4,8,128]{4,3,2,1,0:T(8,128)S(1)}, f32[2,8,4,...) custom-call(f32[16,8,16,256]{3,2,1,0:T(8,128)S(1)} %copy-done, ...), custom_call_target="tpu_custom_call" | custom-call | tf_op jit(solution)/shard_map/first_messages/pallas_call | solution.py:586
  3.5 4.4 %collective-permute-start = (f32[2,8,4,8,128]{4,3,2,1,0:T(8,128)S(1)}, f32[2,8,4,8,128]{4,3,2,1,0:T(8,128)S(1)}, u32[]{:S(2)}, u32[]{:S(2)}) collective-permute-start(f32[2,8,4,8,128]{4,3,2,1,0:T(8,128)S(1)} %get-tuple-element.42), channel_id=1, source_target_pairs={{8,16},{16,8},{24,0},{0,24},{9,17},{17,9},{25,1},{1,25},{10,18},{1... | collective-permute-start | bytes 786440 | tf_op jit(solution)/shard_map/ppermute | solution.py:608
  7.9 2.5 %collective-permute-start.2 = (f32[66,8,128]{2,1,0:T(8,128)S(1)}, f32[66,8,128]{2,1,0:T(8,128)S(1)}, u32[]{:S(2)}, u32[]{:S(2)}) collective-permute-start(f32[66,8,128]{2,1,0:T(8,128)S(1)} %get-tuple-element.44), channel_id=1, source_target_pairs={{32,64},{64,32},{96,0},{0,96},{33,65},{65,33},{97,1},{1,97},{34,66... | collective-permute-start | bytes 811016 | tf_op jit(solution)/shard_map/ppermute | solution.py:608
  10.3 0.0 collective-permute-start.3
  10.3 3.9 %collective-permute-start.4 = (f32[16,2,4,8,128]{4,3,2,1,0:T(8,128)S(1)}, f32[16,2,4,8,128]{4,3,2,1,0:T(8,128)S(1)}, u32[]{:S(2)}, u32[]{:S(2)}) collective-permute-start(f32[16,2,4,8,128]{4,3,2,1,0:T(8,128)S(1)} %get-tuple-element.53), channel_id=1, source_target_pairs={{1,2},{2,1},{3,4},{4,3},{5,6},{6,5},{7,0},{0,7},{9,10},{10,9},{11,... | collective-permute-start | bytes 1572872 | tf_op jit(solution)/shard_map/ppermute | solution.py:608
  14.2 0.0 collective-permute-start.5
  14.2 0.2 collective-permute-done.kx_od
  14.4 0.4 collective-permute-start.1
  14.8 0.0 copy-start.3
  14.8 0.7 %copy-done.3 = s32[16,256]{1,0:T(8,128)S(1)} copy-done((s32[16,256]{1,0:T(8,128)S(1)}, s32[16,256]{1,0:T(8,128)}, u32[]{:S(2)}) %copy-start.3) | copy-done | bytes 16408
  15.6 0.0 copy-start.4
  15.6 0.7 %copy-done.4 = s32[16,256]{1,0:T(8,128)S(1)} copy-done((s32[16,256]{1,0:T(8,128)S(1)}, s32[16,256]{1,0:T(8,128)}, u32[]{:S(2)}) %copy-start.4) | copy-done | bytes 16408
  16.3 3.7 %speeds.1 = (f32[512,8,128]{2,1,0:T(8,128)S(1)}, f32[512,8,128]{2,1,0:T(8,128)S(1)}, f32[544,8,128]{2,1,0:T(8,128)S(1)}, f32[576,8,128]{2,1,0:T(8,128)S(1)}, f32...) custom-call(s32[16,256]{1,0:T(8,128)S(1)} %copy-done.3, s32[16,256]{1,0:T(8,128)S(1)} %copy-done.4), custom_call_target="tpu_custom_call" | custom-call | flops 10000000 | tf_op jit(solution)/shard_map/speeds/pallas_call | solution.py:586
  20.0 0.0 collective-permute-done.1.kx_ev
  20.0 0.0 collective-permute-done.2.x_od
  20.0 0.0 collective-permute-done.3.x_ev
  20.0 0.0 copy-start.1
  20.0 0.7 %copy-done.1 = f32[64,64]{1,0:T(8,128)S(1)} copy-done((f32[64,64]{1,0:T(8,128)S(1)}, f32[64,64]{1,0:T(8,128)}, u32[]{:S(2)}) %copy-start.1) | copy-done | bytes 16408
  20.8 5.2 %stage_one_edges.1 = (f32[640,8,128]{2,1,0:T(8,128)S(1)}, f32[256,8,128]{2,1,0:T(8,128)S(1)}, f32[4,8,128]{2,1,0:T(8,128)S(1)}, f32[32,8,128]{2,1,0:T(8,128)S(1)...) custom-call(f32[640,8,128]{2,1,0:T(8,128)S(1)} %bitcast.5, ...), custom_call_target="tpu_custom_call", output_to_operand_aliasing={{0}: (0, {})} | custom-call | tf_op jit(solution)/shard_map/stage_one_edges/pallas_call | solution.py:586
  25.9 5.2 %collective-permute-start.9 = (f32[128,8,128]{2,1,0:T(8,128)S(1)}, f32[128,8,128]{2,1,0:T(8,128)S(1)}, u32[]{:S(2)}, u32[]{:S(2)}) collective-permute-start(f32[128,8,128]{2,1,0:T(8,128)S(1)} %get-tuple-element.62), channel_id=1, source_target_pairs={{1,2},{2,1},{3,4},{4,3},{5,6},{6,5},{7,0},{0,7},{9,10},{10,9},{11,... | collective-permute-start | bytes 1572872 | tf_op jit(solution)/shard_map/ppermute | solution.py:608
  31.2 0.0 collective-permute-start.10
  31.2 0.0 collective-permute-done.4.ky_od
  31.2 0.0 collective-permute-done.5.ky_ev
  31.2 4.3 %stage_one_rest.1 = (f32[640,8,128]{2,1,0:T(8,128)S(1)}, f32[64,8,128]{2,1,0:T(8,128)S(1)}, f32[64,8,128]{2,1,0:T(8,128)S(1)}, f32[64,8,128]{2,1,0:T(8,128)S(1)}) custom-call(f32[640,8,128]{2,1,0:T(8,128)S(1)} %get-tuple-element.46.np_ref, f32[256,8,128]{2,1,0:T(8,128)S(1)} %get-tuple-element.47.p_ref, f32[512,8,128]{2,1,0:T(8,128)S(1)} %get-tuple-element.36.ax, ...), custom_call_target="tpu_custom_call" | custom-call | tf_op jit(solution)/shard_map/stage_one_rest/pallas_call | solution.py:586
  35.5 3.0 %collective-permute-start.6 = (f32[64,8,128]{2,1,0:T(8,128)S(1)}, f32[64,8,128]{2,1,0:T(8,128)S(1)}, u32[]{:S(2)}, u32[]{:S(2)}) collective-permute-start(f32[64,8,128]{2,1,0:T(8,128)S(1)} %get-tuple-element.57), channel_id=1, source_target_pairs={{8,16},{16,8},{24,0},{0,24},{9,17},{17,9},{25,1},{1,25},{10,18},{1... | collective-permute-start | bytes 786440 | tf_op jit(solution)/shard_map/ppermute | solution.py:608
  38.5 0.1 collective-permute-start.7
  38.6 2.5 %collective-permute-start.8 = (f32[64,8,128]{2,1,0:T(8,128)S(1)}, f32[64,8,128]{2,1,0:T(8,128)S(1)}, u32[]{:S(2)}, u32[]{:S(2)}) collective-permute-start(f32[64,8,128]{2,1,0:T(8,128)S(1)} %get-tuple-element.59), channel_id=1, source_target_pairs={{0,96},{8,104},{16,48},{24,56},{32,0},{40,8},{48,80},{56,88},{64,3... | collective-permute-start | bytes 786440 | tf_op jit(solution)/shard_map/ppermute | solution.py:659
  41.1 10.5 %collective-permute-done.6 = f32[64,8,128]{2,1,0:T(8,128)S(1)} collective-permute-done((f32[64,8,128]{2,1,0:T(8,128)S(1)}, f32[64,8,128]{2,1,0:T(8,128)S(1)}, u32[]{:S(2)}, u32[]{:S(2)}) %collective-permute-start.6) | collective-permute-done | bytes 262176 | tf_op jit(solution)/shard_map/ppermute | solution.py:608
  51.6 0.0 collective-permute-done.7
  51.6 0.0 collective-permute-done.8.x2
  51.6 6.0 %stage_two_most.1 = (f32[640,8,128]{2,1,0:T(8,128)S(1)}, f32[256,8,128]{2,1,0:T(8,128)S(1)}, f32[16,8,16,256]{3,2,1,0:T(8,128)}) custom-call(f32[640,8,128]{2,1,0:T(8,128)S(1)} %get-tuple-element.46.np_ref, f32[640,8,128]{2,1,0:T(8,128)S(1)} %get-tuple-element.55.sp_in, f32[512,8,128]{2,1,0:T(8,128)S(1)} %get-tuple-element.36.ax, ...), custom_call_target="tpu_custom_call", output_to_operand_aliasing={{0}: (1, {})} | custom-call | tf_op jit(solution)/shard_map/stage_two_most/pallas_call | solution.py:586
  57.6 0.0 collective-permute-done.9
  57.6 0.0 collective-permute-done.10
  57.6 4.9 %stage_two_edges.1 = f32[16,8,16,256]{3,2,1,0:T(8,128)} custom-call(f32[640,8,128]{2,1,0:T(8,128)S(1)} %get-tuple-element.60.sp_ref, f32[256,8,128]{2,1,0:T(8,128)S(1)} %get-tuple-element.61.q_ref, f32[576,8,128]{2,1,0:T(8,128)S(1)} %get-tuple-element.39.aky, f32[4,8,128]{2,1,0:T(8,128)S(1)} %get-tuple-element.49.gy, ...), custom_call_target="tpu_custom_call", output_to_operand_aliasing={{}: (8, {})} | custom-call | tf_op jit(solution)/shard_map/stage_two_edges/pallas_call | solution.py:586
Async XLA Ops:
  0.0 1.6 %copy-start = (f32[16,8,16,256]{3,2,1,0:T(8,128)S(1)}, f32[16,8,16,256]{3,2,1,0:T(8,128)}, u32[]{:S(2)}) copy-start(f32[16,8,16,256]{3,2,1,0:T(8,128)} %a_ref.1) | copy-start | bytes 6291460
  1.6 0.7 %copy-start.2 = (s32[16,256]{1,0:T(8,128)S(1)}, s32[16,256]{1,0:T(8,128)}, u32[]{:S(2)}) copy-start(s32[16,256]{1,0:T(8,128)} %depth.3) | copy-start | bytes 49156
  3.5 10.9 %collective-permute-start = (f32[2,8,4,8,128]{4,3,2,1,0:T(8,128)S(1)}, f32[2,8,4,8,128]{4,3,2,1,0:T(8,128)S(1)}, u32[]{:S(2)}, u32[]{:S(2)}) collective-permute-start(f32[2,8,4,8,128]{4,3,2,1,0:T(8,128)S(1)} %get-tuple-element.42), channel_id=1, source_target_pairs={{8,16},{16,8},{24,0},{0,24},{9,17},{17,9},{25,1},{1,25},{10,18},{1... | collective-permute-start | bytes 786440 | tf_op jit(solution)/shard_map/ppermute | solution.py:608
  7.9 12.1 %collective-permute-start.2 = (f32[66,8,128]{2,1,0:T(8,128)S(1)}, f32[66,8,128]{2,1,0:T(8,128)S(1)}, u32[]{:S(2)}, u32[]{:S(2)}) collective-permute-start(f32[66,8,128]{2,1,0:T(8,128)S(1)} %get-tuple-element.44), channel_id=1, source_target_pairs={{32,64},{64,32},{96,0},{0,96},{33,65},{65,33},{97,1},{1,97},{34,66... | collective-permute-start | bytes 811016 | tf_op jit(solution)/shard_map/ppermute | solution.py:608
  10.3 9.7 %collective-permute-start.3 = (f32[66,8,128]{2,1,0:T(8,128)S(1)}, f32[66,8,128]{2,1,0:T(8,128)S(1)}, u32[]{:S(2)}, u32[]{:S(2)}) collective-permute-start(f32[66,8,128]{2,1,0:T(8,128)S(1)} %get-tuple-element.45), channel_id=1, source_target_pairs={{0,32},{32,0},{64,96},{96,64},{1,33},{33,1},{65,97},{97,65},{2,34}... | collective-permute-start | bytes 811016 | tf_op jit(solution)/shard_map/ppermute | solution.py:608
  10.3 20.8 %collective-permute-start.4 = (f32[16,2,4,8,128]{4,3,2,1,0:T(8,128)S(1)}, f32[16,2,4,8,128]{4,3,2,1,0:T(8,128)S(1)}, u32[]{:S(2)}, u32[]{:S(2)}) collective-permute-start(f32[16,2,4,8,128]{4,3,2,1,0:T(8,128)S(1)} %get-tuple-element.53), channel_id=1, source_target_pairs={{1,2},{2,1},{3,4},{4,3},{5,6},{6,5},{7,0},{0,7},{9,10},{10,9},{11,... | collective-permute-start | bytes 1572872 | tf_op jit(solution)/shard_map/ppermute | solution.py:608
  14.2 17.0 %collective-permute-start.5 = (f32[16,2,4,8,128]{4,3,2,1,0:T(8,128)S(1)}, f32[16,2,4,8,128]{4,3,2,1,0:T(8,128)S(1)}, u32[]{:S(2)}, u32[]{:S(2)}) collective-permute-start(f32[16,2,4,8,128]{4,3,2,1,0:T(8,128)S(1)} %get-tuple-element.54), channel_id=1, source_target_pairs={{0,1},{1,0},{2,3},{3,2},{4,5},{5,4},{6,7},{7,6},{8,9},{9,8},{10,11... | collective-permute-start | bytes 1572872 | tf_op jit(solution)/shard_map/ppermute | solution.py:608
  14.4 5.6 %collective-permute-start.1 = (f32[2,8,4,8,128]{4,3,2,1,0:T(8,128)S(1)}, f32[2,8,4,8,128]{4,3,2,1,0:T(8,128)S(1)}, u32[]{:S(2)}, u32[]{:S(2)}) collective-permute-start(f32[2,8,4,8,128]{4,3,2,1,0:T(8,128)S(1)} %get-tuple-element.43), channel_id=1, source_target_pairs={{0,8},{8,0},{16,24},{24,16},{1,9},{9,1},{17,25},{25,17},{2,10},{10... | collective-permute-start | bytes 786440 | tf_op jit(solution)/shard_map/ppermute | solution.py:608
  14.8 0.7 %copy-start.3 = (s32[16,256]{1,0:T(8,128)S(1)}, s32[16,256]{1,0:T(8,128)}, u32[]{:S(2)}) copy-start(s32[16,256]{1,0:T(8,128)} %depth.3) | copy-start | bytes 49156
  15.6 0.7 %copy-start.4 = (s32[16,256]{1,0:T(8,128)S(1)}, s32[16,256]{1,0:T(8,128)}, u32[]{:S(2)}) copy-start(s32[16,256]{1,0:T(8,128)} %mask.1) | copy-start | bytes 49156
  20.0 0.8 %copy-start.1 = (f32[64,64]{1,0:T(8,128)S(1)}, f32[64,64]{1,0:T(8,128)}, u32[]{:S(2)}) copy-start(f32[64,64]{1,0:T(8,128)} %spec.7) | copy-start | bytes 49156
  25.9 31.6 %collective-permute-start.9 = (f32[128,8,128]{2,1,0:T(8,128)S(1)}, f32[128,8,128]{2,1,0:T(8,128)S(1)}, u32[]{:S(2)}, u32[]{:S(2)}) collective-permute-start(f32[128,8,128]{2,1,0:T(8,128)S(1)} %get-tuple-element.62), channel_id=1, source_target_pairs={{1,2},{2,1},{3,4},{4,3},{5,6},{6,5},{7,0},{0,7},{9,10},{10,9},{11,... | collective-permute-start | bytes 1572872 | tf_op jit(solution)/shard_map/ppermute | solution.py:608
  31.2 26.4 %collective-permute-start.10 = (f32[128,8,128]{2,1,0:T(8,128)S(1)}, f32[128,8,128]{2,1,0:T(8,128)S(1)}, u32[]{:S(2)}, u32[]{:S(2)}) collective-permute-start(f32[128,8,128]{2,1,0:T(8,128)S(1)} %get-tuple-element.63), channel_id=1, source_target_pairs={{0,1},{1,0},{2,3},{3,2},{4,5},{5,4},{6,7},{7,6},{8,9},{9,8},{10,11... | collective-permute-start | bytes 1572872 | tf_op jit(solution)/shard_map/ppermute | solution.py:608
  35.5 16.1 %collective-permute-start.6 = (f32[64,8,128]{2,1,0:T(8,128)S(1)}, f32[64,8,128]{2,1,0:T(8,128)S(1)}, u32[]{:S(2)}, u32[]{:S(2)}) collective-permute-start(f32[64,8,128]{2,1,0:T(8,128)S(1)} %get-tuple-element.57), channel_id=1, source_target_pairs={{8,16},{16,8},{24,0},{0,24},{9,17},{17,9},{25,1},{1,25},{10,18},{1... | collective-permute-start | bytes 786440 | tf_op jit(solution)/shard_map/ppermute | solution.py:608
  38.5 13.0 %collective-permute-start.7 = (f32[64,8,128]{2,1,0:T(8,128)S(1)}, f32[64,8,128]{2,1,0:T(8,128)S(1)}, u32[]{:S(2)}, u32[]{:S(2)}) collective-permute-start(f32[64,8,128]{2,1,0:T(8,128)S(1)} %get-tuple-element.58), channel_id=1, source_target_pairs={{0,8},{8,0},{16,24},{24,16},{1,9},{9,1},{17,25},{25,17},{2,10},{10... | collective-permute-start | bytes 786440 | tf_op jit(solution)/shard_map/ppermute | solution.py:608
  38.6 13.0 %collective-permute-start.8 = (f32[64,8,128]{2,1,0:T(8,128)S(1)}, f32[64,8,128]{2,1,0:T(8,128)S(1)}, u32[]{:S(2)}, u32[]{:S(2)}) collective-permute-start(f32[64,8,128]{2,1,0:T(8,128)S(1)} %get-tuple-element.59), channel_id=1, source_target_pairs={{0,96},{8,104},{16,48},{24,56},{32,0},{40,8},{48,80},{56,88},{64,3... | collective-permute-start | bytes 786440 | tf_op jit(solution)/shard_map/ppermute | solution.py:659

commit v3 on v2

v3 whole, which is shorter than its diff:
```python
import jax
import jax.numpy as jnp
from jax import lax
from jax.experimental import pallas as pl
from jax.experimental.pallas import tpu as pltpu
from jax.sharding import PartitionSpec as P

NKX = 64
NKY = 64

gravity = 9.81
spacing = 4.0
k_step = 0.04
time_step = 0.2

BX, BY, BS, NY = 16, 8, 16, 256
T = 4
f32 = jnp.float32
LIMIT = 8 * 2**20
FIRST_LIMIT = 54 * 2**20
EDGES = (0, 1, BY - 2, BY - 1)
MIDDLE = tuple(range(2, BY - 2))

X_SCALE = time_step / spacing * 0.5
K_SCALE = time_step / k_step * 0.5


AXES = ("space", "kx", "ky")


def swaps(sizes, axis, odd, spare):
    pairs = []
    for n in range(sizes[0] * sizes[1] * sizes[2]):
        at = [n // (sizes[1] * sizes[2]), n // sizes[2] % sizes[1], n % sizes[2]]
        other = ((at[axis] + odd) ^ 1) - odd
        if 0 <= other < sizes[axis]:
            at[axis] = other
        else:
            at[spare] ^= 1
        pairs.append((n, (at[0] * sizes[1] + at[1]) * sizes[2] + at[2]))
    return pairs


def ring(sizes):
    pairs = []
    for a in range(sizes[0]):
        for b in range(sizes[1]):
            to = (a + (1 if b >= sizes[1] // 2 else -1)) % sizes[0]
            pairs.append((a * sizes[1] + b, to * sizes[1] + b))
    return pairs


def place():
    s, i, j = lax.axis_index("space"), lax.axis_index("kx"), lax.axis_index("ky")
    return s, i, j, i >= lax.axis_size("kx") // 2, j >= lax.axis_size("ky") // 2


def is_even(i):
    return i % 2 == 0


class Flow:
    def __init__(self):
        _, _, _, x_up, y_up = place()
        x0 = jnp.where(x_up, 0, 8)
        y0 = jnp.where(y_up, 0, 128)
        self.x_up = x_up
        self.x = (pl.multiple_of(x0, 8), pl.multiple_of(8 - x0, 8))
        self.y = (pl.multiple_of(y0, 128), pl.multiple_of(128 - y0, 128))
        self.x_roll = jnp.where(x_up, 1, 7)
        self.y_roll = jnp.where(y_up, 1, 127)
        self.rows = lax.broadcasted_iota(jnp.int32, (8, 128), 0)
        lanes = lax.broadcasted_iota(jnp.int32, (8, 128), 1)
        self.x_first = self.rows == jnp.where(x_up, 0, 7)
        self.x_last = self.rows == jnp.where(x_up, 7, 0)
        self.y_first = lanes == jnp.where(y_up, 0, 127)

    def natural(self, a, b):
        return pl.ds(self.x[a], 8), pl.ds(self.y[b], 128)

    def before_x(self, tiles, b, halo):
        first, second = (pltpu.roll(tiles[a][b], self.x_roll, 0) for a in range(2))
        return [jnp.where(self.x_first, halo, first), jnp.where(self.x_first, first, second)]

    def before_y(self, tiles, a):
        first, second = (pltpu.roll(tiles[a][b], self.y_roll, 1) for b in range(2))
        return [jnp.where(self.y_first, 0.0, first), jnp.where(self.y_first, first, second)]

    def edge_rows(self, tiles):
        out = []
        for up, down in ((7, 0), (6, 1)):
            rows = None
            for j in range(BY):
                shift = jnp.where(self.x_up, (j - up) % 8, (j - down) % 8)
                turned = pltpu.roll(tiles[j], shift, 0)
                rows = turned if rows is None else jnp.where(self.rows == j, turned, rows)
            out.append(rows)
        return out


def load(ref, slab):
    return [[ref[slab * T + 2 * a + b] for b in range(2)] for a in range(2)]


def store(ref, slab, tiles):
    for a in range(2):
        for b in range(2):
            ref[slab * T + 2 * a + b] = tiles[a][b]


def each(fn, *grids):
    return [[fn(*(g[a][b] for g in grids)) for b in range(2)] for a in range(2)]


def row(ref, i, j, b):
    return jnp.broadcast_to(ref[i * 2 + b][j : j + 1, :], (8, 128))


def wait_all(dst, sem):
    pltpu.make_async_copy(dst, dst, sem).wait()


def shifted(h, axis, up):
    size = h.shape[axis]
    place_of = lax.broadcasted_iota(jnp.int32, h.shape, axis)
    if up:
        return jnp.where(place_of == size - 1, h, pltpu.roll(h, size - 1, axis))
    return jnp.where(place_of == 0, h, pltpu.roll(h, 1, axis))


def centre(first, i):
    return ((first + i - NKX // 2).astype(f32) + 0.5) * k_step


def lower_face(first, i):
    return (first + i - NKX // 2).astype(f32) * k_step


def wave(kx, ky):
    square = jnp.broadcast_to(kx * kx + ky * ky, (8, 128))
    inverse = lax.rsqrt(square)
    return square * inverse, inverse


def group_factor(k, inverse):
    return (0.5 * X_SCALE * gravity**0.5) * inverse * (inverse * jnp.sqrt(k))


def refract_factor(k):
    return (0.5 * K_SCALE * gravity**0.5) * k * jnp.sqrt(k)


def group(k, c, h):
    kh = k * h
    t = jnp.tanh(kh)
    return c * ((t + kh * (1.0 - t * t)) * lax.rsqrt(t))


def refract(k, c, h):
    t = jnp.tanh(k * h)
    return c * ((1.0 - t * t) * lax.rsqrt(t))


def first_messages(
    a_ref, depth_ref, mask_ref, inflow_ref,
    np_ref, ky_od, ky_ev, kx_od, kx_ev, x_od, x_ev, depth, mask, inflow, ay, geo, sems,
):
    s, i, j, x_up, y_up = place()
    flow = Flow()
    own = np_ref.at[pl.ds(2, BX)]
    small = [
        pltpu.make_async_copy(src, dst, sems.at[n])
        for n, (src, dst) in enumerate(((depth_ref, depth), (mask_ref, mask), (inflow_ref, inflow)))
    ]
    for c in small:
        c.start()
    for a in range(2):
        for b in range(2):
            x, y = flow.natural(a, b)
            pltpu.make_async_copy(a_ref.at[:, :, x, y], own.at[:, :, 2 * a + b], sems.at[3]).start()
    for c in small:
        c.wait()
    h = depth[...].astype(f32) * 0.01
    hy = 0.5 * (h + jnp.where(y_up, shifted(h, 1, True), shifted(h, 1, False)))
    x_flip, y_flip = jnp.where(x_up, 0, 1), jnp.where(y_up, 0, 1)
    for a in range(2):
        for b in range(2):
            geo[(a ^ x_flip) * 2 + (b ^ y_flip)] = hy[8 * a : 8 * a + 8, 128 * b : 128 * b + 128]
    kx_first, ky_first = i * BX, j * BY

    def y_speeds(i, carry):
        kx = centre(kx_first, i)
        for j in range(BY):
            ky = centre(ky_first, j)
            k, inverse = wave(kx, ky)
            c = group_factor(k, inverse) * jnp.abs(ky)
            store(ay, i * BY + j, each(lambda h: group(k, c, h), load(geo, 0)))
        return carry

    lax.fori_loop(0, BX, y_speeds, 0)
    wait_all(own, sems.at[3])
    low = {"kx": jnp.where(is_even(i), 0, BX - 2), "ky": jnp.where(is_even(j), 0, BY - 2)}
    high = {"kx": jnp.where(is_even(i), BX - 2, 0), "ky": jnp.where(is_even(j), BY - 2, 0)}
    messages = [
        pltpu.make_async_copy(src, dst, sems.at[n])
        for n, (src, dst) in enumerate(
            (
                (own.at[:, pl.ds(low["ky"], 2)], ky_od),
                (own.at[:, pl.ds(high["ky"], 2)], ky_ev),
                (own.at[pl.ds(low["kx"], 2)], kx_od),
                (own.at[pl.ds(high["kx"], 2)], kx_ev),
            ),
            4,
        )
    ]
    for c in messages:
        c.start()
    for b in range(2):
        y = pl.ds(flow.y[b], 128)
        first = jnp.broadcast_to(depth[0:1, y].astype(f32), (8, 128))
        last = jnp.broadcast_to(depth[BS - 1 : BS, y].astype(f32), (8, 128))
        x_od[4 * BX + b] = jnp.where(is_even(s), first, last)
        x_ev[4 * BX + b] = jnp.where(is_even(s), last, first)

    def one_kx(i, carry):
        for b in range(2):
            rows = flow.edge_rows([np_ref[i + 2, j, 2 + b] for j in range(BY)])
            for l in range(2):
                x_od[l * 2 * BX + i * 2 + b] = rows[l]
                x_ev[l * 2 * BX + i * 2 + b] = rows[l]
        return carry

    lax.fori_loop(0, BX, one_kx, 0)
    for c in messages:
        c.wait()


def speeds(depth, mask, inflow, ax, rkx, aky, gy, heights, hold, spec, geo):
    _, kx_place, ky_place, x_up, y_up = place()
    flow = Flow()
    kx_first, ky_first = kx_place * BX, ky_place * BY
    h = depth[...].astype(f32) * 0.01
    heights[...] = h
    y_next, y_last = shifted(h, 1, True), shifted(h, 1, False)
    hx = 0.5 * (h + jnp.where(x_up, shifted(h, 0, True), shifted(h, 0, False)))
    slope = (y_last - y_next) * (1.0 / (2.0 * spacing))
    x_flip, y_flip = jnp.where(x_up, 0, 1), jnp.where(y_up, 0, 1)
    for a in range(2):
        for b in range(2):
            at = (a ^ x_flip) * 2 + (b ^ y_flip)
            part = (slice(8 * a, 8 * a + 8), slice(128 * b, 128 * b + 128))
            gy[at] = slope[part]
            hold[at] = mask[part]
            geo[at] = h[part]
            geo[T + at] = hx[part]

    lanes = lax.broadcasted_iota(jnp.int32, (8, NKY), 1)
    for half in range(BX // 8):
        rows = inflow[pl.ds(pl.multiple_of(kx_first + 8 * half, 8), 8), :]
        for j in range(BY):
            column = jnp.sum(jnp.where(lanes == ky_first + j, rows, 0.0), axis=1, keepdims=True)
            column = jnp.broadcast_to(column, (8, 128))
            for r in range(8):
                spec[(8 * half + r) * BY + j] = jnp.broadcast_to(column[r : r + 1, :], (8, 128))

    def kx_faces(i, j):
        k, _ = wave(lower_face(kx_first, i), centre(ky_first, j))
        c = refract_factor(k)
        store(rkx, i * BY + j, each(lambda h: refract(k, c, h), load(geo, 0)))

    def one_kx(i, carry):
        kx = centre(kx_first, i)
        for j in range(BY):
            ky = centre(ky_first, j)
            k, inverse = wave(kx, ky)
            c = group_factor(k, inverse)
            cx = c * jnp.abs(kx)
            store(ax, i * BY + j, each(lambda h: group(k, cx, h), load(geo, 1)))
            kx_faces(i, j)
        for j in range(BY + 1):
            k, _ = wave(kx, lower_face(ky_first, j))
            c = refract_factor(k)
            store(aky, i * (BY + 1) + j, each(lambda h, g: refract(k, c, h) * g, load(geo, 0), load(gy, 0)))
        return carry

    lax.fori_loop(0, BX, one_kx, 0)
    for j in range(BY):
        kx_faces(BX, j)


def space_change(flow, n, ax_ref, ay_ref, i, j, edge, halo_row, halo_flux):
    slab = i * BY + j
    ax, ay = load(ax_ref, slab), load(ay_ref, slab)
    n3 = each(lambda v: 3.0 * v, n)
    total = [[None, None], [None, None]]
    for b in range(2):
        ax[1][b] = jnp.where(flow.x_last, row(edge, i, j, b), ax[1][b])
        before = flow.before_x(n, b, 0.0 if halo_row is None else row(halo_row, i, j, b))
        out = [[ax[a][b] * (n3[a][b] - before[a])] * 2 for a in range(2)]
        into = flow.before_x(out, b, 0.0 if halo_flux is None else row(halo_flux, i, j, b))
        for a in range(2):
            total[a][b] = out[a][b] - into[a]
    for a in range(2):
        before = flow.before_y(n, a)
        out = [ay[a][b] * (n3[a][b] - before[b]) for b in range(2)]
        into = flow.before_y([out, out], 0)
        for b in range(2):
            total[a][b] = total[a][b] + (out[b] - into[b])
    return total


def face(up, speed, n_2, n_1, n1, n2):
    near = jnp.where(up, n_1, n1)
    far = jnp.where(up, n_2, n2)
    return speed * (3.0 * near - far)


def kx_flux(gx, rkx, n_ref, i, j):
    n = [load(n_ref, (i + d) * BY + j) for d in range(4)]
    return each(lambda g, r, *n: face(g > 0, r * g, *n), gx, load(rkx, i * BY + j), *n)


def ky_flux(gy, aky, layers, i, f):
    return each(lambda g, w, *n: face(g > 0, w, *n), gy, load(aky, i * (BY + 1) + f), *layers[f : f + 4])


class Halo:
    def __init__(self, od, ev, axis, flip):
        p, last = lax.axis_index(axis), lax.axis_size(axis) - 1
        middle = (last + 1) // 2
        self.od, self.ev, self.even = od, ev, is_even(p)
        self.low_empty, self.high_empty = p == 0, p == last
        self.low_at = [jnp.where(p == middle, t ^ flip, t) for t in range(T)]
        self.high_at = [jnp.where(p == middle - 1, t ^ flip, t) for t in range(T)]

    def take(self, first, second, slab, at, empty):
        def tile(t):
            r = slab * T + at[t]
            return jnp.where(empty, 0.0, jnp.where(self.even, first[r], second[r]))

        return [[tile(2 * a + b) for b in range(2)] for a in range(2)]

    def low(self, slab):
        return self.take(self.od, self.ev, slab, self.low_at, self.low_empty)

    def high(self, slab):
        return self.take(self.ev, self.od, slab, self.high_at, self.high_empty)


def pad_kx(n_ref, od, ev):
    halo = Halo(od, ev, "kx", 2)

    def one(r, carry):
        store(n_ref, r, halo.low(r))
        store(n_ref, (BX + 2) * BY + r, halo.high(r))
        return carry

    lax.fori_loop(0, 2 * BY, one, 0)


def no_inflow(x_up):
    s = lax.axis_index("space")
    return s == jnp.where(x_up, 0, lax.axis_size("space") - 1)


def stage_one_edges(
    np_in, ax, ay, rkx, aky, heights, hold_ref, spec, kx_od, kx_ev, x_od, x_ev,
    np_ref, p_ref, gx, edge, halo_speed, xnear, xflux, ky2_od, ky2_ev, fk, hrow,
):
    s, kx_place, ky_place, x_up, y_up = place()
    flow = Flow()
    kx_first, ky_first = kx_place * BX, ky_place * BY
    pad_kx(np_ref, kx_od, kx_ev)
    h = heights[...]
    x_flip, y_flip = jnp.where(x_up, 0, 1), jnp.where(y_up, 0, 1)
    none = no_inflow(x_up)
    use_od = is_even(s) == x_up
    for b in range(2):
        y = b ^ y_flip
        at = 4 * BX + y
        mine = h[:, 128 * b : 128 * b + 128]
        od, ev = x_od[at][0:1, :] * 0.01, x_ev[at][0:1, :] * 0.01
        low = jnp.where(s == 0, mine[0:1, :], jnp.where(is_even(s), od, ev))
        high = jnp.where(s == lax.axis_size("space") - 1, mine[BS - 1 : BS, :], jnp.where(is_even(s), ev, od))
        place_of = lax.broadcasted_iota(jnp.int32, (BS, 128), 0)
        before = jnp.where(place_of == 0, low, pltpu.roll(mine, 1, 0))
        after = jnp.where(place_of == BS - 1, high, pltpu.roll(mine, BS - 1, 0))
        slope = (before - after) * (1.0 / (2.0 * spacing))
        for a in range(2):
            gx[(a ^ x_flip) * 2 + y] = slope[8 * a : 8 * a + 8, :]
        face_low = jnp.broadcast_to(0.5 * (low + mine[0:1, :]), (8, 128))
        face_high = jnp.broadcast_to(0.5 * (high + mine[BS - 1 : BS, :]), (8, 128))
        hrow[y] = jnp.where(x_up, face_high, face_low)
        hrow[2 + y] = jnp.where(x_up, face_low, face_high)
    ky = ((ky_first + flow.rows - NKY // 2).astype(f32) + 0.5) * k_step

    def edges(i, carry):
        kx = centre(kx_first, i)
        k, inverse = wave(kx, ky)
        c = group_factor(k, inverse) * jnp.abs(kx)
        for b in range(2):
            at = i * 2 + b
            near = jnp.where(use_od, x_od[at], x_ev[at])
            far = jnp.where(use_od, x_od[2 * BX + at], x_ev[2 * BX + at])
            edge[at] = group(k, c, hrow[b])
            speed = group(k, c, hrow[2 + b])
            halo_speed[at] = speed
            xnear[at] = jnp.where(none, 0.0, near)
            xflux[at] = jnp.where(none, 0.0, speed * (3.0 * near - far))
        return carry

    lax.fori_loop(0, BX, edges, 0)

    g = load(gx, 0)
    for e, j in enumerate(EDGES):
        store(fk, e, kx_flux(g, rkx, np_ref, 0, j))

    def one_kx(i, carry):
        hold = each(lambda m: m == 1, load(hold_ref, 0))
        g = load(gx, 0)
        part = {}
        for e, j in enumerate(EDGES):
            n = load(np_ref, (i + 2) * BY + j)
            total = space_change(flow, n, ax, ay, i, j, edge, xnear, xflux)
            upper = kx_flux(g, rkx, np_ref, i + 1, j)
            lower = load(fk, e)
            store(fk, e, upper)
            part[j] = each(lambda n, t, u, v: n - (t + (u - v)), n, total, upper, lower)
            store(p_ref, i * len(EDGES) + e, part[j])

        def own(f, a, b):
            w = load(aky, i * (BY + 1) + f)
            a, b = (load(np_ref, (i + 2) * BY + j) for j in (a, b))
            return each(lambda w, a, b: w * (3.0 * a - b), w, a, b)

        def send(j, low, high, l, to):
            v = each(
                lambda m, p, u, v: jnp.where(m, spec[i * BY + j], p - (u - v)), hold, part[j], high, low
            )
            for ref, here in ((ky2_od, to), (ky2_ev, jnp.logical_not(to))):
                @pl.when(here)
                def _():
                    store(ref, i * 2 + l, v)

        f = [own(0, 0, 1), own(1, 1, 2), own(2, 2, 3)]
        send(0, f[0], f[1], 0, is_even(ky_place))
        send(1, f[1], f[2], 1, is_even(ky_place))
        f = [own(BY - 2, BY - 3, BY - 4), own(BY - 1, BY - 2, BY - 3), own(BY, BY - 1, BY - 2)]
        send(BY - 2, f[0], f[1], 0, jnp.logical_not(is_even(ky_place)))
        send(BY - 1, f[1], f[2], 1, jnp.logical_not(is_even(ky_place)))
        return carry

    lax.fori_loop(0, BX, one_kx, 0)


def ky_column(n_ref, halo, i):
    layers = [halo.low(i * 2 + l) for l in range(2)]
    layers += [load(n_ref, (i + 2) * BY + j) for j in range(BY)]
    return layers + [halo.high(i * 2 + l) for l in range(2)]


def stage_one_rest(
    np_ref, p_ref, ax, ay, rkx, aky, gx, gy, edge, xnear, xflux, hold_ref, spec, ky_od, ky_ev,
    sp_ref, kx2_od, kx2_ev, x2, fk, sems,
):
    s, kx_place, ky_place, x_up, y_up = place()
    flow = Flow()
    halo = Halo(ky_od, ky_ev, "ky", 1)
    g = load(gx, 0)
    for e, j in enumerate(MIDDLE):
        store(fk, e, kx_flux(g, rkx, np_ref, 0, j))

    def one_kx(i, carry):
        hold = each(lambda m: m == 1, load(hold_ref, 0))
        g, gk = load(gx, 0), load(gy, 0)
        layers = ky_column(np_ref, halo, i)
        lower_y = ky_flux(gk, aky, layers, i, 0)
        last = [[], []]
        for j in range(BY):
            n = layers[j + 2]
            if j in EDGES:
                p = load(p_ref, i * len(EDGES) + EDGES.index(j))
            else:
                e = MIDDLE.index(j)
                total = space_change(flow, n, ax, ay, i, j, edge, xnear, xflux)
                upper = kx_flux(g, rkx, np_ref, i + 1, j)
                lower = load(fk, e)
                store(fk, e, upper)
                p = each(lambda n, t, u, v: n - (t + (u - v)), n, total, upper, lower)
            upper_y = ky_flux(gk, aky, layers, i, j + 1)
            v = each(
                lambda m, p, u, v: jnp.where(m, spec[i * BY + j], p - (u - v)), hold, p, upper_y, lower_y
            )
            store(sp_ref, (i + 2) * BY + j, v)
            lower_y = upper_y
            for b in range(2):
                last[b].append(v[1][b])
        for b in range(2):
            rows = flow.edge_rows(last[b])
            for l in range(2):
                x2[l * 2 * BX + i * 2 + b] = rows[l]
        return carry

    lax.fori_loop(0, BX, one_kx, 0)
    size = 2 * BY * T
    low, high = 0, (BX - 2) * BY * T
    copies = [
        pltpu.make_async_copy(sp_ref.at[pl.ds(size + jnp.where(is_even(kx_place), *at), size)], ref, sems.at[n])
        for n, (ref, at) in enumerate(((kx2_od, (low, high)), (kx2_ev, (high, low))))
    ]
    for c in copies:
        c.start()
    for c in copies:
        c.wait()


STEP = 4


def send_out(buffer, out, sem, i):
    @pl.when(i % STEP == STEP - 1)
    def _():
        flow = Flow()
        rows = pl.ds(i - (STEP - 1), STEP)
        for a in range(2):
            for b in range(2):
                x, y = flow.natural(a, b)
                pltpu.make_async_copy(buffer.at[rows, :, 2 * a + b], out.at[rows, :, x, y], sem).start()


def stage_two_inner(np_ref, sp_in, ax, ay, rkx, aky, gx, gy, edge, sp_ref, q_ref, fk):
    flow = Flow()
    nothing = each(lambda v: jnp.zeros_like(v), load(gx, 0))

    def clear(r, carry):
        store(sp_ref, r, nothing)
        store(sp_ref, (BX + 2) * BY + r, nothing)
        return carry

    lax.fori_loop(0, 2 * BY, clear, 0)
    g = load(gx, 0)
    for j in range(BY):
        store(fk, j, kx_flux(g, rkx, sp_ref, 0, j))

    def one_kx(i, carry):
        g, gk = load(gx, 0), load(gy, 0)
        layers = [nothing] * 2 + [load(sp_ref, (i + 2) * BY + j) for j in range(BY)] + [nothing] * 2
        lower_y = ky_flux(gk, aky, layers, i, 0)
        for j in range(BY):
            slab = i * BY + j
            n = layers[j + 2]
            total = space_change(flow, n, ax, ay, i, j, edge, None, None)
            upper = kx_flux(g, rkx, sp_ref, i + 1, j)
            lower = load(fk, j)
            store(fk, j, upper)
            upper_y = ky_flux(gk, aky, layers, i, j + 1)
            v = each(
                lambda a, n, t, u, v, p, q: 0.5 * ((a + n) - ((t + (u - v)) + (p - q))),
                load(np_ref, (i + 2) * BY + j), n, total, upper, lower, upper_y, lower_y,
            )
            store(q_ref, slab, v)
            lower_y = upper_y
        return carry

    lax.fori_loop(0, BX, one_kx, 0)


def halo_terms(g, low_speeds, high_speeds, low, high):
    up = [each(lambda g, w: jnp.where(g > 0, 0.5 * w, 0.0), g, w) for w in low_speeds]
    down = [each(lambda g, w: jnp.where(g > 0, 0.0, 0.5 * w), g, w) for w in high_speeds]
    end = each(lambda w, a, b: w * (3.0 * a - b), up[0], low[1], low[0])
    second = each(lambda w, a: w * a, up[1], low[1])
    top = each(lambda w, a, b: w * (3.0 * a - b), down[1], high[0], high[1])
    below_top = each(lambda w, a: w * a, down[0], high[0])
    return (
        each(lambda a, b: a + b, end, second),
        each(lambda b: -b, second),
        below_top,
        each(lambda a, b: -(a + b), top, below_top),
    )


def stage_two_outer(
    q_in, ax, rkx, aky, gx, gy, halo_speed, hold_ref, spec, kx_od, kx_ev, x2, ky_od, ky_ev,
    q_ref, out, xnear, xflux, done, sem,
):
    _, _, _, x_up, _ = place()
    flow = Flow()
    none = no_inflow(x_up)
    near = jnp.where(none, 0.0, x2[pl.ds(0, 2 * BX)])
    xnear[...] = 0.5 * near
    xflux[...] = (3.0 * near - jnp.where(none, 0.0, x2[pl.ds(2 * BX, 2 * BX)])) * (0.5 * halo_speed[...])
    kx_halo, ky_halo = Halo(kx_od, kx_ev, "kx", 2), Halo(ky_od, ky_ev, "ky", 1)

    def kx_ends(j, carry):
        g = load(gx, 0)
        speed = [each(lambda r, g: r * g, load(rkx, f * BY + j), g) for f in (0, 1, BX - 1, BX)]
        low = [kx_halo.low(l * BY + j) for l in range(2)]
        high = [kx_halo.high(l * BY + j) for l in range(2)]
        terms = halo_terms(g, speed[:2], speed[2:], low, high)
        for i, term in zip((0, 1, BX - 2, BX - 1), terms):
            slab = i * BY + j
            store(q_ref, slab, each(lambda q, t: q + t, load(q_ref, slab), term))
        return carry

    lax.fori_loop(0, BY, kx_ends, 0)
    second = flow.rows == jnp.where(x_up, 1, 6)

    def one_kx(i, carry):
        hold = each(lambda m: m == 1, load(hold_ref, 0))
        gk = load(gy, 0)
        speed = [load(aky, i * (BY + 1) + f) for f in (0, 1, BY - 1, BY)]
        low = [ky_halo.low(i * 2 + l) for l in range(2)]
        high = [ky_halo.high(i * 2 + l) for l in range(2)]
        terms = dict(zip(EDGES, halo_terms(gk, speed[:2], speed[2:], low, high)))
        for j in range(BY):
            slab = i * BY + j
            q = load(q_ref, slab)
            if j in terms:
                q = each(lambda q, t: q + t, q, terms[j])
            for b in range(2):
                less = ax[slab * T + b] * row(xnear, i, j, b)
                into = less + row(xflux, i, j, b)
                q[0][b] = q[0][b] + jnp.where(
                    flow.x_first, into, jnp.where(second, -pltpu.roll(less, flow.x_roll, 0), 0.0)
                )
            for a in range(2):
                for b in range(2):
                    done[i, j, 2 * a + b] = jnp.where(hold[a][b], spec[slab], q[a][b])
        send_out(done, out, sem, i)
        return carry

    lax.fori_loop(0, BX, one_kx, 0)
    wait_all(done, sem)


def call(kernel, outs, operands, spaces, out_spaces, scratch=(), alias=None, us=1, limit=LIMIT):
    whole = {
        "v": pl.BlockSpec(memory_space=pltpu.VMEM),
        "h": pl.BlockSpec(memory_space=pltpu.HBM),
    }
    return pl.pallas_call(
        kernel,
        out_shape=tuple(outs),
        in_specs=[whole[c] for c in spaces],
        out_specs=tuple(whole[c] for c in out_spaces),
        scratch_shapes=list(scratch),
        input_output_aliases=alias or {},
        compiler_params=pltpu.CompilerParams(vmem_limit_bytes=limit),
        cost_estimate=pl.CostEstimate(flops=int(us * 1e9), bytes_accessed=0, transcendentals=0),
        name=kernel.__name__,
    )(*operands)


def per_device(action, depth_cm, inflow_mask, inflow):
    slabs, padded = BX * BY * T, (BX + 4) * BY * T
    edge_slabs, ky_tiles, kx_tiles = BX * len(EDGES) * T, BX * 2 * T, 2 * BY * T
    sizes = [lax.axis_size(axis) for axis in AXES]

    def v(*shape):
        return pltpu.VMEM(shape + (8, 128), f32)

    def swap(od, ev, axis, spare):
        at, beside = AXES.index(axis), AXES.index(spare)
        return (
            lax.ppermute(od, AXES, swaps(sizes, at, 1, beside)),
            lax.ppermute(ev, AXES, swaps(sizes, at, 0, beside)),
        )

    sem = pltpu.SemaphoreType.DMA
    np5, ky_od, ky_ev, kx_od, kx_ev, x_od, x_ev, depth, mask, spectrum, ay = call(
        first_messages,
        (v(BX + 4, BY, T), v(BX, 2, T), v(BX, 2, T), v(2, BY, T), v(2, BY, T), v(4 * BX + 2), v(4 * BX + 2),
         pltpu.VMEM((BS, NY), jnp.int32), pltpu.VMEM((BS, NY), jnp.int32), pltpu.VMEM((NKX, NKY), f32), v(slabs)),
        (action, depth_cm, inflow_mask, inflow),
        "hhhh",
        "v" * 11,
        [v(T), sem((8,))],
        us=0,
        limit=FIRST_LIMIT,
    )
    ky_od, ky_ev = (m.reshape(ky_tiles, 8, 128) for m in swap(ky_od, ky_ev, "ky", "kx"))
    kx_od, kx_ev = (m.reshape(kx_tiles, 8, 128) for m in swap(kx_od, kx_ev, "kx", "space"))
    x_od, x_ev = swap(x_od, x_ev, "space", "kx")
    ax, rkx, aky, gy, heights, hold, spec = call(
        speeds,
        (v(slabs), v((BX + 1) * BY * T), v(BX * (BY + 1) * T), v(T), pltpu.VMEM((BS, NY), f32),
         pltpu.VMEM((T, 8, 128), jnp.int32), v(BX * BY)),
        (depth, mask, spectrum),
        "vvv",
        "v" * 7,
        [v(2 * T)],
        us=4,
    )
    np3 = np5.reshape(padded, 8, 128)
    np3, part, gx, edge, halo_speed, xnear, xflux, ky2_od, ky2_ev = call(
        stage_one_edges,
        (v(padded), v(edge_slabs), v(T), v(2 * BX), v(2 * BX), v(2 * BX), v(2 * BX), v(ky_tiles), v(ky_tiles)),
        (np3, ax, ay, rkx, aky, heights, hold, spec, kx_od, kx_ev, x_od, x_ev),
        "v" * 12,
        "v" * 9,
        [v(len(EDGES) * T), v(4)],
        alias={0: 0},
        us=0,
    )
    ky2_od, ky2_ev = swap(ky2_od, ky2_ev, "ky", "kx")
    sp, kx2_od, kx2_ev, x2 = call(
        stage_one_rest,
        (v(padded), v(kx_tiles), v(kx_tiles), v(4 * BX)),
        (np3, part, ax, ay, rkx, aky, gx, gy, edge, xnear, xflux, hold, spec, ky_od, ky_ev),
        "v" * 15,
        "v" * 4,
        [v(len(MIDDLE) * T), sem((2,))],
        us=0,
    )
    kx2_od, kx2_ev = swap(kx2_od, kx2_ev, "kx", "space")
    x2 = lax.ppermute(x2, AXES[:2], ring(sizes))
    sp, q = call(
        stage_two_inner,
        (v(padded), v(slabs)),
        (np3, sp, ax, ay, rkx, aky, gx, gy, edge),
        "v" * 9,
        "vv",
        [v(BY * T)],
        alias={1: 0},
        us=4,
    )
    _, out = call(
        stage_two_outer,
        (v(slabs), jax.ShapeDtypeStruct(action.shape, f32)),
        (q, ax, rkx, aky, gx, gy, halo_speed, hold, spec, kx2_od, kx2_ev, x2, ky2_od, ky2_ev),
        "v" * 14,
        "vh",
        [v(2 * BX), v(2 * BX), v(BX, BY, T), sem],
        alias={0: 0},
        us=0,
    )
    return out


def solution(mesh):
    in_specs = (P("kx", "ky", "space", None), P("space", None), P("space", None), P())
    out_specs = P("kx", "ky", "space", None)
    return jax.shard_map(
        per_device, mesh=mesh, in_specs=in_specs, out_specs=out_specs, check_vma=False
    )
```

time: 62.8 us -> 44.2 us (0.70)
  the two profiles are of different devices: /device:TPU:1 before, /device:TPU:8 now
where the time goes in v3:
time: 44.2 us; the launch traced here: 44.1 us
  Pallas kernels  18.4 us (42%)
  starting transfers between devices  15.4 us (35%)
  waiting for transfers between devices  10.2 us (23%)
    pallas_call x6, Pallas kernels, call(): pl.pallas_call(kernel, out_shape=tuple(outs), in_specs=[whole[c] for c in...  18.4 us
    ppermute x5, starting transfers between devices, swap(): lax.ppermute(od, AXES, swaps(sizes, at, 1, beside))  9.94 us
    ppermute x5, waiting for transfers between devices, swap(): lax.ppermute(od, AXES, swaps(sizes, at, 1, beside))  6.19 us
    ppermute x5, starting transfers between devices, swap(): lax.ppermute(ev, AXES, swaps(sizes, at, 0, beside))  3.99 us
    ppermute x1, waiting for transfers between devices, per_device(): x2 = lax.ppermute(x2, AXES[:2], ring(sizes))  2.81 us
    ppermute x1, starting transfers between devices, per_device(): x2 = lax.ppermute(x2, AXES[:2], ring(sizes))  1.48 us
    ppermute x5, waiting for transfers between devices, swap(): lax.ppermute(ev, AXES, swaps(sizes, at, 0, beside))  1.17 us
  transfers between devices with their start and end apart: 11, of which 4 were waited for; matrix products, arithmetic and copies ran while one was open for 0% of the time, Pallas kernels for 31%

profile of v3, /device:TPU:8, one launch (start us, length us, event | category | flops | bytes accessed | tf_op | source)
XLA Modules:
  0.0 44.1 jit_solution(9469290565139164817)
XLA Ops:
  0.0 2.8 %first_messages.1 = (f32[20,8,4,8,128]{4,3,2,1,0:T(8,128)S(1)}, f32[16,2,4,8,128]{4,3,2,1,0:T(8,128)S(1)}, f32[16,2,4,8,128]{4,3,2,1,0:T(8,128)S(1)}, f32[2,8,4,...) custom-call(f32[16,8,16,256]{3,2,1,0:T(8,128)} %a_ref.1, ...), custom_call_target="tpu_custom_call" | custom-call | tf_op jit(solution)/shard_map/first_messages/pallas_call | solution.py:642
  2.8 1.6 %collective-permute-start = (f32[2,8,4,8,128]{4,3,2,1,0:T(8,128)S(1)}, f32[2,8,4,8,128]{4,3,2,1,0:T(8,128)S(1)}, u32[]{:S(2)}, u32[]{:S(2)}) collective-permute-start(f32[2,8,4,8,128]{4,3,2,1,0:T(8,128)S(1)} %get-tuple-element.49), channel_id=1, source_target_pairs={{0,32},{1,33},{2,34},{3,35},{4,36},{5,37},{6,38},{7,39},{8,16},{9,... | collective-permute-start | bytes 786440 | tf_op jit(solution)/shard_map/ppermute | solution.py:666
  4.4 0.9 %collective-permute-start.1 = (f32[2,8,4,8,128]{4,3,2,1,0:T(8,128)S(1)}, f32[2,8,4,8,128]{4,3,2,1,0:T(8,128)S(1)}, u32[]{:S(2)}, u32[]{:S(2)}) collective-permute-start(f32[2,8,4,8,128]{4,3,2,1,0:T(8,128)S(1)} %get-tuple-element.50), channel_id=1, source_target_pairs={{0,8},{1,9},{2,10},{3,11},{4,12},{5,13},{6,14},{7,15},{8,0},{9,1},... | collective-permute-start | bytes 786440 | tf_op jit(solution)/shard_map/ppermute | solution.py:667
  5.3 0.0 collective-permute-start.2
  5.3 3.0 %collective-permute-start.3 = (f32[66,8,128]{2,1,0:T(8,128)S(1)}, f32[66,8,128]{2,1,0:T(8,128)S(1)}, u32[]{:S(2)}, u32[]{:S(2)}) collective-permute-start(f32[66,8,128]{2,1,0:T(8,128)S(1)} %get-tuple-element.52), channel_id=1, source_target_pairs={{0,32},{1,33},{2,34},{3,35},{4,36},{5,37},{6,38},{7,39},{8,40},{9,... | collective-permute-start | bytes 811016 | tf_op jit(solution)/shard_map/ppermute | solution.py:667
  8.3 4.8 %collective-permute-start.4 = (f32[16,2,4,8,128]{4,3,2,1,0:T(8,128)S(1)}, f32[16,2,4,8,128]{4,3,2,1,0:T(8,128)S(1)}, u32[]{:S(2)}, u32[]{:S(2)}) collective-permute-start(f32[16,2,4,8,128]{4,3,2,1,0:T(8,128)S(1)} %get-tuple-element.60), channel_id=1, source_target_pairs={{0,8},{1,2},{2,1},{3,4},{4,3},{5,6},{6,5},{7,15},{8,0},{9,10},{10,... | collective-permute-start | bytes 1572872 | tf_op jit(solution)/shard_map/ppermute | solution.py:666
  13.1 0.0 collective-permute-done
  13.1 0.0 collective-permute-start.5
  13.1 2.9 %speeds.1 = (f32[512,8,128]{2,1,0:T(8,128)S(1)}, f32[544,8,128]{2,1,0:T(8,128)S(1)}, f32[576,8,128]{2,1,0:T(8,128)S(1)}, f32[4,8,128]{2,1,0:T(8,128)S(1)}, f32[1...) custom-call(s32[16,256]{1,0:T(8,128)S(1)} %get-tuple-element.39.depth, ...), custom_call_target="tpu_custom_call" | custom-call | flops 4000000000 | tf_op jit(solution)/shard_map/speeds/pallas_call | solution.py:642
  16.1 0.0 collective-permute-done.1
  16.1 0.0 collective-permute-done.2.x_od
  16.1 0.0 collective-permute-done.3.x_ev
  16.1 4.0 %stage_one_edges.1 = (f32[640,8,128]{2,1,0:T(8,128)S(1)}, f32[256,8,128]{2,1,0:T(8,128)S(1)}, f32[4,8,128]{2,1,0:T(8,128)S(1)}, f32[32,8,128]{2,1,0:T(8,128)S(1)...) custom-call(f32[640,8,128]{2,1,0:T(8,128)S(1)} %bitcast.5, ...), custom_call_target="tpu_custom_call", output_to_operand_aliasing={{0}: (0, {})} | custom-call | tf_op jit(solution)/shard_map/stage_one_edges/pallas_call | solution.py:642
  20.1 3.5 %collective-permute-start.9 = (f32[128,8,128]{2,1,0:T(8,128)S(1)}, f32[128,8,128]{2,1,0:T(8,128)S(1)}, u32[]{:S(2)}, u32[]{:S(2)}) collective-permute-start(f32[128,8,128]{2,1,0:T(8,128)S(1)} %get-tuple-element.68), channel_id=1, source_target_pairs={{0,8},{1,2},{2,1},{3,4},{4,3},{5,6},{6,5},{7,15},{8,0},{9,10},{10,... | collective-permute-start | bytes 1572872 | tf_op jit(solution)/shard_map/ppermute | solution.py:666
  23.6 0.0 collective-permute-start.10
  23.6 2.4 %collective-permute-done.4 = f32[16,2,4,8,128]{4,3,2,1,0:T(8,128)S(1)} collective-permute-done((f32[16,2,4,8,128]{4,3,2,1,0:T(8,128)S(1)}, f32[16,2,4,8,128]{4,3,2,1,0:T(8,128)S(1)}, u32[]{:S(2)}, u32[]{:S(2)}) %collective-permute-start.4) | collective-permute-done | bytes 524320 | tf_op jit(solution)/shard_map/ppermute | solution.py:666
  26.0 1.2 %collective-permute-done.5 = f32[16,2,4,8,128]{4,3,2,1,0:T(8,128)S(1)} collective-permute-done((f32[16,2,4,8,128]{4,3,2,1,0:T(8,128)S(1)}, f32[16,2,4,8,128]{4,3,2,1,0:T(8,128)S(1)}, u32[]{:S(2)}, u32[]{:S(2)}) %collective-permute-start.5) | collective-permute-done | bytes 524320 | tf_op jit(solution)/shard_map/ppermute | solution.py:667
  27.1 3.1 %stage_one_rest.1 = (f32[640,8,128]{2,1,0:T(8,128)S(1)}, f32[64,8,128]{2,1,0:T(8,128)S(1)}, f32[64,8,128]{2,1,0:T(8,128)S(1)}, f32[64,8,128]{2,1,0:T(8,128)S(1)}) custom-call(f32[640,8,128]{2,1,0:T(8,128)S(1)} %get-tuple-element.53.np_ref, f32[256,8,128]{2,1,0:T(8,128)S(1)} %get-tuple-element.54.p_ref, f32[512,8,128]{2,1,0:T(8,128)S(1)} %get-tuple-element.42.ax, ...), custom_call_target="tpu_custom_call" | custom-call | tf_op jit(solution)/shard_map/stage_one_rest/pallas_call | solution.py:642
  30.2 0.1 collective-permute-start.6
  30.3 0.1 collective-permute-start.7
  30.4 1.5 %collective-permute-start.8 = (f32[64,8,128]{2,1,0:T(8,128)S(1)}, f32[64,8,128]{2,1,0:T(8,128)S(1)}, u32[]{:S(2)}, u32[]{:S(2)}) collective-permute-start(f32[64,8,128]{2,1,0:T(8,128)S(1)} %get-tuple-element.67), channel_id=1, source_target_pairs={{0,96},{8,104},{16,48},{24,56},{32,0},{40,8},{48,80},{56,88},{64,3... | collective-permute-start | bytes 786440 | tf_op jit(solution)/shard_map/ppermute | solution.py:717
  31.9 3.6 %stage_two_inner.1 = (f32[640,8,128]{2,1,0:T(8,128)S(1)}, f32[512,8,128]{2,1,0:T(8,128)S(1)}) custom-call(f32[640,8,128]{2,1,0:T(8,128)S(1)} %get-tuple-element.53.np_ref, f32[640,8,128]{2,1,0:T(8,128)S(1)} %get-tuple-element.62.sp_in, f32[512,8,128]{2,1,0:T(8,128)S(1)} %get-tuple-element.42.ax, ...), custom_call_target="tpu_custom_call", output_to_operand_aliasing={{0}: (1, {})} | custom-call | flops 4000000000 | tf_op jit(solution)/shard_map/stage_two_inner/pallas_call | solution.py:642
  35.5 3.8 %collective-permute-done.6.kx_od = f32[64,8,128]{2,1,0:T(8,128)S(1)} collective-permute-done((f32[64,8,128]{2,1,0:T(8,128)S(1)}, f32[64,8,128]{2,1,0:T(8,128)S(1)}, u32[]{:S(2)}, u32[]{:S(2)}) %collective-permute-start.6) | collective-permute-done | bytes 262176 | tf_op jit(solution)/shard_map/ppermute | solution.py:666
  39.3 0.0 collective-permute-done.7.kx_ev
  39.3 2.8 %collective-permute-done.8.x2 = f32[64,8,128]{2,1,0:T(8,128)S(1)} collective-permute-done((f32[64,8,128]{2,1,0:T(8,128)S(1)}, f32[64,8,128]{2,1,0:T(8,128)S(1)}, u32[]{:S(2)}, u32[]{:S(2)}) %collective-permute-start.8) | collective-permute-done | bytes 262176 | tf_op jit(solution)/shard_map/ppermute | solution.py:717
  42.1 0.0 collective-permute-done.9.ky_od
  42.1 0.0 collective-permute-done.10.ky_ev
  42.1 1.9 %stage_two_outer.1 = (f32[512,8,128]{2,1,0:T(8,128)S(1)}, f32[16,8,16,256]{3,2,1,0:T(8,128)}) custom-call(f32[512,8,128]{2,1,0:T(8,128)S(1)} %get-tuple-element.63.q_in, f32[512,8,128]{2,1,0:T(8,128)S(1)} %get-tuple-element.42.ax, f32[544,8,128]{2,1,0:T(8,128)S(1)} %get-tuple-element.44.rkx, ...), custom_call_target="tpu_custom_call", output_to_operand_aliasing={{0}: (0, {})} | custom-call | tf_op jit(solution)/shard_map/stage_two_outer/pallas_call | solution.py:642
Async XLA Ops:
  2.8 10.3 %collective-permute-start = (f32[2,8,4,8,128]{4,3,2,1,0:T(8,128)S(1)}, f32[2,8,4,8,128]{4,3,2,1,0:T(8,128)S(1)}, u32[]{:S(2)}, u32[]{:S(2)}) collective-permute-start(f32[2,8,4,8,128]{4,3,2,1,0:T(8,128)S(1)} %get-tuple-element.49), channel_id=1, source_target_pairs={{0,32},{1,33},{2,34},{3,35},{4,36},{5,37},{6,38},{7,39},{8,16},{9,... | collective-permute-start | bytes 786440 | tf_op jit(solution)/shard_map/ppermute | solution.py:666
  4.4 11.7 %collective-permute-start.1 = (f32[2,8,4,8,128]{4,3,2,1,0:T(8,128)S(1)}, f32[2,8,4,8,128]{4,3,2,1,0:T(8,128)S(1)}, u32[]{:S(2)}, u32[]{:S(2)}) collective-permute-start(f32[2,8,4,8,128]{4,3,2,1,0:T(8,128)S(1)} %get-tuple-element.50), channel_id=1, source_target_pairs={{0,8},{1,9},{2,10},{3,11},{4,12},{5,13},{6,14},{7,15},{8,0},{9,1},... | collective-permute-start | bytes 786440 | tf_op jit(solution)/shard_map/ppermute | solution.py:667
  5.3 10.8 %collective-permute-start.2 = (f32[66,8,128]{2,1,0:T(8,128)S(1)}, f32[66,8,128]{2,1,0:T(8,128)S(1)}, u32[]{:S(2)}, u32[]{:S(2)}) collective-permute-start(f32[66,8,128]{2,1,0:T(8,128)S(1)} %get-tuple-element.51), channel_id=1, source_target_pairs={{0,8},{1,9},{2,10},{3,11},{4,12},{5,13},{6,14},{7,15},{8,0},{9,1},... | collective-permute-start | bytes 811016 | tf_op jit(solution)/shard_map/ppermute | solution.py:666
  5.3 10.8 %collective-permute-start.3 = (f32[66,8,128]{2,1,0:T(8,128)S(1)}, f32[66,8,128]{2,1,0:T(8,128)S(1)}, u32[]{:S(2)}, u32[]{:S(2)}) collective-permute-start(f32[66,8,128]{2,1,0:T(8,128)S(1)} %get-tuple-element.52), channel_id=1, source_target_pairs={{0,32},{1,33},{2,34},{3,35},{4,36},{5,37},{6,38},{7,39},{8,40},{9,... | collective-permute-start | bytes 811016 | tf_op jit(solution)/shard_map/ppermute | solution.py:667
  8.3 17.7 %collective-permute-start.4 = (f32[16,2,4,8,128]{4,3,2,1,0:T(8,128)S(1)}, f32[16,2,4,8,128]{4,3,2,1,0:T(8,128)S(1)}, u32[]{:S(2)}, u32[]{:S(2)}) collective-permute-start(f32[16,2,4,8,128]{4,3,2,1,0:T(8,128)S(1)} %get-tuple-element.60), channel_id=1, source_target_pairs={{0,8},{1,2},{2,1},{3,4},{4,3},{5,6},{6,5},{7,15},{8,0},{9,10},{10,... | collective-permute-start | bytes 1572872 | tf_op jit(solution)/shard_map/ppermute | solution.py:666
  13.1 14.0 %collective-permute-start.5 = (f32[16,2,4,8,128]{4,3,2,1,0:T(8,128)S(1)}, f32[16,2,4,8,128]{4,3,2,1,0:T(8,128)S(1)}, u32[]{:S(2)}, u32[]{:S(2)}) collective-permute-start(f32[16,2,4,8,128]{4,3,2,1,0:T(8,128)S(1)} %get-tuple-element.61), channel_id=1, source_target_pairs={{0,1},{1,0},{2,3},{3,2},{4,5},{5,4},{6,7},{7,6},{8,9},{9,8},{10,11... | collective-permute-start | bytes 1572872 | tf_op jit(solution)/shard_map/ppermute | solution.py:667
  20.1 22.0 %collective-permute-start.9 = (f32[128,8,128]{2,1,0:T(8,128)S(1)}, f32[128,8,128]{2,1,0:T(8,128)S(1)}, u32[]{:S(2)}, u32[]{:S(2)}) collective-permute-start(f32[128,8,128]{2,1,0:T(8,128)S(1)} %get-tuple-element.68), channel_id=1, source_target_pairs={{0,8},{1,2},{2,1},{3,4},{4,3},{5,6},{6,5},{7,15},{8,0},{9,10},{10,... | collective-permute-start | bytes 1572872 | tf_op jit(solution)/shard_map/ppermute | solution.py:666
  23.6 18.5 %collective-permute-start.10 = (f32[128,8,128]{2,1,0:T(8,128)S(1)}, f32[128,8,128]{2,1,0:T(8,128)S(1)}, u32[]{:S(2)}, u32[]{:S(2)}) collective-permute-start(f32[128,8,128]{2,1,0:T(8,128)S(1)} %get-tuple-element.69), channel_id=1, source_target_pairs={{0,1},{1,0},{2,3},{3,2},{4,5},{5,4},{6,7},{7,6},{8,9},{9,8},{10,11... | collective-permute-start | bytes 1572872 | tf_op jit(solution)/shard_map/ppermute | solution.py:667
  30.2 9.1 %collective-permute-start.6 = (f32[64,8,128]{2,1,0:T(8,128)S(1)}, f32[64,8,128]{2,1,0:T(8,128)S(1)}, u32[]{:S(2)}, u32[]{:S(2)}) collective-permute-start(f32[64,8,128]{2,1,0:T(8,128)S(1)} %get-tuple-element.65), channel_id=1, source_target_pairs={{0,32},{1,33},{2,34},{3,35},{4,36},{5,37},{6,38},{7,39},{8,16},{9,... | collective-permute-start | bytes 786440 | tf_op jit(solution)/shard_map/ppermute | solution.py:666
  30.3 9.0 %collective-permute-start.7 = (f32[64,8,128]{2,1,0:T(8,128)S(1)}, f32[64,8,128]{2,1,0:T(8,128)S(1)}, u32[]{:S(2)}, u32[]{:S(2)}) collective-permute-start(f32[64,8,128]{2,1,0:T(8,128)S(1)} %get-tuple-element.66), channel_id=1, source_target_pairs={{0,8},{1,9},{2,10},{3,11},{4,12},{5,13},{6,14},{7,15},{8,0},{9,1},... | collective-permute-start | bytes 786440 | tf_op jit(solution)/shard_map/ppermute | solution.py:667
  30.4 11.7 %collective-permute-start.8 = (f32[64,8,128]{2,1,0:T(8,128)S(1)}, f32[64,8,128]{2,1,0:T(8,128)S(1)}, u32[]{:S(2)}, u32[]{:S(2)}) collective-permute-start(f32[64,8,128]{2,1,0:T(8,128)S(1)} %get-tuple-element.67), channel_id=1, source_target_pairs={{0,96},{8,104},{16,48},{24,56},{32,0},{40,8},{48,80},{56,88},{64,3... | collective-permute-start | bytes 786440 | tf_op jit(solution)/shard_map/ppermute | solution.py:717

commit v4 on v3

--- a/solution.py
+++ b/solution.py
@@ -15,6 +15,7 @@
 
 BX, BY, BS, NY = 16, 8, 16, 256
 T = 4
+SPARE = 3
 f32 = jnp.float32
 LIMIT = 8 * 2**20
 FIRST_LIMIT = 54 * 2**20
@@ -41,11 +42,11 @@
     return pairs
 
 
-def ring(sizes):
+def ring(sizes, way):
     pairs = []
     for a in range(sizes[0]):
         for b in range(sizes[1]):
-            to = (a + (1 if b >= sizes[1] // 2 else -1)) % sizes[0]
+            to = (a + (way if b >= sizes[1] // 2 else -way)) % sizes[0]
             pairs.append((a * sizes[1] + b, to * sizes[1] + b))
     return pairs
 
@@ -142,12 +143,20 @@
     return square * inverse, inverse
 
 
+def centre_rows(flow, first):
+    return ((first + flow.rows - NKY // 2).astype(f32) + 0.5) * k_step
+
+
+def pick(tile, j):
+    return jnp.broadcast_to(tile[j : j + 1, :], (8, 128))
+
+
 def group_factor(k, inverse):
-    return (0.5 * X_SCALE * gravity**0.5) * inverse * (inverse * jnp.sqrt(k))
+    return (0.5 * X_SCALE * gravity**0.5) * inverse * lax.rsqrt(k)
 
 
 def refract_factor(k):
-    return (0.5 * K_SCALE * gravity**0.5) * k * jnp.sqrt(k)
+    return (0.5 * K_SCALE * gravity**0.5) * (k * k) * lax.rsqrt(k)
 
 
 def group(k, c, h):
@@ -163,7 +172,7 @@
 
 def first_messages(
     a_ref, depth_ref, mask_ref, inflow_ref,
-    np_ref, ky_od, ky_ev, kx_od, kx_ev, x_od, x_ev, depth, mask, inflow, ay, geo, sems,
+    np_ref, kx_od, kx_ev, x1, depth, mask, inflow, ay, geo, sems,
 ):
     s, i, j, x_up, y_up = place()
     flow = Flow()
@@ -189,48 +198,57 @@
     kx_first, ky_first = i * BX, j * BY
 
     def y_speeds(i, carry):
-        kx = centre(kx_first, i)
+        kx, ky = centre(kx_first, i), centre_rows(flow, ky_first)
+        k, inverse = wave(kx, ky)
+        c = group_factor(k, inverse) * jnp.abs(ky)
         for j in range(BY):
-            ky = centre(ky_first, j)
-            k, inverse = wave(kx, ky)
-            c = group_factor(k, inverse) * jnp.abs(ky)
-            store(ay, i * BY + j, each(lambda h: group(k, c, h), load(geo, 0)))
+            kj, cj = pick(k, j), pick(c, j)
+            store(ay, i * BY + j, each(lambda h: group(kj, cj, h), load(geo, 0)))
         return carry
 
     lax.fori_loop(0, BX, y_speeds, 0)
     wait_all(own, sems.at[3])
-    low = {"kx": jnp.where(is_even(i), 0, BX - 2), "ky": jnp.where(is_even(j), 0, BY - 2)}
-    high = {"kx": jnp.where(is_even(i), BX - 2, 0), "ky": jnp.where(is_even(j), BY - 2, 0)}
+    low, high = 2 * BY * T, BX * BY * T
+    low, high = jnp.where(is_even(i), low, high), jnp.where(is_even(i), high, low)
+    flat, size = np_ref.reshape((BX + 4) * BY * T, 8, 128), 2 * BY * T
     messages = [
-        pltpu.make_async_copy(src, dst, sems.at[n])
-        for n, (src, dst) in enumerate(
-            (
-                (own.at[:, pl.ds(low["ky"], 2)], ky_od),
-                (own.at[:, pl.ds(high["ky"], 2)], ky_ev),
-                (own.at[pl.ds(low["kx"], 2)], kx_od),
-                (own.at[pl.ds(high["kx"], 2)], kx_ev),
-            ),
-            4,
-        )
+        pltpu.make_async_copy(flat.at[pl.ds(at, size)], ref.at[pl.ds(0, size)], sems.at[n])
+        for n, (at, ref) in enumerate(((low, kx_od), (high, kx_ev)), 4)
     ]
+    for t in range(size, size + SPARE):
+        kx_ev[t] = jnp.zeros((8, 128), f32)
     for c in messages:
         c.start()
     for b in range(2):
         y = pl.ds(flow.y[b], 128)
         first = jnp.broadcast_to(depth[0:1, y].astype(f32), (8, 128))
         last = jnp.broadcast_to(depth[BS - 1 : BS, y].astype(f32), (8, 128))
-        x_od[4 * BX + b] = jnp.where(is_even(s), first, last)
-        x_ev[4 * BX + b] = jnp.where(is_even(s), last, first)
+        x1[4 * BX + b] = jnp.where(x_up, last, first)
 
     def one_kx(i, carry):
         for b in range(2):
             rows = flow.edge_rows([np_ref[i + 2, j, 2 + b] for j in range(BY)])
             for l in range(2):
-                x_od[l * 2 * BX + i * 2 + b] = rows[l]
-                x_ev[l * 2 * BX + i * 2 + b] = rows[l]
+                x1[l * 2 * BX + i * 2 + b] = rows[l]
         return carry
 
     lax.fori_loop(0, BX, one_kx, 0)
+    for c in messages:
+        c.wait()
+
+
+def ky_messages(np_ref, next_depth, ky_od, ky_ev, next_row, sems):
+    _, _, j, x_up, _ = place()
+    own = np_ref.at[pl.ds(2, BX)]
+    low, high = jnp.where(is_even(j), 0, BY - 2), jnp.where(is_even(j), BY - 2, 0)
+    messages = [
+        pltpu.make_async_copy(own.at[:, pl.ds(at, 2)], ref, sems.at[n])
+        for n, (at, ref) in enumerate(((low, ky_od), (high, ky_ev)))
+    ]
+    for c in messages:
+        c.start()
+    coming = jnp.where(x_up, next_depth[0:1, :], next_depth[BS - 1 : BS, :]).astype(f32) * 0.01
+    next_row[...] = jnp.broadcast_to(coming, (8, NY))
     for c in messages:
         c.wait()
 
@@ -263,29 +281,35 @@
             for r in range(8):
                 spec[(8 * half + r) * BY + j] = jnp.broadcast_to(column[r : r + 1, :], (8, 128))
 
-    def kx_faces(i, j):
-        k, _ = wave(lower_face(kx_first, i), centre(ky_first, j))
+    ky = centre_rows(flow, ky_first)
+    ky_face = (ky_first + flow.rows - NKY // 2).astype(f32) * k_step
+
+    def kx_faces(i):
+        k, _ = wave(lower_face(kx_first, i), ky)
         c = refract_factor(k)
-        store(rkx, i * BY + j, each(lambda h: refract(k, c, h), load(geo, 0)))
+        for j in range(BY):
+            kj, cj = pick(k, j), pick(c, j)
+            store(rkx, i * BY + j, each(lambda h: refract(kj, cj, h), load(geo, 0)))
 
     def one_kx(i, carry):
         kx = centre(kx_first, i)
+        k, inverse = wave(kx, ky)
+        c = group_factor(k, inverse) * jnp.abs(kx)
         for j in range(BY):
-            ky = centre(ky_first, j)
-            k, inverse = wave(kx, ky)
-            c = group_factor(k, inverse)
-            cx = c * jnp.abs(kx)
-            store(ax, i * BY + j, each(lambda h: group(k, cx, h), load(geo, 1)))
-            kx_faces(i, j)
+            kj, cj = pick(k, j), pick(c, j)
+            store(ax, i * BY + j, each(lambda h: group(kj, cj, h), load(geo, 1)))
+        kx_faces(i)
+        k, _ = wave(kx, ky_face)
+        c = refract_factor(k)
+        end, _ = wave(kx, lower_face(ky_first, BY))
+        end_c = refract_factor(end)
         for j in range(BY + 1):
-            k, _ = wave(kx, lower_face(ky_first, j))
-            c = refract_factor(k)
-            store(aky, i * (BY + 1) + j, each(lambda h, g: refract(k, c, h) * g, load(geo, 0), load(gy, 0)))
+            kj, cj = (pick(k, j), pick(c, j)) if j < BY else (end, end_c)
+            store(aky, i * (BY + 1) + j, each(lambda h, g: refract(kj, cj, h) * g, load(geo, 0), load(gy, 0)))
         return carry
 
     lax.fori_loop(0, BX, one_kx, 0)
-    for j in range(BY):
-        kx_faces(BX, j)
+    kx_faces(BX)
 
 
 def space_change(flow, n, ax_ref, ay_ref, i, j, edge, halo_row, halo_flux):
@@ -347,41 +371,41 @@
         return self.take(self.ev, self.od, slab, self.high_at, self.high_empty)
 
 
-def pad_kx(n_ref, od, ev):
-    halo = Halo(od, ev, "kx", 2)
-
-    def one(r, carry):
-        store(n_ref, r, halo.low(r))
-        store(n_ref, (BX + 2) * BY + r, halo.high(r))
-        return carry
-
-    lax.fori_loop(0, 2 * BY, one, 0)
-
-
 def no_inflow(x_up):
     s = lax.axis_index("space")
     return s == jnp.where(x_up, 0, lax.axis_size("space") - 1)
 
 
 def stage_one_edges(
-    np_in, ax, ay, rkx, aky, heights, hold_ref, spec, kx_od, kx_ev, x_od, x_ev,
+    np_in, ax, ay, rkx, aky, heights, hold_ref, spec, kx_od, x1, kx_ev, next_row,
     np_ref, p_ref, gx, edge, halo_speed, xnear, xflux, ky2_od, ky2_ev, fk, hrow,
 ):
     s, kx_place, ky_place, x_up, y_up = place()
     flow = Flow()
     kx_first, ky_first = kx_place * BX, ky_place * BY
-    pad_kx(np_ref, kx_od, kx_ev)
+    odd_low = is_even(kx_place)
+    empty = jnp.where(odd_low, kx_place == 0, kx_place == lax.axis_size("kx") - 1)
+    base = jnp.where(odd_low, 0, (BX + 2) * BY)
+
+    def odd_side(r, carry):
+        tiles = [[kx_od[r * T + 2 * (1 - a) + b] for b in range(2)] for a in range(2)]
+        store(np_ref, base + r, each(lambda v: jnp.where(empty, 0.0, v), tiles))
+        return carry
+
+    lax.fori_loop(0, 2 * BY, odd_side, 0)
+    size = 2 * BY * T
+    np_ref[pl.ds(jnp.where(odd_low, (BX + 2) * BY * T, 0), size)] = kx_ev[pl.ds(0, size)]
     h = heights[...]
     x_flip, y_flip = jnp.where(x_up, 0, 1), jnp.where(y_up, 0, 1)
     none = no_inflow(x_up)
-    use_od = is_even(s) == x_up
     for b in range(2):
         y = b ^ y_flip
         at = 4 * BX + y
         mine = h[:, 128 * b : 128 * b + 128]
-        od, ev = x_od[at][0:1, :] * 0.01, x_ev[at][0:1, :] * 0.01
-        low = jnp.where(s == 0, mine[0:1, :], jnp.where(is_even(s), od, ev))
-        high = jnp.where(s == lax.axis_size("space") - 1, mine[BS - 1 : BS, :], jnp.where(is_even(s), ev, od))
+        last = x1[at][0:1, :] * 0.01
+        coming = next_row[0:1, 128 * b : 128 * b + 128]
+        low = jnp.where(s == 0, mine[0:1, :], jnp.where(x_up, last, coming))
+        high = jnp.where(s == lax.axis_size("space") - 1, mine[BS - 1 : BS, :], jnp.where(x_up, coming, last))
         place_of = lax.broadcasted_iota(jnp.int32, (BS, 128), 0)
         before = jnp.where(place_of == 0, low, pltpu.roll(mine, 1, 0))
         after = jnp.where(place_of == BS - 1, high, pltpu.roll(mine, BS - 1, 0))
@@ -400,8 +424,7 @@
         c = group_factor(k, inverse) * jnp.abs(kx)
         for b in range(2):
             at = i * 2 + b
-            near = jnp.where(use_od, x_od[at], x_ev[at])
-            far = jnp.where(use_od, x_od[2 * BX + at], x_ev[2 * BX + at])
+            near, far = x1[at], x1[2 * BX + at]
             edge[at] = group(k, c, hrow[b])
             speed = group(k, c, hrow[2 + b])
             halo_speed[at] = speed
@@ -433,21 +456,16 @@
             a, b = (load(np_ref, (i + 2) * BY + j) for j in (a, b))
             return each(lambda w, a, b: w * (3.0 * a - b), w, a, b)
 
-        def send(j, low, high, l, to):
-            v = each(
-                lambda m, p, u, v: jnp.where(m, spec[i * BY + j], p - (u - v)), hold, part[j], high, low
-            )
-            for ref, here in ((ky2_od, to), (ky2_ev, jnp.logical_not(to))):
-                @pl.when(here)
-                def _():
-                    store(ref, i * 2 + l, v)
+        def edge_layer(j, low, high):
+            return each(lambda m, p, u, v: jnp.where(m, spec[i * BY + j], p - (u - v)), hold, part[j], high, low)
 
         f = [own(0, 0, 1), own(1, 1, 2), own(2, 2, 3)]
-        send(0, f[0], f[1], 0, is_even(ky_place))
-        send(1, f[1], f[2], 1, is_even(ky_place))
+        down = [edge_layer(0, f[0], f[1]), edge_layer(1, f[1], f[2])]
         f = [own(BY - 2, BY - 3, BY - 4), own(BY - 1, BY - 2, BY - 3), own(BY, BY - 1, BY - 2)]
-        send(BY - 2, f[0], f[1], 0, jnp.logical_not(is_even(ky_place)))
-        send(BY - 1, f[1], f[2], 1, jnp.logical_not(is_even(ky_place)))
+        up = [edge_layer(BY - 2, f[0], f[1]), edge_layer(BY - 1, f[1], f[2])]
+        for l in range(2):
+            store(ky2_od, i * 2 + l, each(lambda a, b: jnp.where(is_even(ky_place), a, b), down[l], up[l]))
+            store(ky2_ev, i * 2 + l, each(lambda a, b: jnp.where(is_even(ky_place), b, a), down[l], up[l]))
         return carry
 
     lax.fori_loop(0, BX, one_kx, 0)
@@ -461,7 +479,7 @@
 
 def stage_one_rest(
     np_ref, p_ref, ax, ay, rkx, aky, gx, gy, edge, xnear, xflux, hold_ref, spec, ky_od, ky_ev,
-    sp_ref, kx2_od, kx2_ev, x2, fk, sems,
+    sp_ref, x2, fk,
 ):
     s, kx_place, ky_place, x_up, y_up = place()
     flow = Flow()
@@ -502,15 +520,21 @@
         return carry
 
     lax.fori_loop(0, BX, one_kx, 0)
+
+
+def kx_messages(sp_in, sp_ref, kx2_od, kx2_ev, sems):
+    _, kx_place, _, _, _ = place()
     size = 2 * BY * T
-    low, high = 0, (BX - 2) * BY * T
-    copies = [
-        pltpu.make_async_copy(sp_ref.at[pl.ds(size + jnp.where(is_even(kx_place), *at), size)], ref, sems.at[n])
+    low, high = size, size + (BX - 2) * BY * T
+    messages = [
+        pltpu.make_async_copy(sp_ref.at[pl.ds(jnp.where(is_even(kx_place), *at), size)], ref, sems.at[n])
         for n, (ref, at) in enumerate(((kx2_od, (low, high)), (kx2_ev, (high, low))))
     ]
-    for c in copies:
+    for c in messages:
         c.start()
-    for c in copies:
+    sp_ref[pl.ds(0, size)] = jnp.zeros((size, 8, 128), f32)
+    sp_ref[pl.ds((BX + 2) * BY * T, size)] = jnp.zeros((size, 8, 128), f32)
+    for c in messages:
         c.wait()
 
 
@@ -528,16 +552,10 @@
                 pltpu.make_async_copy(buffer.at[rows, :, 2 * a + b], out.at[rows, :, x, y], sem).start()
 
 
-def stage_two_inner(np_ref, sp_in, ax, ay, rkx, aky, gx, gy, edge, sp_ref, q_ref, fk):
+def stage_two_inner(np_ref, sp_ref, ax, ay, rkx, aky, gx, gy, edge, q_ref, fk):
     flow = Flow()
     nothing = each(lambda v: jnp.zeros_like(v), load(gx, 0))
 
-    def clear(r, carry):
-        store(sp_ref, r, nothing)
-        store(sp_ref, (BX + 2) * BY + r, nothing)
-        return carry
-
-    lax.fori_loop(0, 2 * BY, clear, 0)
     g = load(gx, 0)
     for j in range(BY):
         store(fk, j, kx_flux(g, rkx, sp_ref, 0, j))
@@ -660,28 +678,39 @@
     def v(*shape):
         return pltpu.VMEM(shape + (8, 128), f32)
 
-    def swap(od, ev, axis, spare):
-        at, beside = AXES.index(axis), AXES.index(spare)
-        return (
-            lax.ppermute(od, AXES, swaps(sizes, at, 1, beside)),
-            lax.ppermute(ev, AXES, swaps(sizes, at, 0, beside)),
-        )
+    def swap_odd(message, axis, spare):
+        return lax.ppermute(message, AXES, swaps(sizes, AXES.index(axis), 1, AXES.index(spare)))
+
+    def swap_even(message, axis):
+        return lax.ppermute(message, AXES, swaps(sizes, AXES.index(axis), 0, 0))
 
     sem = pltpu.SemaphoreType.DMA
-    np5, ky_od, ky_ev, kx_od, kx_ev, x_od, x_ev, depth, mask, spectrum, ay = call(
+    np5, kx_od, kx_ev, x1, depth, mask, spectrum, ay = call(
         first_messages,
-        (v(BX + 4, BY, T), v(BX, 2, T), v(BX, 2, T), v(2, BY, T), v(2, BY, T), v(4 * BX + 2), v(4 * BX + 2),
-         pltpu.VMEM((BS, NY), jnp.int32), pltpu.VMEM((BS, NY), jnp.int32), pltpu.VMEM((NKX, NKY), f32), v(slabs)),
+        (v(BX + 4, BY, T), v(kx_tiles), v(kx_tiles + SPARE), v(4 * BX + 2), pltpu.VMEM((BS, NY), jnp.int32),
+         pltpu.VMEM((BS, NY), jnp.int32), pltpu.VMEM((NKX, NKY), f32), v(slabs)),
         (action, depth_cm, inflow_mask, inflow),
         "hhhh",
-        "v" * 11,
-        [v(T), sem((8,))],
+        "v" * 8,
+        [v(T), sem((6,))],
         us=0,
         limit=FIRST_LIMIT,
     )
-    ky_od, ky_ev = (m.reshape(ky_tiles, 8, 128) for m in swap(ky_od, ky_ev, "ky", "kx"))
-    kx_od, kx_ev = (m.reshape(kx_tiles, 8, 128) for m in swap(kx_od, kx_ev, "kx", "space"))
-    x_od, x_ev = swap(x_od, x_ev, "space", "kx")
+    next_depth = lax.ppermute(depth, AXES[:2], ring(sizes, -1))
+    x1 = lax.ppermute(x1, AXES[:2], ring(sizes, 1))
+    kx_od, kx_ev = swap_odd(kx_od, "kx", "space"), swap_even(kx_ev, "kx")
+    ky_od, ky_ev, next_row = call(
+        ky_messages,
+        (v(BX, 2, T), v(BX, 2, T), pltpu.VMEM((8, NY), f32)),
+        (np5, next_depth),
+        "v" * 2,
+        "v" * 3,
+        [sem((2,))],
+        us=0,
+    )
+    ky_od = swap_odd(ky_od, "ky", "kx").reshape(ky_tiles, 8, 128)
+    ky_ev = swap_even(ky_ev, "ky").reshape(ky_tiles, 8, 128)
+    np3 = np5.reshape(padded, 8, 128)
     ax, rkx, aky, gy, heights, hold, spec = call(
         speeds,
         (v(slabs), v((BX + 1) * BY * T), v(BX * (BY + 1) * T), v(T), pltpu.VMEM((BS, NY), f32),
@@ -692,37 +721,45 @@
         [v(2 * T)],
         us=4,
     )
-    np3 = np5.reshape(padded, 8, 128)
     np3, part, gx, edge, halo_speed, xnear, xflux, ky2_od, ky2_ev = call(
         stage_one_edges,
         (v(padded), v(edge_slabs), v(T), v(2 * BX), v(2 * BX), v(2 * BX), v(2 * BX), v(ky_tiles), v(ky_tiles)),
-        (np3, ax, ay, rkx, aky, heights, hold, spec, kx_od, kx_ev, x_od, x_ev),
+        (np3, ax, ay, rkx, aky, heights, hold, spec, kx_od, x1, kx_ev, next_row),
         "v" * 12,
         "v" * 9,
         [v(len(EDGES) * T), v(4)],
         alias={0: 0},
         us=0,
     )
-    ky2_od, ky2_ev = swap(ky2_od, ky2_ev, "ky", "kx")
-    sp, kx2_od, kx2_ev, x2 = call(
+    ky2_od, ky2_ev = swap_odd(ky2_od, "ky", "kx"), swap_even(ky2_ev, "ky")
+    sp, x2 = call(
         stage_one_rest,
-        (v(padded), v(kx_tiles), v(kx_tiles), v(4 * BX)),
+        (v(padded), v(4 * BX)),
         (np3, part, ax, ay, rkx, aky, gx, gy, edge, xnear, xflux, hold, spec, ky_od, ky_ev),
         "v" * 15,
-        "v" * 4,
-        [v(len(MIDDLE) * T), sem((2,))],
+        "v" * 2,
+        [v(len(MIDDLE) * T)],
         us=0,
     )
-    kx2_od, kx2_ev = swap(kx2_od, kx2_ev, "kx", "space")
-    x2 = lax.ppermute(x2, AXES[:2], ring(sizes))
-    sp, q = call(
+    x2 = lax.ppermute(x2, AXES[:2], ring(sizes, 1))
+    sp, kx2_od, kx2_ev = call(
+        kx_messages,
+        (v(padded), v(kx_tiles), v(kx_tiles)),
+        (sp,),
+        "v",
+        "v" * 3,
+        [sem((2,))],
+        alias={0: 0},
+        us=0,
+    )
+    kx2_od, kx2_ev = swap_odd(kx2_od, "kx", "space"), swap_even(kx2_ev, "kx")
+    (q,) = call(
         stage_two_inner,
-        (v(padded), v(slabs)),
+        (v(slabs),),
         (np3, sp, ax, ay, rkx, aky, gx, gy, edge),
         "v" * 9,
-        "vv",
+        "v",
         [v(BY * T)],
-        alias={1: 0},
         us=4,
     )
     _, out = call(

time: 44.2 us -> 43.3 us (0.980)
  starting transfers between devices: 15.4 us -> 18.2 us
  waiting for transfers between devices: 10.2 us -> 7.73 us
  Pallas kernels: 18.4 us -> 17.2 us
    ppermute x11, starting transfers between devices: 15.4 us -> 18.2 us  [the longest x4 9.44 us: swap_odd(): lax.ppermute(message, AXES, swaps(sizes, AXES.index(axis), 1, AXES.index(...]
    ppermute x11, waiting for transfers between devices: 10.2 us -> 7.73 us  [the longest x4 4.6 us: swap_odd(): lax.ppermute(message, AXES, swaps(sizes, AXES.index(axis), 1, AXES.index(...]
    pallas_call x6 -> x8, Pallas kernels: 18.4 us -> 17.2 us  [call(): pl.pallas_call(kernel, out_shape=tuple(outs), in_specs=[whole[c] for c in...]
  transfers between devices with their start and end apart: 11 -> 11, of which waited for: 4 -> 6; matrix products, arithmetic and copies ran while one was open for 0% -> 0% of each run, Pallas kernels for 31% -> 30%
where the time goes in v4:
time: 43.3 us; the launch traced here: 43.1 us
  starting transfers between devices  18.2 us (42%)
  Pallas kernels  17.2 us (40%)
  waiting for transfers between devices  7.73 us (18%)
    pallas_call x8, Pallas kernels, call(): pl.pallas_call(kernel, out_shape=tuple(outs), in_specs=[whole[c] for c in...  17.2 us
    ppermute x4, starting transfers between devices, swap_odd(): lax.ppermute(message, AXES, swaps(sizes, AXES.index(axis), 1, AXES.index(...  9.44 us
    ppermute x4, waiting for transfers between devices, swap_odd(): lax.ppermute(message, AXES, swaps(sizes, AXES.index(axis), 1, AXES.index(...  4.6 us
    ppermute x4, starting transfers between devices, swap_even(): return lax.ppermute(message, AXES, swaps(sizes, AXES.index(axis), 0, 0))  3.99 us
    ppermute x4, waiting for transfers between devices, swap_even(): return lax.ppermute(message, AXES, swaps(sizes, AXES.index(axis), 0, 0))  2.25 us
    ppermute x1, starting transfers between devices, per_device(): x1 = lax.ppermute(x1, AXES[:2], ring(sizes, 1))  1.8 us
    ppermute x1, starting transfers between devices, per_device(): next_depth = lax.ppermute(depth, AXES[:2], ring(sizes, -1))  1.56 us
    ppermute x1, starting transfers between devices, per_device(): x2 = lax.ppermute(x2, AXES[:2], ring(sizes, 1))  1.37 us
  transfers between devices with their start and end apart: 11, of which 6 were waited for; matrix products, arithmetic and copies ran while one was open for 0% of the time, Pallas kernels for 30%

profile of v4, /device:TPU:8, one launch (start us, length us, event | category | flops | bytes accessed | tf_op | source)
XLA Modules:
  0.0 43.1 jit_solution(2419830087321890488)
XLA Ops:
  0.0 2.4 %first_messages.1 = (f32[20,8,4,8,128]{4,3,2,1,0:T(8,128)S(1)}, f32[64,8,128]{2,1,0:T(8,128)S(1)}, f32[67,8,128]{2,1,0:T(8,128)S(1)}, f32[66,8,128]{2,1,0:T(8,12...) custom-call(f32[16,8,16,256]{3,2,1,0:T(8,128)} %a_ref.1, ...), custom_call_target="tpu_custom_call" | custom-call | tf_op jit(solution)/shard_map/first_messages/pallas_call | solution.py:660
  2.4 1.6 %collective-permute-start.3 = (s32[16,256]{1,0:T(8,128)S(1)}, s32[16,256]{1,0:T(8,128)S(1)}, u32[]{:S(2)}, u32[]{:S(2)}) collective-permute-start(s32[16,256]{1,0:T(8,128)S(1)} %get-tuple-element.39.depth), channel_id=1, source_target_pairs={{0,32},{8,40},{16,112},{24,120},{32,64},{40,72},{48,16},{56,24},{6... | collective-permute-start | bytes 49160 | tf_op jit(solution)/shard_map/ppermute | solution.py:699
  4.0 1.5 %collective-permute-start = (f32[64,8,128]{2,1,0:T(8,128)S(1)}, f32[64,8,128]{2,1,0:T(8,128)S(1)}, u32[]{:S(2)}, u32[]{:S(2)}) collective-permute-start(f32[64,8,128]{2,1,0:T(8,128)S(1)} %get-tuple-element.49), channel_id=1, source_target_pairs={{0,32},{1,33},{2,34},{3,35},{4,36},{5,37},{6,38},{7,39},{8,16},{9,... | collective-permute-start | bytes 786440 | tf_op jit(solution)/shard_map/ppermute | solution.py:682
  5.5 1.8 %collective-permute-start.1 = (f32[66,8,128]{2,1,0:T(8,128)S(1)}, f32[66,8,128]{2,1,0:T(8,128)S(1)}, u32[]{:S(2)}, u32[]{:S(2)}) collective-permute-start(f32[66,8,128]{2,1,0:T(8,128)S(1)} %get-tuple-element.50), channel_id=1, source_target_pairs={{0,96},{8,104},{16,48},{24,56},{32,0},{40,8},{48,80},{56,88},{64,3... | collective-permute-start | bytes 811016 | tf_op jit(solution)/shard_map/ppermute | solution.py:700
  7.3 0.2 collective-permute-done.3.next_depth
  7.5 0.1 ky_messages.1
  7.6 4.0 %collective-permute-start.4 = (f32[16,2,4,8,128]{4,3,2,1,0:T(8,128)S(1)}, f32[16,2,4,8,128]{4,3,2,1,0:T(8,128)S(1)}, u32[]{:S(2)}, u32[]{:S(2)}) collective-permute-start(f32[16,2,4,8,128]{4,3,2,1,0:T(8,128)S(1)} %get-tuple-element.60), channel_id=1, source_target_pairs={{0,8},{1,2},{2,1},{3,4},{4,3},{5,6},{6,5},{7,15},{8,0},{9,10},{10,... | collective-permute-start | bytes 1572872 | tf_op jit(solution)/shard_map/ppermute | solution.py:682
  11.6 0.0 collective-permute-start.5
  11.6 1.4 %collective-permute-start.2 = (f32[67,8,128]{2,1,0:T(8,128)S(1)}, f32[67,8,128]{2,1,0:T(8,128)S(1)}, u32[]{:S(2)}, u32[]{:S(2)}) collective-permute-start(f32[67,8,128]{2,1,0:T(8,128)S(1)} %get-tuple-element.51), channel_id=1, source_target_pairs={{0,8},{1,9},{2,10},{3,11},{4,12},{5,13},{6,14},{7,15},{8,0},{9,1},... | collective-permute-start | bytes 823304 | tf_op jit(solution)/shard_map/ppermute | solution.py:685
  13.0 2.5 %speeds.1 = (f32[512,8,128]{2,1,0:T(8,128)S(1)}, f32[544,8,128]{2,1,0:T(8,128)S(1)}, f32[576,8,128]{2,1,0:T(8,128)S(1)}, f32[4,8,128]{2,1,0:T(8,128)S(1)}, f32[1...) custom-call(s32[16,256]{1,0:T(8,128)S(1)} %get-tuple-element.39.depth, ...), custom_call_target="tpu_custom_call" | custom-call | flops 4000000000 | tf_op jit(solution)/shard_map/speeds/pallas_call | solution.py:660
  15.4 0.0 collective-permute-done.kx_od
  15.5 0.7 %collective-permute-done.1.x1 = f32[66,8,128]{2,1,0:T(8,128)S(1)} collective-permute-done((f32[66,8,128]{2,1,0:T(8,128)S(1)}, f32[66,8,128]{2,1,0:T(8,128)S(1)}, u32[]{:S(2)}, u32[]{:S(2)}) %collective-permute-start.1) | collective-permute-done | bytes 270368 | tf_op jit(solution)/shard_map/ppermute | solution.py:700
  16.2 0.0 collective-permute-done.2.kx_ev
  16.2 3.4 %stage_one_edges.1 = (f32[640,8,128]{2,1,0:T(8,128)S(1)}, f32[256,8,128]{2,1,0:T(8,128)S(1)}, f32[4,8,128]{2,1,0:T(8,128)S(1)}, f32[32,8,128]{2,1,0:T(8,128)S(1)...) custom-call(f32[640,8,128]{2,1,0:T(8,128)S(1)} %bitcast.3, ...), custom_call_target="tpu_custom_call", output_to_operand_aliasing={{0}: (0, {})} | custom-call | tf_op jit(solution)/shard_map/stage_one_edges/pallas_call | solution.py:660
  19.6 3.1 %collective-permute-start.9 = (f32[128,8,128]{2,1,0:T(8,128)S(1)}, f32[128,8,128]{2,1,0:T(8,128)S(1)}, u32[]{:S(2)}, u32[]{:S(2)}) collective-permute-start(f32[128,8,128]{2,1,0:T(8,128)S(1)} %get-tuple-element.68), channel_id=1, source_target_pairs={{0,8},{1,2},{2,1},{3,4},{4,3},{5,6},{6,5},{7,15},{8,0},{9,10},{10,... | collective-permute-start | bytes 1572872 | tf_op jit(solution)/shard_map/ppermute | solution.py:682
  22.7 0.8 %collective-permute-start.10 = (f32[128,8,128]{2,1,0:T(8,128)S(1)}, f32[128,8,128]{2,1,0:T(8,128)S(1)}, u32[]{:S(2)}, u32[]{:S(2)}) collective-permute-start(f32[128,8,128]{2,1,0:T(8,128)S(1)} %get-tuple-element.69), channel_id=1, source_target_pairs={{0,1},{1,0},{2,3},{3,2},{4,5},{5,4},{6,7},{7,6},{8,9},{9,8},{10,11... | collective-permute-start | bytes 1572872 | tf_op jit(solution)/shard_map/ppermute | solution.py:685
  23.5 1.0 %collective-permute-done.4 = f32[16,2,4,8,128]{4,3,2,1,0:T(8,128)S(1)} collective-permute-done((f32[16,2,4,8,128]{4,3,2,1,0:T(8,128)S(1)}, f32[16,2,4,8,128]{4,3,2,1,0:T(8,128)S(1)}, u32[]{:S(2)}, u32[]{:S(2)}) %collective-permute-start.4) | collective-permute-done | bytes 524320 | tf_op jit(solution)/shard_map/ppermute | solution.py:682
  24.5 1.5 %collective-permute-done.5 = f32[16,2,4,8,128]{4,3,2,1,0:T(8,128)S(1)} collective-permute-done((f32[16,2,4,8,128]{4,3,2,1,0:T(8,128)S(1)}, f32[16,2,4,8,128]{4,3,2,1,0:T(8,128)S(1)}, u32[]{:S(2)}, u32[]{:S(2)}) %collective-permute-start.5) | collective-permute-done | bytes 524320 | tf_op jit(solution)/shard_map/ppermute | solution.py:685
  26.0 3.1 %stage_one_rest.1 = (f32[640,8,128]{2,1,0:T(8,128)S(1)}, f32[64,8,128]{2,1,0:T(8,128)S(1)}) custom-call(f32[640,8,128]{2,1,0:T(8,128)S(1)} %get-tuple-element.53.np_ref, f32[256,8,128]{2,1,0:T(8,128)S(1)} %get-tuple-element.54.p_ref, f32[512,8,128]{2,1,0:T(8,128)S(1)} %get-tuple-element.42.ax, f32[512,8,128]{2,1,0:T(8,128)S(1)} %get-tuple-element.43.ay, ...), custom_call_target="tpu_custom_call" | custom-call | tf_op jit(solution)/shard_map/stage_one_rest/pallas_call | solution.py:660
  29.1 1.4 %collective-permute-start.8 = (f32[64,8,128]{2,1,0:T(8,128)S(1)}, f32[64,8,128]{2,1,0:T(8,128)S(1)}, u32[]{:S(2)}, u32[]{:S(2)}) collective-permute-start(f32[64,8,128]{2,1,0:T(8,128)S(1)} %get-tuple-element.67), channel_id=1, source_target_pairs={{0,96},{8,104},{16,48},{24,56},{32,0},{40,8},{48,80},{56,88},{64,3... | collective-permute-start | bytes 786440 | tf_op jit(solution)/shard_map/ppermute | solution.py:744
  30.5 0.1 kx_messages.1
  30.6 0.8 %collective-permute-start.6 = (f32[64,8,128]{2,1,0:T(8,128)S(1)}, f32[64,8,128]{2,1,0:T(8,128)S(1)}, u32[]{:S(2)}, u32[]{:S(2)}) collective-permute-start(f32[64,8,128]{2,1,0:T(8,128)S(1)} %get-tuple-element.65), channel_id=1, source_target_pairs={{0,32},{1,33},{2,34},{3,35},{4,36},{5,37},{6,38},{7,39},{8,16},{9,... | collective-permute-start | bytes 786440 | tf_op jit(solution)/shard_map/ppermute | solution.py:682
  31.4 1.8 %collective-permute-start.7 = (f32[64,8,128]{2,1,0:T(8,128)S(1)}, f32[64,8,128]{2,1,0:T(8,128)S(1)}, u32[]{:S(2)}, u32[]{:S(2)}) collective-permute-start(f32[64,8,128]{2,1,0:T(8,128)S(1)} %get-tuple-element.66), channel_id=1, source_target_pairs={{0,8},{1,9},{2,10},{3,11},{4,12},{5,13},{6,14},{7,15},{8,0},{9,1},... | collective-permute-start | bytes 786440 | tf_op jit(solution)/shard_map/ppermute | solution.py:685
  33.2 3.6 %stage_two_inner.1.q_in = f32[512,8,128]{2,1,0:T(8,128)S(1)} custom-call(f32[640,8,128]{2,1,0:T(8,128)S(1)} %get-tuple-element.53.np_ref, f32[640,8,128]{2,1,0:T(8,128)S(1)} %get-tuple-element.63.sp_ref, f32[512,8,128]{2,1,0:T(8,128)S(1)} %get-tuple-element.42.ax, f32[512,8,128]{2,1,0:T(8,128)S(1)} %get-tuple-element.43.ay, ...), custom_call_target="tpu_custom_call" | custom-call | flops 4000000000 | tf_op jit(solution)/shard_map/stage_two_inner/pallas_call | solution.py:660
  36.8 0.0 collective-permute-done.9.ky_od
  36.9 0.7 %collective-permute-done.10.ky_ev = f32[128,8,128]{2,1,0:T(8,128)S(1)} collective-permute-done((f32[128,8,128]{2,1,0:T(8,128)S(1)}, f32[128,8,128]{2,1,0:T(8,128)S(1)}, u32[]{:S(2)}, u32[]{:S(2)}) %collective-permute-start.10) | collective-permute-done | bytes 524320 | tf_op jit(solution)/shard_map/ppermute | solution.py:685
  37.6 0.0 collective-permute-done.8.x2
  37.6 3.6 %collective-permute-done.6.kx_od = f32[64,8,128]{2,1,0:T(8,128)S(1)} collective-permute-done((f32[64,8,128]{2,1,0:T(8,128)S(1)}, f32[64,8,128]{2,1,0:T(8,128)S(1)}, u32[]{:S(2)}, u32[]{:S(2)}) %collective-permute-start.6) | collective-permute-done | bytes 262176 | tf_op jit(solution)/shard_map/ppermute | solution.py:682
  41.2 0.0 collective-permute-done.7.kx_ev
  41.2 1.9 %stage_two_outer.1 = (f32[512,8,128]{2,1,0:T(8,128)S(1)}, f32[16,8,16,256]{3,2,1,0:T(8,128)}) custom-call(f32[512,8,128]{2,1,0:T(8,128)S(1)} %stage_two_inner.1.q_in, f32[512,8,128]{2,1,0:T(8,128)S(1)} %get-tuple-element.42.ax, f32[544,8,128]{2,1,0:T(8,128)S(1)} %get-tuple-element.44.rkx, ...), custom_call_target="tpu_custom_call", output_to_operand_aliasing={{0}: (0, {})} | custom-call | tf_op jit(solution)/shard_map/stage_two_outer/pallas_call | solution.py:660
Async XLA Ops:
  2.4 5.0 %collective-permute-start.3 = (s32[16,256]{1,0:T(8,128)S(1)}, s32[16,256]{1,0:T(8,128)S(1)}, u32[]{:S(2)}, u32[]{:S(2)}) collective-permute-start(s32[16,256]{1,0:T(8,128)S(1)} %get-tuple-element.39.depth), channel_id=1, source_target_pairs={{0,32},{8,40},{16,112},{24,120},{32,64},{40,72},{48,16},{56,24},{6... | collective-permute-start | bytes 49160 | tf_op jit(solution)/shard_map/ppermute | solution.py:699
  4.0 11.4 %collective-permute-start = (f32[64,8,128]{2,1,0:T(8,128)S(1)}, f32[64,8,128]{2,1,0:T(8,128)S(1)}, u32[]{:S(2)}, u32[]{:S(2)}) collective-permute-start(f32[64,8,128]{2,1,0:T(8,128)S(1)} %get-tuple-element.49), channel_id=1, source_target_pairs={{0,32},{1,33},{2,34},{3,35},{4,36},{5,37},{6,38},{7,39},{8,16},{9,... | collective-permute-start | bytes 786440 | tf_op jit(solution)/shard_map/ppermute | solution.py:682
  5.5 10.7 %collective-permute-start.1 = (f32[66,8,128]{2,1,0:T(8,128)S(1)}, f32[66,8,128]{2,1,0:T(8,128)S(1)}, u32[]{:S(2)}, u32[]{:S(2)}) collective-permute-start(f32[66,8,128]{2,1,0:T(8,128)S(1)} %get-tuple-element.50), channel_id=1, source_target_pairs={{0,96},{8,104},{16,48},{24,56},{32,0},{40,8},{48,80},{56,88},{64,3... | collective-permute-start | bytes 811016 | tf_op jit(solution)/shard_map/ppermute | solution.py:700
  7.6 17.0 %collective-permute-start.4 = (f32[16,2,4,8,128]{4,3,2,1,0:T(8,128)S(1)}, f32[16,2,4,8,128]{4,3,2,1,0:T(8,128)S(1)}, u32[]{:S(2)}, u32[]{:S(2)}) collective-permute-start(f32[16,2,4,8,128]{4,3,2,1,0:T(8,128)S(1)} %get-tuple-element.60), channel_id=1, source_target_pairs={{0,8},{1,2},{2,1},{3,4},{4,3},{5,6},{6,5},{7,15},{8,0},{9,10},{10,... | collective-permute-start | bytes 1572872 | tf_op jit(solution)/shard_map/ppermute | solution.py:682
  11.6 14.5 %collective-permute-start.5 = (f32[16,2,4,8,128]{4,3,2,1,0:T(8,128)S(1)}, f32[16,2,4,8,128]{4,3,2,1,0:T(8,128)S(1)}, u32[]{:S(2)}, u32[]{:S(2)}) collective-permute-start(f32[16,2,4,8,128]{4,3,2,1,0:T(8,128)S(1)} %get-tuple-element.61), channel_id=1, source_target_pairs={{0,1},{1,0},{2,3},{3,2},{4,5},{5,4},{6,7},{7,6},{8,9},{9,8},{10,11... | collective-permute-start | bytes 1572872 | tf_op jit(solution)/shard_map/ppermute | solution.py:685
  11.6 4.6 %collective-permute-start.2 = (f32[67,8,128]{2,1,0:T(8,128)S(1)}, f32[67,8,128]{2,1,0:T(8,128)S(1)}, u32[]{:S(2)}, u32[]{:S(2)}) collective-permute-start(f32[67,8,128]{2,1,0:T(8,128)S(1)} %get-tuple-element.51), channel_id=1, source_target_pairs={{0,8},{1,9},{2,10},{3,11},{4,12},{5,13},{6,14},{7,15},{8,0},{9,1},... | collective-permute-start | bytes 823304 | tf_op jit(solution)/shard_map/ppermute | solution.py:685
  19.6 17.2 %collective-permute-start.9 = (f32[128,8,128]{2,1,0:T(8,128)S(1)}, f32[128,8,128]{2,1,0:T(8,128)S(1)}, u32[]{:S(2)}, u32[]{:S(2)}) collective-permute-start(f32[128,8,128]{2,1,0:T(8,128)S(1)} %get-tuple-element.68), channel_id=1, source_target_pairs={{0,8},{1,2},{2,1},{3,4},{4,3},{5,6},{6,5},{7,15},{8,0},{9,10},{10,... | collective-permute-start | bytes 1572872 | tf_op jit(solution)/shard_map/ppermute | solution.py:682
  22.7 14.9 %collective-permute-start.10 = (f32[128,8,128]{2,1,0:T(8,128)S(1)}, f32[128,8,128]{2,1,0:T(8,128)S(1)}, u32[]{:S(2)}, u32[]{:S(2)}) collective-permute-start(f32[128,8,128]{2,1,0:T(8,128)S(1)} %get-tuple-element.69), channel_id=1, source_target_pairs={{0,1},{1,0},{2,3},{3,2},{4,5},{5,4},{6,7},{7,6},{8,9},{9,8},{10,11... | collective-permute-start | bytes 1572872 | tf_op jit(solution)/shard_map/ppermute | solution.py:685
  29.1 8.5 %collective-permute-start.8 = (f32[64,8,128]{2,1,0:T(8,128)S(1)}, f32[64,8,128]{2,1,0:T(8,128)S(1)}, u32[]{:S(2)}, u32[]{:S(2)}) collective-permute-start(f32[64,8,128]{2,1,0:T(8,128)S(1)} %get-tuple-element.67), channel_id=1, source_target_pairs={{0,96},{8,104},{16,48},{24,56},{32,0},{40,8},{48,80},{56,88},{64,3... | collective-permute-start | bytes 786440 | tf_op jit(solution)/shard_map/ppermute | solution.py:744
  30.6 10.6 %collective-permute-start.6 = (f32[64,8,128]{2,1,0:T(8,128)S(1)}, f32[64,8,128]{2,1,0:T(8,128)S(1)}, u32[]{:S(2)}, u32[]{:S(2)}) collective-permute-start(f32[64,8,128]{2,1,0:T(8,128)S(1)} %get-tuple-element.65), channel_id=1, source_target_pairs={{0,32},{1,33},{2,34},{3,35},{4,36},{5,37},{6,38},{7,39},{8,16},{9,... | collective-permute-start | bytes 786440 | tf_op jit(solution)/shard_map/ppermute | solution.py:682
  31.4 9.8 %collective-permute-start.7 = (f32[64,8,128]{2,1,0:T(8,128)S(1)}, f32[64,8,128]{2,1,0:T(8,128)S(1)}, u32[]{:S(2)}, u32[]{:S(2)}) collective-permute-start(f32[64,8,128]{2,1,0:T(8,128)S(1)} %get-tuple-element.66), channel_id=1, source_target_pairs={{0,8},{1,9},{2,10},{3,11},{4,12},{5,13},{6,14},{7,15},{8,0},{9,1},... | collective-permute-start | bytes 786440 | tf_op jit(solution)/shard_map/ppermute | solution.py:685

commit v5 on v4

--- a/solution.py
+++ b/solution.py
@@ -15,7 +15,6 @@
 
 BX, BY, BS, NY = 16, 8, 16, 256
 T = 4
-SPARE = 3
 f32 = jnp.float32
 LIMIT = 8 * 2**20
 FIRST_LIMIT = 54 * 2**20
@@ -29,24 +28,26 @@
 AXES = ("space", "kx", "ky")
 
 
-def swaps(sizes, axis, odd, spare):
+def swaps(sizes, axis, odd, spare, against=False):
     pairs = []
     for n in range(sizes[0] * sizes[1] * sizes[2]):
         at = [n // (sizes[1] * sizes[2]), n // sizes[2] % sizes[1], n % sizes[2]]
         other = ((at[axis] + odd) ^ 1) - odd
         if 0 <= other < sizes[axis]:
             at[axis] = other
+        elif against:
+            at[0] = (at[0] + (1 if at[1] < sizes[1] // 2 else -1)) % sizes[0]
         else:
             at[spare] ^= 1
         pairs.append((n, (at[0] * sizes[1] + at[1]) * sizes[2] + at[2]))
     return pairs
 
 
-def ring(sizes, way):
+def ring(sizes):
     pairs = []
     for a in range(sizes[0]):
         for b in range(sizes[1]):
-            to = (a + (way if b >= sizes[1] // 2 else -way)) % sizes[0]
+            to = (a + (1 if b >= sizes[1] // 2 else -1)) % sizes[0]
             pairs.append((a * sizes[1] + b, to * sizes[1] + b))
     return pairs
 
@@ -58,6 +59,15 @@
 
 def is_even(i):
     return i % 2 == 0
+
+
+def loop(count, body, step):
+    def several(n, carry):
+        for k in range(step):
+            carry = body(n * step + k, carry)
+        return carry
+
+    lax.fori_loop(0, count // step, several, 0)
 
 
 class Flow:
@@ -172,7 +182,7 @@
 
 def first_messages(
     a_ref, depth_ref, mask_ref, inflow_ref,
-    np_ref, kx_od, kx_ev, x1, depth, mask, inflow, ay, geo, sems,
+    np_ref, kx_od, kx_ev, x_od, x_ev, depth, mask, inflow, ay, geo, sems,
 ):
     s, i, j, x_up, y_up = place()
     flow = Flow()
@@ -206,40 +216,38 @@
             store(ay, i * BY + j, each(lambda h: group(kj, cj, h), load(geo, 0)))
         return carry
 
-    lax.fori_loop(0, BX, y_speeds, 0)
+    loop(BX, y_speeds, 4)
     wait_all(own, sems.at[3])
-    low, high = 2 * BY * T, BX * BY * T
-    low, high = jnp.where(is_even(i), low, high), jnp.where(is_even(i), high, low)
-    flat, size = np_ref.reshape((BX + 4) * BY * T, 8, 128), 2 * BY * T
+    low, high = jnp.where(is_even(i), 0, BX - 2), jnp.where(is_even(i), BX - 2, 0)
     messages = [
-        pltpu.make_async_copy(flat.at[pl.ds(at, size)], ref.at[pl.ds(0, size)], sems.at[n])
+        pltpu.make_async_copy(own.at[pl.ds(at, 2)], ref, sems.at[n])
         for n, (at, ref) in enumerate(((low, kx_od), (high, kx_ev)), 4)
     ]
-    for t in range(size, size + SPARE):
-        kx_ev[t] = jnp.zeros((8, 128), f32)
     for c in messages:
         c.start()
     for b in range(2):
         y = pl.ds(flow.y[b], 128)
         first = jnp.broadcast_to(depth[0:1, y].astype(f32), (8, 128))
         last = jnp.broadcast_to(depth[BS - 1 : BS, y].astype(f32), (8, 128))
-        x1[4 * BX + b] = jnp.where(x_up, last, first)
+        x_od[4 * BX + b] = jnp.where(is_even(s), first, last)
+        x_ev[4 * BX + b] = jnp.where(is_even(s), last, first)
 
     def one_kx(i, carry):
         for b in range(2):
             rows = flow.edge_rows([np_ref[i + 2, j, 2 + b] for j in range(BY)])
             for l in range(2):
-                x1[l * 2 * BX + i * 2 + b] = rows[l]
-        return carry
-
-    lax.fori_loop(0, BX, one_kx, 0)
+                x_od[l * 2 * BX + i * 2 + b] = rows[l]
+                x_ev[l * 2 * BX + i * 2 + b] = rows[l]
+        return carry
+
+    loop(BX, one_kx, 4)
     for c in messages:
         c.wait()
 
 
-def ky_messages(np_ref, next_depth, ky_od, ky_ev, next_row, sems):
-    _, _, j, x_up, _ = place()
-    own = np_ref.at[pl.ds(2, BX)]
+def ky_messages(np_in, kx_ev, np_ref, ky_od, ky_ev, sems):
+    s, i, j, x_up, _ = place()
+    own = np_ref.reshape(BX + 4, BY, T, 8, 128).at[pl.ds(2, BX)]
     low, high = jnp.where(is_even(j), 0, BY - 2), jnp.where(is_even(j), BY - 2, 0)
     messages = [
         pltpu.make_async_copy(own.at[:, pl.ds(at, 2)], ref, sems.at[n])
@@ -247,8 +255,8 @@
     ]
     for c in messages:
         c.start()
-    coming = jnp.where(x_up, next_depth[0:1, :], next_depth[BS - 1 : BS, :]).astype(f32) * 0.01
-    next_row[...] = jnp.broadcast_to(coming, (8, NY))
+    size = 2 * BY * T
+    np_ref[pl.ds(jnp.where(is_even(i), (BX + 2) * BY * T, 0), size)] = kx_ev[...]
     for c in messages:
         c.wait()
 
@@ -308,7 +316,7 @@
             store(aky, i * (BY + 1) + j, each(lambda h, g: refract(kj, cj, h) * g, load(geo, 0), load(gy, 0)))
         return carry
 
-    lax.fori_loop(0, BX, one_kx, 0)
+    loop(BX, one_kx, 4)
     kx_faces(BX)
 
 
@@ -377,7 +385,7 @@
 
 
 def stage_one_edges(
-    np_in, ax, ay, rkx, aky, heights, hold_ref, spec, kx_od, x1, kx_ev, next_row,
+    np_in, ax, ay, rkx, aky, heights, hold_ref, spec, kx_od, x_od, x_ev,
     np_ref, p_ref, gx, edge, halo_speed, xnear, xflux, ky2_od, ky2_ev, fk, hrow,
 ):
     s, kx_place, ky_place, x_up, y_up = place()
@@ -392,20 +400,18 @@
         store(np_ref, base + r, each(lambda v: jnp.where(empty, 0.0, v), tiles))
         return carry
 
-    lax.fori_loop(0, 2 * BY, odd_side, 0)
-    size = 2 * BY * T
-    np_ref[pl.ds(jnp.where(odd_low, (BX + 2) * BY * T, 0), size)] = kx_ev[pl.ds(0, size)]
+    loop(2 * BY, odd_side, 8)
     h = heights[...]
     x_flip, y_flip = jnp.where(x_up, 0, 1), jnp.where(y_up, 0, 1)
     none = no_inflow(x_up)
+    use_od = is_even(s) == x_up
     for b in range(2):
         y = b ^ y_flip
         at = 4 * BX + y
         mine = h[:, 128 * b : 128 * b + 128]
-        last = x1[at][0:1, :] * 0.01
-        coming = next_row[0:1, 128 * b : 128 * b + 128]
-        low = jnp.where(s == 0, mine[0:1, :], jnp.where(x_up, last, coming))
-        high = jnp.where(s == lax.axis_size("space") - 1, mine[BS - 1 : BS, :], jnp.where(x_up, coming, last))
+        od, ev = x_od[at][0:1, :] * 0.01, x_ev[at][0:1, :] * 0.01
+        low = jnp.where(s == 0, mine[0:1, :], jnp.where(is_even(s), od, ev))
+        high = jnp.where(s == lax.axis_size("space") - 1, mine[BS - 1 : BS, :], jnp.where(is_even(s), ev, od))
         place_of = lax.broadcasted_iota(jnp.int32, (BS, 128), 0)
         before = jnp.where(place_of == 0, low, pltpu.roll(mine, 1, 0))
         after = jnp.where(place_of == BS - 1, high, pltpu.roll(mine, BS - 1, 0))
@@ -424,7 +430,8 @@
         c = group_factor(k, inverse) * jnp.abs(kx)
         for b in range(2):
             at = i * 2 + b
-            near, far = x1[at], x1[2 * BX + at]
+            near = jnp.where(use_od, x_od[at], x_ev[at])
+            far = jnp.where(use_od, x_od[2 * BX + at], x_ev[2 * BX + at])
             edge[at] = group(k, c, hrow[b])
             speed = group(k, c, hrow[2 + b])
             halo_speed[at] = speed
@@ -432,7 +439,7 @@
             xflux[at] = jnp.where(none, 0.0, speed * (3.0 * near - far))
         return carry
 
-    lax.fori_loop(0, BX, edges, 0)
+    loop(BX, edges, 8)
 
     g = load(gx, 0)
     for e, j in enumerate(EDGES):
@@ -468,7 +475,7 @@
             store(ky2_ev, i * 2 + l, each(lambda a, b: jnp.where(is_even(ky_place), b, a), down[l], up[l]))
         return carry
 
-    lax.fori_loop(0, BX, one_kx, 0)
+    loop(BX, one_kx, 4)
 
 
 def ky_column(n_ref, halo, i):
@@ -519,7 +526,7 @@
                 x2[l * 2 * BX + i * 2 + b] = rows[l]
         return carry
 
-    lax.fori_loop(0, BX, one_kx, 0)
+    loop(BX, one_kx, 4)
 
 
 def kx_messages(sp_in, sp_ref, kx2_od, kx2_ev, sems):
@@ -580,7 +587,7 @@
             lower_y = upper_y
         return carry
 
-    lax.fori_loop(0, BX, one_kx, 0)
+    loop(BX, one_kx, 2)
 
 
 def halo_terms(g, low_speeds, high_speeds, low, high):
@@ -621,7 +628,7 @@
             store(q_ref, slab, each(lambda q, t: q + t, load(q_ref, slab), term))
         return carry
 
-    lax.fori_loop(0, BY, kx_ends, 0)
+    loop(BY, kx_ends, 4)
     second = flow.rows == jnp.where(x_up, 1, 6)
 
     def one_kx(i, carry):
@@ -648,7 +655,7 @@
         send_out(done, out, sem, i)
         return carry
 
-    lax.fori_loop(0, BX, one_kx, 0)
+    loop(BX, one_kx, 4)
     wait_all(done, sem)
 
 
@@ -685,32 +692,33 @@
         return lax.ppermute(message, AXES, swaps(sizes, AXES.index(axis), 0, 0))
 
     sem = pltpu.SemaphoreType.DMA
-    np5, kx_od, kx_ev, x1, depth, mask, spectrum, ay = call(
+    np5, kx_od, kx_ev, x_od, x_ev, depth, mask, spectrum, ay = call(
         first_messages,
-        (v(BX + 4, BY, T), v(kx_tiles), v(kx_tiles + SPARE), v(4 * BX + 2), pltpu.VMEM((BS, NY), jnp.int32),
+        (v(BX + 4, BY, T), v(2, BY, T), v(2, BY, T), v(4 * BX + 2), v(4 * BX + 2), pltpu.VMEM((BS, NY), jnp.int32),
          pltpu.VMEM((BS, NY), jnp.int32), pltpu.VMEM((NKX, NKY), f32), v(slabs)),
         (action, depth_cm, inflow_mask, inflow),
         "hhhh",
-        "v" * 8,
+        "v" * 9,
         [v(T), sem((6,))],
         us=0,
         limit=FIRST_LIMIT,
     )
-    next_depth = lax.ppermute(depth, AXES[:2], ring(sizes, -1))
-    x1 = lax.ppermute(x1, AXES[:2], ring(sizes, 1))
-    kx_od, kx_ev = swap_odd(kx_od, "kx", "space"), swap_even(kx_ev, "kx")
-    ky_od, ky_ev, next_row = call(
+    kx_ev = swap_even(kx_ev, "kx").reshape(kx_tiles, 8, 128)
+    x_od = swap_odd(x_od, "space", "kx")
+    x_ev = swap_even(x_ev, "space")
+    kx_od = swap_odd(kx_od, "kx", "space").reshape(kx_tiles, 8, 128)
+    np3, ky_od, ky_ev = call(
         ky_messages,
-        (v(BX, 2, T), v(BX, 2, T), pltpu.VMEM((8, NY), f32)),
-        (np5, next_depth),
+        (v(padded), v(BX, 2, T), v(BX, 2, T)),
+        (np5.reshape(padded, 8, 128), kx_ev),
         "v" * 2,
         "v" * 3,
         [sem((2,))],
+        alias={0: 0},
         us=0,
     )
     ky_od = swap_odd(ky_od, "ky", "kx").reshape(ky_tiles, 8, 128)
     ky_ev = swap_even(ky_ev, "ky").reshape(ky_tiles, 8, 128)
-    np3 = np5.reshape(padded, 8, 128)
     ax, rkx, aky, gy, heights, hold, spec = call(
         speeds,
         (v(slabs), v((BX + 1) * BY * T), v(BX * (BY + 1) * T), v(T), pltpu.VMEM((BS, NY), f32),
@@ -724,8 +732,8 @@
     np3, part, gx, edge, halo_speed, xnear, xflux, ky2_od, ky2_ev = call(
         stage_one_edges,
         (v(padded), v(edge_slabs), v(T), v(2 * BX), v(2 * BX), v(2 * BX), v(2 * BX), v(ky_tiles), v(ky_tiles)),
-        (np3, ax, ay, rkx, aky, heights, hold, spec, kx_od, x1, kx_ev, next_row),
-        "v" * 12,
+        (np3, ax, ay, rkx, aky, heights, hold, spec, kx_od, x_od, x_ev),
+        "v" * 11,
         "v" * 9,
         [v(len(EDGES) * T), v(4)],
         alias={0: 0},
@@ -741,7 +749,7 @@
         [v(len(MIDDLE) * T)],
         us=0,
     )
-    x2 = lax.ppermute(x2, AXES[:2], ring(sizes, 1))
+    x2 = lax.ppermute(x2, AXES[:2], ring(sizes))
     sp, kx2_od, kx2_ev = call(
         kx_messages,
         (v(padded), v(kx_tiles), v(kx_tiles)),
@@ -752,7 +760,7 @@
         alias={0: 0},
         us=0,
     )
-    kx2_od, kx2_ev = swap_odd(kx2_od, "kx", "space"), swap_even(kx2_ev, "kx")
+    kx2_od, kx2_ev = lax.ppermute(kx2_od, AXES, swaps(sizes, 1, 1, 0, True)), swap_even(kx2_ev, "kx")
     (q,) = call(
         stage_two_inner,
         (v(slabs),),

time: 43.3 us -> 39.3 us (0.908)
  Pallas kernels: 17.2 us -> 12.8 us
  waiting for transfers between devices: 7.73 us -> 11.8 us
  starting transfers between devices: 18.2 us -> 14.5 us
    ppermute x4 -> x5, waiting for transfers between devices: 2.25 us -> 6.82 us  [swap_even(): return lax.ppermute(message, AXES, swaps(sizes, AXES.index(axis), 0, 0))]
    pallas_call x8, Pallas kernels: 17.2 us -> 12.8 us  [call(): pl.pallas_call(kernel, out_shape=tuple(outs), in_specs=[whole[c] for c in...]
    ppermute x4 -> x5, starting transfers between devices: 3.99 us -> 2.38 us  [swap_even(): return lax.ppermute(message, AXES, swaps(sizes, AXES.index(axis), 0, 0))]
    ppermute x4, starting transfers between devices: 9.44 us -> 7.97 us  [swap_odd(): lax.ppermute(message, AXES, swaps(sizes, AXES.index(axis), 1, AXES.index(...]
    ppermute x3 -> x2, waiting for transfers between devices: 0.88 us -> 0.01 us  [the longest x1 0.01 us: per_device(): x2 = lax.ppermute(x2, AXES[:2], ring(sizes))]
    ppermute x3 -> x2, starting transfers between devices: 4.73 us -> 4.11 us  [the longest x1 4.04 us: per_device(): x2 = lax.ppermute(x2, AXES[:2], ring(sizes))]
  transfers between devices with their start and end apart: 11 -> 11, of which waited for: 6 -> 4; matrix products, arithmetic and copies ran while one was open for 0% -> 0% of each run, Pallas kernels for 30% -> 23%
where the time goes in v5:
time: 39.3 us; the launch traced here: 39.1 us
  starting transfers between devices  14.5 us (37%)
  Pallas kernels  12.8 us (33%)
  waiting for transfers between devices  11.8 us (30%)
    pallas_call x8, Pallas kernels, call(): pl.pallas_call(kernel, out_shape=tuple(outs), in_specs=[whole[c] for c in...  12.8 us
    ppermute x4, starting transfers between devices, swap_odd(): lax.ppermute(message, AXES, swaps(sizes, AXES.index(axis), 1, AXES.index(...  7.97 us
    ppermute x5, waiting for transfers between devices, swap_even(): return lax.ppermute(message, AXES, swaps(sizes, AXES.index(axis), 0, 0))  6.82 us
    ppermute x4, waiting for transfers between devices, swap_odd(): lax.ppermute(message, AXES, swaps(sizes, AXES.index(axis), 1, AXES.index(...  4.94 us
    ppermute x1, starting transfers between devices, per_device(): x2 = lax.ppermute(x2, AXES[:2], ring(sizes))  4.04 us
    ppermute x5, starting transfers between devices, swap_even(): return lax.ppermute(message, AXES, swaps(sizes, AXES.index(axis), 0, 0))  2.38 us
  transfers between devices with their start and end apart: 11, of which 4 were waited for; matrix products, arithmetic and copies ran while one was open for 0% of the time, Pallas kernels for 23%

profile of v5, /device:TPU:8, one launch (start us, length us, event | category | flops | bytes accessed | tf_op | source)
XLA Modules:
  0.0 39.1 jit_solution(1296301583593828480)
XLA Ops:
  0.0 2.0 %first_messages.1 = (f32[20,8,4,8,128]{4,3,2,1,0:T(8,128)S(1)}, f32[2,8,4,8,128]{4,3,2,1,0:T(8,128)S(1)}, f32[2,8,4,8,128]{4,3,2,1,0:T(8,128)S(1)}, f32[66,8,128...) custom-call(f32[16,8,16,256]{3,2,1,0:T(8,128)} %a_ref.1, ...), custom_call_target="tpu_custom_call" | custom-call | tf_op jit(solution)/shard_map/first_messages/pallas_call | solution.py:667
  2.0 0.1 collective-permute-start
  2.1 1.6 %collective-permute-start.1 = (f32[2,8,4,8,128]{4,3,2,1,0:T(8,128)S(1)}, f32[2,8,4,8,128]{4,3,2,1,0:T(8,128)S(1)}, u32[]{:S(2)}, u32[]{:S(2)}) collective-permute-start(f32[2,8,4,8,128]{4,3,2,1,0:T(8,128)S(1)} %get-tuple-element.52), channel_id=1, source_target_pairs={{0,32},{1,33},{2,34},{3,35},{4,36},{5,37},{6,38},{7,39},{8,16},{9,... | collective-permute-start | bytes 786440 | tf_op jit(solution)/shard_map/ppermute | solution.py:689
  3.6 0.9 %collective-permute-start.2 = (f32[66,8,128]{2,1,0:T(8,128)S(1)}, f32[66,8,128]{2,1,0:T(8,128)S(1)}, u32[]{:S(2)}, u32[]{:S(2)}) collective-permute-start(f32[66,8,128]{2,1,0:T(8,128)S(1)} %get-tuple-element.53), channel_id=1, source_target_pairs={{0,8},{1,9},{2,10},{3,11},{4,12},{5,13},{6,14},{7,15},{8,0},{9,1},... | collective-permute-start | bytes 811016 | tf_op jit(solution)/shard_map/ppermute | solution.py:689
  4.6 0.0 collective-permute-done
  4.6 0.1 ky_messages.1
  4.7 4.9 %collective-permute-start.4 = (f32[16,2,4,8,128]{4,3,2,1,0:T(8,128)S(1)}, f32[16,2,4,8,128]{4,3,2,1,0:T(8,128)S(1)}, u32[]{:S(2)}, u32[]{:S(2)}) collective-permute-start(f32[16,2,4,8,128]{4,3,2,1,0:T(8,128)S(1)} %get-tuple-element.62), channel_id=1, source_target_pairs={{0,8},{1,2},{2,1},{3,4},{4,3},{5,6},{6,5},{7,15},{8,0},{9,10},{10,... | collective-permute-start | bytes 1572872 | tf_op jit(solution)/shard_map/ppermute | solution.py:689
  9.6 0.0 collective-permute-start.5
  9.6 0.9 %collective-permute-start.3 = (f32[66,8,128]{2,1,0:T(8,128)S(1)}, f32[66,8,128]{2,1,0:T(8,128)S(1)}, u32[]{:S(2)}, u32[]{:S(2)}) collective-permute-start(f32[66,8,128]{2,1,0:T(8,128)S(1)} %get-tuple-element.54), channel_id=1, source_target_pairs={{0,32},{1,33},{2,34},{3,35},{4,36},{5,37},{6,38},{7,39},{8,40},{9,... | collective-permute-start | bytes 811016 | tf_op jit(solution)/shard_map/ppermute | solution.py:692
  10.5 2.2 %speeds.1 = (f32[512,8,128]{2,1,0:T(8,128)S(1)}, f32[544,8,128]{2,1,0:T(8,128)S(1)}, f32[576,8,128]{2,1,0:T(8,128)S(1)}, f32[4,8,128]{2,1,0:T(8,128)S(1)}, f32[1...) custom-call(s32[16,256]{1,0:T(8,128)S(1)} %get-tuple-element.42.depth, ...), custom_call_target="tpu_custom_call" | custom-call | flops 4000000000 | tf_op jit(solution)/shard_map/speeds/pallas_call | solution.py:667
  12.7 0.0 collective-permute-done.1
  12.7 0.0 collective-permute-done.2.x_od
  12.7 6.0 %collective-permute-done.3.x_ev = f32[66,8,128]{2,1,0:T(8,128)S(1)} collective-permute-done((f32[66,8,128]{2,1,0:T(8,128)S(1)}, f32[66,8,128]{2,1,0:T(8,128)S(1)}, u32[]{:S(2)}, u32[]{:S(2)}) %collective-permute-start.3) | collective-permute-done | bytes 270368 | tf_op jit(solution)/shard_map/ppermute | solution.py:692
  18.7 1.6 %stage_one_edges.1 = (f32[640,8,128]{2,1,0:T(8,128)S(1)}, f32[256,8,128]{2,1,0:T(8,128)S(1)}, f32[4,8,128]{2,1,0:T(8,128)S(1)}, f32[32,8,128]{2,1,0:T(8,128)S(1)...) custom-call(f32[640,8,128]{2,1,0:T(8,128)S(1)} %get-tuple-element.41, ...), custom_call_target="tpu_custom_call", output_to_operand_aliasing={{0}: (0, {})} | custom-call | tf_op jit(solution)/shard_map/stage_one_edges/pallas_call | solution.py:667
  20.3 0.6 %collective-permute-start.9 = (f32[128,8,128]{2,1,0:T(8,128)S(1)}, f32[128,8,128]{2,1,0:T(8,128)S(1)}, u32[]{:S(2)}, u32[]{:S(2)}) collective-permute-start(f32[128,8,128]{2,1,0:T(8,128)S(1)} %get-tuple-element.70), channel_id=1, source_target_pairs={{0,8},{1,2},{2,1},{3,4},{4,3},{5,6},{6,5},{7,15},{8,0},{9,10},{10,... | collective-permute-start | bytes 1572872 | tf_op jit(solution)/shard_map/ppermute | solution.py:689
  20.9 1.3 %collective-permute-start.10 = (f32[128,8,128]{2,1,0:T(8,128)S(1)}, f32[128,8,128]{2,1,0:T(8,128)S(1)}, u32[]{:S(2)}, u32[]{:S(2)}) collective-permute-start(f32[128,8,128]{2,1,0:T(8,128)S(1)} %get-tuple-element.71), channel_id=1, source_target_pairs={{0,1},{1,0},{2,3},{3,2},{4,5},{5,4},{6,7},{7,6},{8,9},{9,8},{10,11... | collective-permute-start | bytes 1572872 | tf_op jit(solution)/shard_map/ppermute | solution.py:692
  22.2 0.1 collective-permute-done.4
  22.3 0.9 %collective-permute-done.5 = f32[16,2,4,8,128]{4,3,2,1,0:T(8,128)S(1)} collective-permute-done((f32[16,2,4,8,128]{4,3,2,1,0:T(8,128)S(1)}, f32[16,2,4,8,128]{4,3,2,1,0:T(8,128)S(1)}, u32[]{:S(2)}, u32[]{:S(2)}) %collective-permute-start.5) | collective-permute-done | bytes 524320 | tf_op jit(solution)/shard_map/ppermute | solution.py:692
  23.2 2.1 %stage_one_rest.1 = (f32[640,8,128]{2,1,0:T(8,128)S(1)}, f32[64,8,128]{2,1,0:T(8,128)S(1)}) custom-call(f32[640,8,128]{2,1,0:T(8,128)S(1)} %get-tuple-element.55.np_ref, f32[256,8,128]{2,1,0:T(8,128)S(1)} %get-tuple-element.56.p_ref, f32[512,8,128]{2,1,0:T(8,128)S(1)} %get-tuple-element.45.ax, f32[512,8,128]{2,1,0:T(8,128)S(1)} %get-tuple-element.46.ay, ...), custom_call_target="tpu_custom_call" | custom-call | tf_op jit(solution)/shard_map/stage_one_rest/pallas_call | solution.py:667
  25.3 4.0 %collective-permute-start.8 = (f32[64,8,128]{2,1,0:T(8,128)S(1)}, f32[64,8,128]{2,1,0:T(8,128)S(1)}, u32[]{:S(2)}, u32[]{:S(2)}) collective-permute-start(f32[64,8,128]{2,1,0:T(8,128)S(1)} %get-tuple-element.69), channel_id=1, source_target_pairs={{0,96},{8,104},{16,48},{24,56},{32,0},{40,8},{48,80},{56,88},{64,3... | collective-permute-start | bytes 786440 | tf_op jit(solution)/shard_map/ppermute | solution.py:752
  29.3 0.1 kx_messages.1
  29.4 0.1 collective-permute-start.6
  29.5 0.1 collective-permute-start.7
  29.6 2.9 %stage_two_inner.1.q_in = f32[512,8,128]{2,1,0:T(8,128)S(1)} custom-call(f32[640,8,128]{2,1,0:T(8,128)S(1)} %get-tuple-element.55.np_ref, f32[640,8,128]{2,1,0:T(8,128)S(1)} %get-tuple-element.65.sp_ref, f32[512,8,128]{2,1,0:T(8,128)S(1)} %get-tuple-element.45.ax, f32[512,8,128]{2,1,0:T(8,128)S(1)} %get-tuple-element.46.ay, ...), custom_call_target="tpu_custom_call" | custom-call | flops 4000000000 | tf_op jit(solution)/shard_map/stage_two_inner/pallas_call | solution.py:667
  32.5 4.8 %collective-permute-done.9.ky_od = f32[128,8,128]{2,1,0:T(8,128)S(1)} collective-permute-done((f32[128,8,128]{2,1,0:T(8,128)S(1)}, f32[128,8,128]{2,1,0:T(8,128)S(1)}, u32[]{:S(2)}, u32[]{:S(2)}) %collective-permute-start.9) | collective-permute-done | bytes 524320 | tf_op jit(solution)/shard_map/ppermute | solution.py:689
  37.3 0.0 collective-permute-done.10.ky_ev
  37.3 0.0 collective-permute-done.8.x2
  37.3 0.0 collective-permute-done.6.kx_od
  37.3 0.0 collective-permute-done.7.kx_ev
  37.3 1.8 %stage_two_outer.1 = (f32[512,8,128]{2,1,0:T(8,128)S(1)}, f32[16,8,16,256]{3,2,1,0:T(8,128)}) custom-call(f32[512,8,128]{2,1,0:T(8,128)S(1)} %stage_two_inner.1.q_in, f32[512,8,128]{2,1,0:T(8,128)S(1)} %get-tuple-element.45.ax, f32[544,8,128]{2,1,0:T(8,128)S(1)} %get-tuple-element.47.rkx, ...), custom_call_target="tpu_custom_call", output_to_operand_aliasing={{0}: (0, {})} | custom-call | tf_op jit(solution)/shard_map/stage_two_outer/pallas_call | solution.py:667
Async XLA Ops:
  2.0 2.6 %collective-permute-start = (f32[2,8,4,8,128]{4,3,2,1,0:T(8,128)S(1)}, f32[2,8,4,8,128]{4,3,2,1,0:T(8,128)S(1)}, u32[]{:S(2)}, u32[]{:S(2)}) collective-permute-start(f32[2,8,4,8,128]{4,3,2,1,0:T(8,128)S(1)} %get-tuple-element.40), channel_id=1, source_target_pairs={{0,8},{1,9},{2,10},{3,11},{4,12},{5,13},{6,14},{7,15},{8,0},{9,1},... | collective-permute-start | bytes 786440 | tf_op jit(solution)/shard_map/ppermute | solution.py:692
  2.1 10.6 %collective-permute-start.1 = (f32[2,8,4,8,128]{4,3,2,1,0:T(8,128)S(1)}, f32[2,8,4,8,128]{4,3,2,1,0:T(8,128)S(1)}, u32[]{:S(2)}, u32[]{:S(2)}) collective-permute-start(f32[2,8,4,8,128]{4,3,2,1,0:T(8,128)S(1)} %get-tuple-element.52), channel_id=1, source_target_pairs={{0,32},{1,33},{2,34},{3,35},{4,36},{5,37},{6,38},{7,39},{8,16},{9,... | collective-permute-start | bytes 786440 | tf_op jit(solution)/shard_map/ppermute | solution.py:689
  3.6 9.1 %collective-permute-start.2 = (f32[66,8,128]{2,1,0:T(8,128)S(1)}, f32[66,8,128]{2,1,0:T(8,128)S(1)}, u32[]{:S(2)}, u32[]{:S(2)}) collective-permute-start(f32[66,8,128]{2,1,0:T(8,128)S(1)} %get-tuple-element.53), channel_id=1, source_target_pairs={{0,8},{1,9},{2,10},{3,11},{4,12},{5,13},{6,14},{7,15},{8,0},{9,1},... | collective-permute-start | bytes 811016 | tf_op jit(solution)/shard_map/ppermute | solution.py:689
  4.7 17.7 %collective-permute-start.4 = (f32[16,2,4,8,128]{4,3,2,1,0:T(8,128)S(1)}, f32[16,2,4,8,128]{4,3,2,1,0:T(8,128)S(1)}, u32[]{:S(2)}, u32[]{:S(2)}) collective-permute-start(f32[16,2,4,8,128]{4,3,2,1,0:T(8,128)S(1)} %get-tuple-element.62), channel_id=1, source_target_pairs={{0,8},{1,2},{2,1},{3,4},{4,3},{5,6},{6,5},{7,15},{8,0},{9,10},{10,... | collective-permute-start | bytes 1572872 | tf_op jit(solution)/shard_map/ppermute | solution.py:689
  9.6 13.6 %collective-permute-start.5 = (f32[16,2,4,8,128]{4,3,2,1,0:T(8,128)S(1)}, f32[16,2,4,8,128]{4,3,2,1,0:T(8,128)S(1)}, u32[]{:S(2)}, u32[]{:S(2)}) collective-permute-start(f32[16,2,4,8,128]{4,3,2,1,0:T(8,128)S(1)} %get-tuple-element.63), channel_id=1, source_target_pairs={{0,1},{1,0},{2,3},{3,2},{4,5},{5,4},{6,7},{7,6},{8,9},{9,8},{10,11... | collective-permute-start | bytes 1572872 | tf_op jit(solution)/shard_map/ppermute | solution.py:692
  9.6 9.1 %collective-permute-start.3 = (f32[66,8,128]{2,1,0:T(8,128)S(1)}, f32[66,8,128]{2,1,0:T(8,128)S(1)}, u32[]{:S(2)}, u32[]{:S(2)}) collective-permute-start(f32[66,8,128]{2,1,0:T(8,128)S(1)} %get-tuple-element.54), channel_id=1, source_target_pairs={{0,32},{1,33},{2,34},{3,35},{4,36},{5,37},{6,38},{7,39},{8,40},{9,... | collective-permute-start | bytes 811016 | tf_op jit(solution)/shard_map/ppermute | solution.py:692
  20.3 17.0 %collective-permute-start.9 = (f32[128,8,128]{2,1,0:T(8,128)S(1)}, f32[128,8,128]{2,1,0:T(8,128)S(1)}, u32[]{:S(2)}, u32[]{:S(2)}) collective-permute-start(f32[128,8,128]{2,1,0:T(8,128)S(1)} %get-tuple-element.70), channel_id=1, source_target_pairs={{0,8},{1,2},{2,1},{3,4},{4,3},{5,6},{6,5},{7,15},{8,0},{9,10},{10,... | collective-permute-start | bytes 1572872 | tf_op jit(solution)/shard_map/ppermute | solution.py:689
  20.9 16.4 %collective-permute-start.10 = (f32[128,8,128]{2,1,0:T(8,128)S(1)}, f32[128,8,128]{2,1,0:T(8,128)S(1)}, u32[]{:S(2)}, u32[]{:S(2)}) collective-permute-start(f32[128,8,128]{2,1,0:T(8,128)S(1)} %get-tuple-element.71), channel_id=1, source_target_pairs={{0,1},{1,0},{2,3},{3,2},{4,5},{5,4},{6,7},{7,6},{8,9},{9,8},{10,11... | collective-permute-start | bytes 1572872 | tf_op jit(solution)/shard_map/ppermute | solution.py:692
  25.3 12.0 %collective-permute-start.8 = (f32[64,8,128]{2,1,0:T(8,128)S(1)}, f32[64,8,128]{2,1,0:T(8,128)S(1)}, u32[]{:S(2)}, u32[]{:S(2)}) collective-permute-start(f32[64,8,128]{2,1,0:T(8,128)S(1)} %get-tuple-element.69), channel_id=1, source_target_pairs={{0,96},{8,104},{16,48},{24,56},{32,0},{40,8},{48,80},{56,88},{64,3... | collective-permute-start | bytes 786440 | tf_op jit(solution)/shard_map/ppermute | solution.py:752
  29.4 7.9 %collective-permute-start.6 = (f32[64,8,128]{2,1,0:T(8,128)S(1)}, f32[64,8,128]{2,1,0:T(8,128)S(1)}, u32[]{:S(2)}, u32[]{:S(2)}) collective-permute-start(f32[64,8,128]{2,1,0:T(8,128)S(1)} %get-tuple-element.67), channel_id=1, source_target_pairs={{0,32},{1,33},{2,34},{3,35},{4,36},{5,37},{6,38},{7,39},{8,16},{9,... | collective-permute-start | bytes 786440 | tf_op jit(solution)/shard_map/ppermute | solution.py:763
  29.5 7.8 %collective-permute-start.7 = (f32[64,8,128]{2,1,0:T(8,128)S(1)}, f32[64,8,128]{2,1,0:T(8,128)S(1)}, u32[]{:S(2)}, u32[]{:S(2)}) collective-permute-start(f32[64,8,128]{2,1,0:T(8,128)S(1)} %get-tuple-element.68), channel_id=1, source_target_pairs={{0,8},{1,9},{2,10},{3,11},{4,12},{5,13},{6,14},{7,15},{8,0},{9,1},... | collective-permute-start | bytes 786440 | tf_op jit(solution)/shard_map/ppermute | solution.py:692

commit v6 on v5

--- a/solution.py
+++ b/solution.py
@@ -182,7 +182,7 @@
 
 def first_messages(
     a_ref, depth_ref, mask_ref, inflow_ref,
-    np_ref, kx_od, kx_ev, x_od, x_ev, depth, mask, inflow, ay, geo, sems,
+    np_ref, kx_od, kx_ev, ky_od, depth, mask, inflow, sems,
 ):
     s, i, j, x_up, y_up = place()
     flow = Flow()
@@ -197,34 +197,31 @@
         for b in range(2):
             x, y = flow.natural(a, b)
             pltpu.make_async_copy(a_ref.at[:, :, x, y], own.at[:, :, 2 * a + b], sems.at[3]).start()
-    for c in small:
-        c.wait()
-    h = depth[...].astype(f32) * 0.01
-    hy = 0.5 * (h + jnp.where(y_up, shifted(h, 1, True), shifted(h, 1, False)))
-    x_flip, y_flip = jnp.where(x_up, 0, 1), jnp.where(y_up, 0, 1)
-    for a in range(2):
-        for b in range(2):
-            geo[(a ^ x_flip) * 2 + (b ^ y_flip)] = hy[8 * a : 8 * a + 8, 128 * b : 128 * b + 128]
-    kx_first, ky_first = i * BX, j * BY
-
-    def y_speeds(i, carry):
-        kx, ky = centre(kx_first, i), centre_rows(flow, ky_first)
-        k, inverse = wave(kx, ky)
-        c = group_factor(k, inverse) * jnp.abs(ky)
-        for j in range(BY):
-            kj, cj = pick(k, j), pick(c, j)
-            store(ay, i * BY + j, each(lambda h: group(kj, cj, h), load(geo, 0)))
-        return carry
-
-    loop(BX, y_speeds, 4)
     wait_all(own, sems.at[3])
     low, high = jnp.where(is_even(i), 0, BX - 2), jnp.where(is_even(i), BX - 2, 0)
     messages = [
-        pltpu.make_async_copy(own.at[pl.ds(at, 2)], ref, sems.at[n])
-        for n, (at, ref) in enumerate(((low, kx_od), (high, kx_ev)), 4)
+        pltpu.make_async_copy(src, ref, sems.at[n])
+        for n, (src, ref) in enumerate(
+            (
+                (own.at[:, pl.ds(jnp.where(is_even(j), 0, BY - 2), 2)], ky_od),
+                (own.at[pl.ds(low, 2)], kx_od),
+                (own.at[pl.ds(high, 2)], kx_ev),
+            ),
+            4,
+        )
     ]
     for c in messages:
         c.start()
+    for c in small + messages:
+        c.wait()
+
+
+def more_messages(np_in, depth, kx_ev, np_ref, ky_ev, x_od, x_ev, sem):
+    s, i, j, x_up, _ = place()
+    flow = Flow()
+    own = np_ref.reshape(BX + 4, BY, T, 8, 128).at[pl.ds(2, BX)]
+    message = pltpu.make_async_copy(own.at[:, pl.ds(jnp.where(is_even(j), BY - 2, 0), 2)], ky_ev, sem)
+    message.start()
     for b in range(2):
         y = pl.ds(flow.y[b], 128)
         first = jnp.broadcast_to(depth[0:1, y].astype(f32), (8, 128))
@@ -234,34 +231,19 @@
 
     def one_kx(i, carry):
         for b in range(2):
-            rows = flow.edge_rows([np_ref[i + 2, j, 2 + b] for j in range(BY)])
+            rows = flow.edge_rows([np_ref[((i + 2) * BY + j) * T + 2 + b] for j in range(BY)])
             for l in range(2):
                 x_od[l * 2 * BX + i * 2 + b] = rows[l]
                 x_ev[l * 2 * BX + i * 2 + b] = rows[l]
         return carry
 
     loop(BX, one_kx, 4)
-    for c in messages:
-        c.wait()
-
-
-def ky_messages(np_in, kx_ev, np_ref, ky_od, ky_ev, sems):
-    s, i, j, x_up, _ = place()
-    own = np_ref.reshape(BX + 4, BY, T, 8, 128).at[pl.ds(2, BX)]
-    low, high = jnp.where(is_even(j), 0, BY - 2), jnp.where(is_even(j), BY - 2, 0)
-    messages = [
-        pltpu.make_async_copy(own.at[:, pl.ds(at, 2)], ref, sems.at[n])
-        for n, (at, ref) in enumerate(((low, ky_od), (high, ky_ev)))
-    ]
-    for c in messages:
-        c.start()
     size = 2 * BY * T
     np_ref[pl.ds(jnp.where(is_even(i), (BX + 2) * BY * T, 0), size)] = kx_ev[...]
-    for c in messages:
-        c.wait()
-
-
-def speeds(depth, mask, inflow, ax, rkx, aky, gy, heights, hold, spec, geo):
+    message.wait()
+
+
+def speeds(depth, mask, inflow, ax, ay, rkx, aky, gy, heights, hold, spec, geo):
     _, kx_place, ky_place, x_up, y_up = place()
     flow = Flow()
     kx_first, ky_first = kx_place * BX, ky_place * BY
@@ -269,6 +251,7 @@
     heights[...] = h
     y_next, y_last = shifted(h, 1, True), shifted(h, 1, False)
     hx = 0.5 * (h + jnp.where(x_up, shifted(h, 0, True), shifted(h, 0, False)))
+    hy = 0.5 * (h + jnp.where(y_up, y_next, y_last))
     slope = (y_last - y_next) * (1.0 / (2.0 * spacing))
     x_flip, y_flip = jnp.where(x_up, 0, 1), jnp.where(y_up, 0, 1)
     for a in range(2):
@@ -279,6 +262,7 @@
             hold[at] = mask[part]
             geo[at] = h[part]
             geo[T + at] = hx[part]
+            geo[2 * T + at] = hy[part]
 
     lanes = lax.broadcasted_iota(jnp.int32, (8, NKY), 1)
     for half in range(BX // 8):
@@ -302,10 +286,12 @@
     def one_kx(i, carry):
         kx = centre(kx_first, i)
         k, inverse = wave(kx, ky)
-        c = group_factor(k, inverse) * jnp.abs(kx)
+        c = group_factor(k, inverse)
+        cx, cy = c * jnp.abs(kx), c * jnp.abs(ky)
         for j in range(BY):
-            kj, cj = pick(k, j), pick(c, j)
-            store(ax, i * BY + j, each(lambda h: group(kj, cj, h), load(geo, 1)))
+            kj, cxj, cyj = pick(k, j), pick(cx, j), pick(cy, j)
+            store(ax, i * BY + j, each(lambda h: group(kj, cxj, h), load(geo, 1)))
+            store(ay, i * BY + j, each(lambda h: group(kj, cyj, h), load(geo, 2)))
         kx_faces(i)
         k, _ = wave(kx, ky_face)
         c = refract_factor(k)
@@ -320,24 +306,28 @@
     kx_faces(BX)
 
 
-def space_change(flow, n, ax_ref, ay_ref, i, j, edge, halo_row, halo_flux):
-    slab = i * BY + j
-    ax, ay = load(ax_ref, slab), load(ay_ref, slab)
-    n3 = each(lambda v: 3.0 * v, n)
+def x_change(flow, n, ax_ref, i, j, edge, halo_row, halo_flux):
+    ax = load(ax_ref, i * BY + j)
     total = [[None, None], [None, None]]
     for b in range(2):
         ax[1][b] = jnp.where(flow.x_last, row(edge, i, j, b), ax[1][b])
         before = flow.before_x(n, b, 0.0 if halo_row is None else row(halo_row, i, j, b))
-        out = [[ax[a][b] * (n3[a][b] - before[a])] * 2 for a in range(2)]
+        out = [[ax[a][b] * (3.0 * n[a][b] - before[a])] * 2 for a in range(2)]
         into = flow.before_x(out, b, 0.0 if halo_flux is None else row(halo_flux, i, j, b))
         for a in range(2):
             total[a][b] = out[a][b] - into[a]
+    return total
+
+
+def y_change(flow, n, ay_ref, i, j):
+    ay = load(ay_ref, i * BY + j)
+    total = [[None, None], [None, None]]
     for a in range(2):
         before = flow.before_y(n, a)
-        out = [ay[a][b] * (n3[a][b] - before[b]) for b in range(2)]
+        out = [ay[a][b] * (3.0 * n[a][b] - before[b]) for b in range(2)]
         into = flow.before_y([out, out], 0)
         for b in range(2):
-            total[a][b] = total[a][b] + (out[b] - into[b])
+            total[a][b] = out[b] - into[b]
     return total
 
 
@@ -384,8 +374,20 @@
     return s == jnp.where(x_up, 0, lax.axis_size("space") - 1)
 
 
+def stage_one_y(np_ref, ay, p_ref):
+    flow = Flow()
+
+    def one_kx(i, carry):
+        for j in range(BY):
+            n = load(np_ref, (i + 2) * BY + j)
+            store(p_ref, i * BY + j, each(lambda n, t: n - t, n, y_change(flow, n, ay, i, j)))
+        return carry
+
+    loop(BX, one_kx, 2)
+
+
 def stage_one_edges(
-    np_in, ax, ay, rkx, aky, heights, hold_ref, spec, kx_od, x_od, x_ev,
+    np_in, p_y, ax, rkx, aky, heights, hold_ref, spec, kx_od, x_od, x_ev,
     np_ref, p_ref, gx, edge, halo_speed, xnear, xflux, ky2_od, ky2_ev, fk, hrow,
 ):
     s, kx_place, ky_place, x_up, y_up = place()
@@ -451,11 +453,11 @@
         part = {}
         for e, j in enumerate(EDGES):
             n = load(np_ref, (i + 2) * BY + j)
-            total = space_change(flow, n, ax, ay, i, j, edge, xnear, xflux)
+            total = x_change(flow, n, ax, i, j, edge, xnear, xflux)
             upper = kx_flux(g, rkx, np_ref, i + 1, j)
             lower = load(fk, e)
             store(fk, e, upper)
-            part[j] = each(lambda n, t, u, v: n - (t + (u - v)), n, total, upper, lower)
+            part[j] = each(lambda p, t, u, v: p - (t + (u - v)), load(p_y, i * BY + j), total, upper, lower)
             store(p_ref, i * len(EDGES) + e, part[j])
 
         def own(f, a, b):
@@ -484,38 +486,44 @@
     return layers + [halo.high(i * 2 + l) for l in range(2)]
 
 
-def stage_one_rest(
-    np_ref, p_ref, ax, ay, rkx, aky, gx, gy, edge, xnear, xflux, hold_ref, spec, ky_od, ky_ev,
-    sp_ref, x2, fk,
-):
-    s, kx_place, ky_place, x_up, y_up = place()
-    flow = Flow()
-    halo = Halo(ky_od, ky_ev, "ky", 1)
+def stage_one_middle(np_ref, p_y, ax, rkx, gx, edge, xnear, xflux, p_ref, fk):
+    flow = Flow()
     g = load(gx, 0)
     for e, j in enumerate(MIDDLE):
         store(fk, e, kx_flux(g, rkx, np_ref, 0, j))
 
     def one_kx(i, carry):
+        g = load(gx, 0)
+        for e, j in enumerate(MIDDLE):
+            n = load(np_ref, (i + 2) * BY + j)
+            total = x_change(flow, n, ax, i, j, edge, xnear, xflux)
+            upper = kx_flux(g, rkx, np_ref, i + 1, j)
+            lower = load(fk, e)
+            store(fk, e, upper)
+            p = each(lambda p, t, u, v: p - (t + (u - v)), load(p_y, i * BY + j), total, upper, lower)
+            store(p_ref, i * len(MIDDLE) + e, p)
+        return carry
+
+    loop(BX, one_kx, 4)
+
+
+def stage_one_rest(np_ref, p_ref, p_middle, aky, gy, hold_ref, spec, ky_od, ky_ev, sp_ref, x2):
+    flow = Flow()
+    halo = Halo(ky_od, ky_ev, "ky", 1)
+
+    def one_kx(i, carry):
         hold = each(lambda m: m == 1, load(hold_ref, 0))
-        g, gk = load(gx, 0), load(gy, 0)
+        gk = load(gy, 0)
         layers = ky_column(np_ref, halo, i)
         lower_y = ky_flux(gk, aky, layers, i, 0)
         last = [[], []]
         for j in range(BY):
-            n = layers[j + 2]
             if j in EDGES:
                 p = load(p_ref, i * len(EDGES) + EDGES.index(j))
             else:
-                e = MIDDLE.index(j)
-                total = space_change(flow, n, ax, ay, i, j, edge, xnear, xflux)
-                upper = kx_flux(g, rkx, np_ref, i + 1, j)
-                lower = load(fk, e)
-                store(fk, e, upper)
-                p = each(lambda n, t, u, v: n - (t + (u - v)), n, total, upper, lower)
+                p = load(p_middle, i * len(MIDDLE) + MIDDLE.index(j))
             upper_y = ky_flux(gk, aky, layers, i, j + 1)
-            v = each(
-                lambda m, p, u, v: jnp.where(m, spec[i * BY + j], p - (u - v)), hold, p, upper_y, lower_y
-            )
+            v = each(lambda m, p, u, v: jnp.where(m, spec[i * BY + j], p - (u - v)), hold, p, upper_y, lower_y)
             store(sp_ref, (i + 2) * BY + j, v)
             lower_y = upper_y
             for b in range(2):
@@ -546,17 +554,16 @@
 
 
 STEP = 4
-
-
-def send_out(buffer, out, sem, i):
-    @pl.when(i % STEP == STEP - 1)
-    def _():
-        flow = Flow()
-        rows = pl.ds(i - (STEP - 1), STEP)
-        for a in range(2):
-            for b in range(2):
-                x, y = flow.natural(a, b)
-                pltpu.make_async_copy(buffer.at[rows, :, 2 * a + b], out.at[rows, :, x, y], sem).start()
+INNER = range(2, BX - 2)
+
+
+def send_out(buffer, out, sem, first, rows, layers):
+    flow = Flow()
+    rows, layers = pl.ds(first, rows), pl.ds(layers[0], len(layers))
+    for a in range(2):
+        for b in range(2):
+            x, y = flow.natural(a, b)
+            pltpu.make_async_copy(buffer.at[:, :, 2 * a + b], out.at[rows, layers, x, y], sem).start()
 
 
 def stage_two_inner(np_ref, sp_ref, ax, ay, rkx, aky, gx, gy, edge, q_ref, fk):
@@ -574,7 +581,8 @@
         for j in range(BY):
             slab = i * BY + j
             n = layers[j + 2]
-            total = space_change(flow, n, ax, ay, i, j, edge, None, None)
+            total = x_change(flow, n, ax, i, j, edge, None, None)
+            total = each(lambda t, u: t + u, total, y_change(flow, n, ay, i, j))
             upper = kx_flux(g, rkx, sp_ref, i + 1, j)
             lower = load(fk, j)
             store(fk, j, upper)
@@ -605,16 +613,51 @@
     )
 
 
-def stage_two_outer(
-    q_in, ax, rkx, aky, gx, gy, halo_speed, hold_ref, spec, kx_od, kx_ev, x2, ky_od, ky_ev,
-    q_ref, out, xnear, xflux, done, sem,
-):
+def stage_two_x(q_in, ax, halo_speed, hold_ref, spec, x2, q_ref, out, xnear, xflux, done, sem):
     _, _, _, x_up, _ = place()
     flow = Flow()
     none = no_inflow(x_up)
     near = jnp.where(none, 0.0, x2[pl.ds(0, 2 * BX)])
     xnear[...] = 0.5 * near
     xflux[...] = (3.0 * near - jnp.where(none, 0.0, x2[pl.ds(2 * BX, 2 * BX)])) * (0.5 * halo_speed[...])
+    second = flow.rows == jnp.where(x_up, 1, 6)
+
+    def one_kx(i, inner):
+        hold = each(lambda m: m == 1, load(hold_ref, 0))
+        for j in range(BY):
+            slab = i * BY + j
+            q = load(q_ref, slab)
+            for b in range(2):
+                less = ax[slab * T + b] * row(xnear, i, j, b)
+                into = less + row(xflux, i, j, b)
+                q[0][b] = q[0][b] + jnp.where(
+                    flow.x_first, into, jnp.where(second, -pltpu.roll(less, flow.x_roll, 0), 0.0)
+                )
+            if inner and j in MIDDLE:
+                for a in range(2):
+                    for b in range(2):
+                        done[i - INNER[0], j - MIDDLE[0], 2 * a + b] = jnp.where(hold[a][b], spec[slab], q[a][b])
+            else:
+                for b in range(2):
+                    q_ref[slab * T + b] = q[0][b]
+
+    def several(n, carry):
+        first = INNER[0] + n * STEP
+        for k in range(STEP):
+            one_kx(first + k, True)
+        send_out(done.at[pl.ds(n * STEP, STEP)], out, sem, first, STEP, MIDDLE)
+        return carry
+
+    lax.fori_loop(0, len(INNER) // STEP, several, 0)
+    for i in (0, 1, BX - 2, BX - 1):
+        one_kx(i, False)
+    wait_all(done, sem)
+
+
+def stage_two_ends(
+    q_in, rkx, aky, gx, gy, hold_ref, spec, kx_od, kx_ev, ky_od, ky_ev, out_in,
+    q_ref, out, done, ends, sems,
+):
     kx_halo, ky_halo = Halo(kx_od, kx_ev, "kx", 2), Halo(ky_od, ky_ev, "ky", 1)
 
     def kx_ends(j, carry):
@@ -629,34 +672,41 @@
         return carry
 
     loop(BY, kx_ends, 4)
-    second = flow.rows == jnp.where(x_up, 1, 6)
-
-    def one_kx(i, carry):
+    hold = each(lambda m: m == 1, load(hold_ref, 0))
+    for e, i in enumerate((0, 1, BX - 2, BX - 1)):
+        for j in MIDDLE:
+            slab = i * BY + j
+            q = load(q_ref, slab)
+            for a in range(2):
+                for b in range(2):
+                    ends[e, j - MIDDLE[0], 2 * a + b] = jnp.where(hold[a][b], spec[slab], q[a][b])
+    send_out(ends.at[pl.ds(0, 2)], out, sems.at[0], 0, 2, MIDDLE)
+    send_out(ends.at[pl.ds(2, 2)], out, sems.at[0], BX - 2, 2, MIDDLE)
+
+    def one_kx(i):
         hold = each(lambda m: m == 1, load(hold_ref, 0))
         gk = load(gy, 0)
         speed = [load(aky, i * (BY + 1) + f) for f in (0, 1, BY - 1, BY)]
         low = [ky_halo.low(i * 2 + l) for l in range(2)]
         high = [ky_halo.high(i * 2 + l) for l in range(2)]
-        terms = dict(zip(EDGES, halo_terms(gk, speed[:2], speed[2:], low, high)))
-        for j in range(BY):
+        for e, (j, term) in enumerate(zip(EDGES, halo_terms(gk, speed[:2], speed[2:], low, high))):
             slab = i * BY + j
-            q = load(q_ref, slab)
-            if j in terms:
-                q = each(lambda q, t: q + t, q, terms[j])
-            for b in range(2):
-                less = ax[slab * T + b] * row(xnear, i, j, b)
-                into = less + row(xflux, i, j, b)
-                q[0][b] = q[0][b] + jnp.where(
-                    flow.x_first, into, jnp.where(second, -pltpu.roll(less, flow.x_roll, 0), 0.0)
-                )
+            q = each(lambda q, t: q + t, load(q_ref, slab), term)
             for a in range(2):
                 for b in range(2):
-                    done[i, j, 2 * a + b] = jnp.where(hold[a][b], spec[slab], q[a][b])
-        send_out(done, out, sem, i)
-        return carry
-
-    loop(BX, one_kx, 4)
-    wait_all(done, sem)
+                    done[i, e, 2 * a + b] = jnp.where(hold[a][b], spec[slab], q[a][b])
+
+    def several(n, carry):
+        for k in range(STEP):
+            one_kx(n * STEP + k)
+        rows = done.at[pl.ds(n * STEP, STEP)]
+        send_out(rows.at[:, pl.ds(0, 2)], out, sems.at[1], n * STEP, STEP, EDGES[:2])
+        send_out(rows.at[:, pl.ds(2, 2)], out, sems.at[1], n * STEP, STEP, EDGES[2:])
+        return carry
+
+    lax.fori_loop(0, BX // STEP, several, 0)
+    wait_all(ends, sems.at[0])
+    wait_all(done, sems.at[1])
 
 
 def call(kernel, outs, operands, spaces, out_spaces, scratch=(), alias=None, us=1, limit=LIMIT):
@@ -692,47 +742,47 @@
         return lax.ppermute(message, AXES, swaps(sizes, AXES.index(axis), 0, 0))
 
     sem = pltpu.SemaphoreType.DMA
-    np5, kx_od, kx_ev, x_od, x_ev, depth, mask, spectrum, ay = call(
+    np5, kx_od, kx_ev, ky_od, depth, mask, spectrum = call(
         first_messages,
-        (v(BX + 4, BY, T), v(2, BY, T), v(2, BY, T), v(4 * BX + 2), v(4 * BX + 2), pltpu.VMEM((BS, NY), jnp.int32),
-         pltpu.VMEM((BS, NY), jnp.int32), pltpu.VMEM((NKX, NKY), f32), v(slabs)),
+        (v(BX + 4, BY, T), v(2, BY, T), v(2, BY, T), v(BX, 2, T), pltpu.VMEM((BS, NY), jnp.int32),
+         pltpu.VMEM((BS, NY), jnp.int32), pltpu.VMEM((NKX, NKY), f32)),
         (action, depth_cm, inflow_mask, inflow),
         "hhhh",
-        "v" * 9,
-        [v(T), sem((6,))],
+        "v" * 7,
+        [sem((7,))],
         us=0,
         limit=FIRST_LIMIT,
     )
+    ky_od = swap_odd(ky_od, "ky", "kx").reshape(ky_tiles, 8, 128)
     kx_ev = swap_even(kx_ev, "kx").reshape(kx_tiles, 8, 128)
-    x_od = swap_odd(x_od, "space", "kx")
-    x_ev = swap_even(x_ev, "space")
     kx_od = swap_odd(kx_od, "kx", "space").reshape(kx_tiles, 8, 128)
-    np3, ky_od, ky_ev = call(
-        ky_messages,
-        (v(padded), v(BX, 2, T), v(BX, 2, T)),
-        (np5.reshape(padded, 8, 128), kx_ev),
-        "v" * 2,
+    np3, ky_ev, x_od, x_ev = call(
+        more_messages,
+        (v(padded), v(BX, 2, T), v(4 * BX + 2), v(4 * BX + 2)),
+        (np5.reshape(padded, 8, 128), depth, kx_ev),
         "v" * 3,
-        [sem((2,))],
+        "v" * 4,
+        [sem],
         alias={0: 0},
         us=0,
     )
-    ky_od = swap_odd(ky_od, "ky", "kx").reshape(ky_tiles, 8, 128)
+    x_od, x_ev = swap_odd(x_od, "space", "kx"), swap_even(x_ev, "space")
     ky_ev = swap_even(ky_ev, "ky").reshape(ky_tiles, 8, 128)
-    ax, rkx, aky, gy, heights, hold, spec = call(
+    ax, ay, rkx, aky, gy, heights, hold, spec = call(
         speeds,
-        (v(slabs), v((BX + 1) * BY * T), v(BX * (BY + 1) * T), v(T), pltpu.VMEM((BS, NY), f32),
+        (v(slabs), v(slabs), v((BX + 1) * BY * T), v(BX * (BY + 1) * T), v(T), pltpu.VMEM((BS, NY), f32),
          pltpu.VMEM((T, 8, 128), jnp.int32), v(BX * BY)),
         (depth, mask, spectrum),
         "vvv",
-        "v" * 7,
-        [v(2 * T)],
-        us=4,
-    )
+        "v" * 8,
+        [v(3 * T)],
+        us=3,
+    )
+    (p_y,) = call(stage_one_y, (v(slabs),), (np3, ay), "vv", "v", us=1)
     np3, part, gx, edge, halo_speed, xnear, xflux, ky2_od, ky2_ev = call(
         stage_one_edges,
         (v(padded), v(edge_slabs), v(T), v(2 * BX), v(2 * BX), v(2 * BX), v(2 * BX), v(ky_tiles), v(ky_tiles)),
-        (np3, ax, ay, rkx, aky, heights, hold, spec, kx_od, x_od, x_ev),
+        (np3, p_y, ax, rkx, aky, heights, hold, spec, kx_od, x_od, x_ev),
         "v" * 11,
         "v" * 9,
         [v(len(EDGES) * T), v(4)],
@@ -740,13 +790,21 @@
         us=0,
     )
     ky2_od, ky2_ev = swap_odd(ky2_od, "ky", "kx"), swap_even(ky2_ev, "ky")
+    (p_middle,) = call(
+        stage_one_middle,
+        (v(BX * len(MIDDLE) * T),),
+        (np3, p_y, ax, rkx, gx, edge, xnear, xflux),
+        "v" * 8,
+        "v",
+        [v(len(MIDDLE) * T)],
+        us=2,
+    )
     sp, x2 = call(
         stage_one_rest,
         (v(padded), v(4 * BX)),
-        (np3, part, ax, ay, rkx, aky, gx, gy, edge, xnear, xflux, hold, spec, ky_od, ky_ev),
-        "v" * 15,
+        (np3, part, p_middle, aky, gy, hold, spec, ky_od, ky_ev),
+        "v" * 9,
         "v" * 2,
-        [v(len(MIDDLE) * T)],
         us=0,
     )
     x2 = lax.ppermute(x2, AXES[:2], ring(sizes))
@@ -770,14 +828,24 @@
         [v(BY * T)],
         us=4,
     )
+    q, out = call(
+        stage_two_x,
+        (v(slabs), jax.ShapeDtypeStruct(action.shape, f32)),
+        (q, ax, halo_speed, hold, spec, x2),
+        "v" * 6,
+        "vh",
+        [v(2 * BX), v(2 * BX), v(len(INNER), len(MIDDLE), T), sem],
+        alias={0: 0},
+        us=2,
+    )
     _, out = call(
-        stage_two_outer,
+        stage_two_ends,
         (v(slabs), jax.ShapeDtypeStruct(action.shape, f32)),
-        (q, ax, rkx, aky, gx, gy, halo_speed, hold, spec, kx2_od, kx2_ev, x2, ky2_od, ky2_ev),
-        "v" * 14,
+        (q, rkx, aky, gx, gy, hold, spec, kx2_od, kx2_ev, ky2_od, ky2_ev, out),
+        "v" * 11 + "h",
         "vh",
-        [v(2 * BX), v(2 * BX), v(BX, BY, T), sem],
-        alias={0: 0},
+        [v(BX, len(EDGES), T), v(4, len(MIDDLE), T), sem((2,))],
+        alias={0: 0, 11: 1},
         us=0,
     )
     return out

time: 39.3 us -> 38.3 us (0.975)
  starting transfers between devices: 14.5 us -> 11 us
  Pallas kernels: 12.8 us -> 15.1 us
    ppermute x4, waiting for transfers between devices: 4.94 us -> 0.9 us  [swap_odd(): lax.ppermute(message, AXES, swaps(sizes, AXES.index(axis), 1, AXES.index(...]
    ppermute x1, waiting for transfers between devices: 0.01 us -> 3.69 us  [per_device(): x2 = lax.ppermute(x2, AXES[:2], ring(sizes))]
    pallas_call x8 -> x11, Pallas kernels: 12.8 us -> 15.1 us  [call(): pl.pallas_call(kernel, out_shape=tuple(outs), in_specs=[whole[c] for c in...]
    ppermute x1, starting transfers between devices: 4.04 us -> 1.98 us  [per_device(): x2 = lax.ppermute(x2, AXES[:2], ring(sizes))]
    ppermute x5, starting transfers between devices: 2.38 us -> 1.39 us  [swap_even(): return lax.ppermute(message, AXES, swaps(sizes, AXES.index(axis), 0, 0))]
    ppermute x4, starting transfers between devices: 7.97 us -> 7.47 us  [swap_odd(): lax.ppermute(message, AXES, swaps(sizes, AXES.index(axis), 1, AXES.index(...]
    ppermute x5, waiting for transfers between devices: 6.82 us -> 7.25 us  [swap_even(): return lax.ppermute(message, AXES, swaps(sizes, AXES.index(axis), 0, 0))]
  transfers between devices with their start and end apart: 11 -> 11, of which waited for: 4 -> 4; matrix products, arithmetic and copies ran while one was open for 0% -> 0% of each run, Pallas kernels for 23% -> 31%
where the time goes in v6:
time: 38.3 us; the launch traced here: 38.1 us
  Pallas kernels  15.1 us (39%)
  waiting for transfers between devices  11.8 us (31%)
  starting transfers between devices  11 us (29%)
    pallas_call x11, Pallas kernels, call(): pl.pallas_call(kernel, out_shape=tuple(outs), in_specs=[whole[c] for c in...  15.1 us
    ppermute x4, starting transfers between devices, swap_odd(): lax.ppermute(message, AXES, swaps(sizes, AXES.index(axis), 1, AXES.index(...  7.47 us
    ppermute x5, waiting for transfers between devices, swap_even(): return lax.ppermute(message, AXES, swaps(sizes, AXES.index(axis), 0, 0))  7.25 us
    ppermute x1, waiting for transfers between devices, per_device(): x2 = lax.ppermute(x2, AXES[:2], ring(sizes))  3.69 us
    ppermute x1, starting transfers between devices, per_device(): x2 = lax.ppermute(x2, AXES[:2], ring(sizes))  1.98 us
    ppermute x5, starting transfers between devices, swap_even(): return lax.ppermute(message, AXES, swaps(sizes, AXES.index(axis), 0, 0))  1.39 us
    ppermute x4, waiting for transfers between devices, swap_odd(): lax.ppermute(message, AXES, swaps(sizes, AXES.index(axis), 1, AXES.index(...  0.9 us
  transfers between devices with their start and end apart: 11, of which 4 were waited for; matrix products, arithmetic and copies ran while one was open for 0% of the time, Pallas kernels for 31%

profile of v6, /device:TPU:8, one launch (start us, length us, event | category | flops | bytes accessed | tf_op | source)
XLA Modules:
  0.0 38.1 jit_solution(6243171163300875103)
XLA Ops:
  0.0 1.7 %first_messages.1 = (f32[20,8,4,8,128]{4,3,2,1,0:T(8,128)S(1)}, f32[2,8,4,8,128]{4,3,2,1,0:T(8,128)S(1)}, f32[2,8,4,8,128]{4,3,2,1,0:T(8,128)S(1)}, f32[16,2,4,8...) custom-call(f32[16,8,16,256]{3,2,1,0:T(8,128)} %a_ref.1, ...), custom_call_target="tpu_custom_call" | custom-call | tf_op jit(solution)/shard_map/first_messages/pallas_call | solution.py:717
  1.7 0.1 collective-permute-start
  1.8 1.6 %collective-permute-start.1 = (f32[2,8,4,8,128]{4,3,2,1,0:T(8,128)S(1)}, f32[2,8,4,8,128]{4,3,2,1,0:T(8,128)S(1)}, u32[]{:S(2)}, u32[]{:S(2)}) collective-permute-start(f32[2,8,4,8,128]{4,3,2,1,0:T(8,128)S(1)} %get-tuple-element.54), channel_id=1, source_target_pairs={{0,32},{1,33},{2,34},{3,35},{4,36},{5,37},{6,38},{7,39},{8,16},{9,... | collective-permute-start | bytes 786440 | tf_op jit(solution)/shard_map/ppermute | solution.py:739
  3.4 3.9 %collective-permute-start.4 = (f32[16,2,4,8,128]{4,3,2,1,0:T(8,128)S(1)}, f32[16,2,4,8,128]{4,3,2,1,0:T(8,128)S(1)}, u32[]{:S(2)}, u32[]{:S(2)}) collective-permute-start(f32[16,2,4,8,128]{4,3,2,1,0:T(8,128)S(1)} %get-tuple-element.64), channel_id=1, source_target_pairs={{0,8},{1,2},{2,1},{3,4},{4,3},{5,6},{6,5},{7,15},{8,0},{9,10},{10,... | collective-permute-start | bytes 1572872 | tf_op jit(solution)/shard_map/ppermute | solution.py:739
  7.3 0.0 collective-permute-done
  7.3 0.2 more_messages.1
  7.6 1.6 %collective-permute-start.2 = (f32[66,8,128]{2,1,0:T(8,128)S(1)}, f32[66,8,128]{2,1,0:T(8,128)S(1)}, u32[]{:S(2)}, u32[]{:S(2)}) collective-permute-start(f32[66,8,128]{2,1,0:T(8,128)S(1)} %get-tuple-element.55), channel_id=1, source_target_pairs={{0,8},{1,9},{2,10},{3,11},{4,12},{5,13},{6,14},{7,15},{8,0},{9,1},... | collective-permute-start | bytes 811016 | tf_op jit(solution)/shard_map/ppermute | solution.py:739
  9.2 1.1 %collective-permute-start.3 = (f32[66,8,128]{2,1,0:T(8,128)S(1)}, f32[66,8,128]{2,1,0:T(8,128)S(1)}, u32[]{:S(2)}, u32[]{:S(2)}) collective-permute-start(f32[66,8,128]{2,1,0:T(8,128)S(1)} %get-tuple-element.56), channel_id=1, source_target_pairs={{0,32},{1,33},{2,34},{3,35},{4,36},{5,37},{6,38},{7,39},{8,40},{9,... | collective-permute-start | bytes 811016 | tf_op jit(solution)/shard_map/ppermute | solution.py:742
  10.4 0.0 collective-permute-start.5
  10.4 2.9 %speeds.1 = (f32[512,8,128]{2,1,0:T(8,128)S(1)}, f32[512,8,128]{2,1,0:T(8,128)S(1)}, f32[544,8,128]{2,1,0:T(8,128)S(1)}, f32[576,8,128]{2,1,0:T(8,128)S(1)}, f32...) custom-call(s32[16,256]{1,0:T(8,128)S(1)} %get-tuple-element.42.depth, ...), custom_call_target="tpu_custom_call" | custom-call | flops 3000000000 | tf_op jit(solution)/shard_map/speeds/pallas_call | solution.py:717
  13.3 2.1 %stage_one_y.1.p_y = f32[512,8,128]{2,1,0:T(8,128)S(1)} custom-call(f32[640,8,128]{2,1,0:T(8,128)S(1)} %get-tuple-element.44.np_ref.np_in, f32[512,8,128]{2,1,0:T(8,128)S(1)} %get-tuple-element.47.ay), custom_call_target="tpu_custom_call" | custom-call | flops 1000000000 | tf_op jit(solution)/shard_map/stage_one_y/pallas_call | solution.py:717
  15.4 0.0 collective-permute-done.1
  15.4 0.0 collective-permute-done.2.x_od
  15.4 3.1 %collective-permute-done.3.x_ev = f32[66,8,128]{2,1,0:T(8,128)S(1)} collective-permute-done((f32[66,8,128]{2,1,0:T(8,128)S(1)}, f32[66,8,128]{2,1,0:T(8,128)S(1)}, u32[]{:S(2)}, u32[]{:S(2)}) %collective-permute-start.3) | collective-permute-done | bytes 270368 | tf_op jit(solution)/shard_map/ppermute | solution.py:742
  18.5 1.1 %stage_one_edges.1 = (f32[640,8,128]{2,1,0:T(8,128)S(1)}, f32[256,8,128]{2,1,0:T(8,128)S(1)}, f32[4,8,128]{2,1,0:T(8,128)S(1)}, f32[32,8,128]{2,1,0:T(8,128)S(1)...) custom-call(f32[640,8,128]{2,1,0:T(8,128)S(1)} %get-tuple-element.44, ...), custom_call_target="tpu_custom_call", output_to_operand_aliasing={{0}: (0, {})} | custom-call | tf_op jit(solution)/shard_map/stage_one_edges/pallas_call | solution.py:717
  19.7 0.4 collective-permute-start.9
  20.1 0.0 collective-permute-start.10
  20.1 0.6 %stage_one_middle.1.p_middle = f32[256,8,128]{2,1,0:T(8,128)S(1)} custom-call(f32[640,8,128]{2,1,0:T(8,128)S(1)} %get-tuple-element.57.np_ref, f32[512,8,128]{2,1,0:T(8,128)S(1)} %stage_one_y.1.p_y, f32[512,8,128]{2,1,0:T(8,128)S(1)} %get-tuple-element.48.ax, f32[544,8,128]{2,1,0:T(8,128)S(1)} %get-tuple-element.49.rkx, ...), custom_call_target="tpu_custom_call" | custom-call | flops 2000000000 | tf_op jit(solution)/shard_map/stage_one_middle/pallas_call | solution.py:717
  20.7 0.0 collective-permute-done.4
  20.7 4.1 %collective-permute-done.5 = f32[16,2,4,8,128]{4,3,2,1,0:T(8,128)S(1)} collective-permute-done((f32[16,2,4,8,128]{4,3,2,1,0:T(8,128)S(1)}, f32[16,2,4,8,128]{4,3,2,1,0:T(8,128)S(1)}, u32[]{:S(2)}, u32[]{:S(2)}) %collective-permute-start.5) | collective-permute-done | bytes 524320 | tf_op jit(solution)/shard_map/ppermute | solution.py:742
  24.8 0.9 %stage_one_rest.1 = (f32[640,8,128]{2,1,0:T(8,128)S(1)}, f32[64,8,128]{2,1,0:T(8,128)S(1)}) custom-call(f32[640,8,128]{2,1,0:T(8,128)S(1)} %get-tuple-element.57.np_ref, f32[256,8,128]{2,1,0:T(8,128)S(1)} %get-tuple-element.58.p_ref, f32[256,8,128]{2,1,0:T(8,128)S(1)} %stage_one_middle.1.p_middle, f32[576,8,128]{2,1,0:T(8,128)S(1)} %get-tuple-element.50.aky, ...), custom_call_target="tpu_custom_call" | custom-call | tf_op jit(solution)/shard_map/stage_one_rest/pallas_call | solution.py:717
  25.8 2.0 %collective-permute-start.6 = (f32[64,8,128]{2,1,0:T(8,128)S(1)}, f32[64,8,128]{2,1,0:T(8,128)S(1)}, u32[]{:S(2)}, u32[]{:S(2)}) collective-permute-start(f32[64,8,128]{2,1,0:T(8,128)S(1)} %get-tuple-element.69), channel_id=1, source_target_pairs={{0,96},{8,104},{16,48},{24,56},{32,0},{40,8},{48,80},{56,88},{64,3... | collective-permute-start | bytes 786440 | tf_op jit(solution)/shard_map/ppermute | solution.py:810
  27.7 0.1 kx_messages.1
  27.8 0.2 collective-permute-start.7
  28.0 0.1 collective-permute-start.8
  28.2 2.9 %stage_two_inner.1.q_in = f32[512,8,128]{2,1,0:T(8,128)S(1)} custom-call(f32[640,8,128]{2,1,0:T(8,128)S(1)} %get-tuple-element.57.np_ref, f32[640,8,128]{2,1,0:T(8,128)S(1)} %get-tuple-element.67.sp_ref, f32[512,8,128]{2,1,0:T(8,128)S(1)} %get-tuple-element.48.ax, f32[512,8,128]{2,1,0:T(8,128)S(1)} %get-tuple-element.47.ay, ...), custom_call_target="tpu_custom_call" | custom-call | flops 4000000000 | tf_op jit(solution)/shard_map/stage_two_inner/pallas_call | solution.py:717
  31.1 3.7 %collective-permute-done.6.x2 = f32[64,8,128]{2,1,0:T(8,128)S(1)} collective-permute-done((f32[64,8,128]{2,1,0:T(8,128)S(1)}, f32[64,8,128]{2,1,0:T(8,128)S(1)}, u32[]{:S(2)}, u32[]{:S(2)}) %collective-permute-start.6) | collective-permute-done | bytes 262176 | tf_op jit(solution)/shard_map/ppermute | solution.py:810
  34.8 1.0 %stage_two_x.1 = (f32[512,8,128]{2,1,0:T(8,128)S(1)}, f32[16,8,16,256]{3,2,1,0:T(8,128)}) custom-call(f32[512,8,128]{2,1,0:T(8,128)S(1)} %stage_two_inner.1.q_in, f32[512,8,128]{2,1,0:T(8,128)S(1)} %get-tuple-element.48.ax, f32[32,8,128]{2,1,0:T(8,128)S(1)} %get-tuple-element.68.halo_speed, ...), custom_call_target="tpu_custom_call", output_to_operand_aliasing={{0}: (0, {})} | custom-call | flops 2000000000 | tf_op jit(solution)/shard_map/stage_two_x/pallas_call | solution.py:717
  35.7 0.0 collective-permute-done.7.kx_od
  35.8 0.0 collective-permute-done.8.kx_ev
  35.8 0.9 %collective-permute-done.9.ky_od = f32[128,8,128]{2,1,0:T(8,128)S(1)} collective-permute-done((f32[128,8,128]{2,1,0:T(8,128)S(1)}, f32[128,8,128]{2,1,0:T(8,128)S(1)}, u32[]{:S(2)}, u32[]{:S(2)}) %collective-permute-start.9) | collective-permute-done | bytes 524320 | tf_op jit(solution)/shard_map/ppermute | solution.py:739
  36.7 0.0 collective-permute-done.10.ky_ev
  36.7 1.5 %stage_two_ends.1 = (f32[512,8,128]{2,1,0:T(8,128)S(1)}, f32[16,8,16,256]{3,2,1,0:T(8,128)}) custom-call(f32[512,8,128]{2,1,0:T(8,128)S(1)} %get-tuple-element.70.q_in, f32[544,8,128]{2,1,0:T(8,128)S(1)} %get-tuple-element.49.rkx, f32[576,8,128]{2,1,0:T(8,128)S(1)} %get-tuple-element.50.aky, ...), custom_call_target="tpu_custom_call", output_to_operand_aliasing={{0}: (0, {}), {1}: (11, {})} | custom-call | tf_op jit(solution)/shard_map/stage_two_ends/pallas_call | solution.py:717
Async XLA Ops:
  1.7 5.6 %collective-permute-start = (f32[2,8,4,8,128]{4,3,2,1,0:T(8,128)S(1)}, f32[2,8,4,8,128]{4,3,2,1,0:T(8,128)S(1)}, u32[]{:S(2)}, u32[]{:S(2)}) collective-permute-start(f32[2,8,4,8,128]{4,3,2,1,0:T(8,128)S(1)} %get-tuple-element.43), channel_id=1, source_target_pairs={{0,8},{1,9},{2,10},{3,11},{4,12},{5,13},{6,14},{7,15},{8,0},{9,1},... | collective-permute-start | bytes 786440 | tf_op jit(solution)/shard_map/ppermute | solution.py:742
  1.8 13.6 %collective-permute-start.1 = (f32[2,8,4,8,128]{4,3,2,1,0:T(8,128)S(1)}, f32[2,8,4,8,128]{4,3,2,1,0:T(8,128)S(1)}, u32[]{:S(2)}, u32[]{:S(2)}) collective-permute-start(f32[2,8,4,8,128]{4,3,2,1,0:T(8,128)S(1)} %get-tuple-element.54), channel_id=1, source_target_pairs={{0,32},{1,33},{2,34},{3,35},{4,36},{5,37},{6,38},{7,39},{8,16},{9,... | collective-permute-start | bytes 786440 | tf_op jit(solution)/shard_map/ppermute | solution.py:739
  3.4 17.3 %collective-permute-start.4 = (f32[16,2,4,8,128]{4,3,2,1,0:T(8,128)S(1)}, f32[16,2,4,8,128]{4,3,2,1,0:T(8,128)S(1)}, u32[]{:S(2)}, u32[]{:S(2)}) collective-permute-start(f32[16,2,4,8,128]{4,3,2,1,0:T(8,128)S(1)} %get-tuple-element.64), channel_id=1, source_target_pairs={{0,8},{1,2},{2,1},{3,4},{4,3},{5,6},{6,5},{7,15},{8,0},{9,10},{10,... | collective-permute-start | bytes 1572872 | tf_op jit(solution)/shard_map/ppermute | solution.py:739
  7.6 7.8 %collective-permute-start.2 = (f32[66,8,128]{2,1,0:T(8,128)S(1)}, f32[66,8,128]{2,1,0:T(8,128)S(1)}, u32[]{:S(2)}, u32[]{:S(2)}) collective-permute-start(f32[66,8,128]{2,1,0:T(8,128)S(1)} %get-tuple-element.55), channel_id=1, source_target_pairs={{0,8},{1,9},{2,10},{3,11},{4,12},{5,13},{6,14},{7,15},{8,0},{9,1},... | collective-permute-start | bytes 811016 | tf_op jit(solution)/shard_map/ppermute | solution.py:739
  9.2 9.3 %collective-permute-start.3 = (f32[66,8,128]{2,1,0:T(8,128)S(1)}, f32[66,8,128]{2,1,0:T(8,128)S(1)}, u32[]{:S(2)}, u32[]{:S(2)}) collective-permute-start(f32[66,8,128]{2,1,0:T(8,128)S(1)} %get-tuple-element.56), channel_id=1, source_target_pairs={{0,32},{1,33},{2,34},{3,35},{4,36},{5,37},{6,38},{7,39},{8,40},{9,... | collective-permute-start | bytes 811016 | tf_op jit(solution)/shard_map/ppermute | solution.py:742
  10.4 14.5 %collective-permute-start.5 = (f32[16,2,4,8,128]{4,3,2,1,0:T(8,128)S(1)}, f32[16,2,4,8,128]{4,3,2,1,0:T(8,128)S(1)}, u32[]{:S(2)}, u32[]{:S(2)}) collective-permute-start(f32[16,2,4,8,128]{4,3,2,1,0:T(8,128)S(1)} %get-tuple-element.65), channel_id=1, source_target_pairs={{0,1},{1,0},{2,3},{3,2},{4,5},{5,4},{6,7},{7,6},{8,9},{9,8},{10,11... | collective-permute-start | bytes 1572872 | tf_op jit(solution)/shard_map/ppermute | solution.py:742
  19.7 17.0 %collective-permute-start.9 = (f32[128,8,128]{2,1,0:T(8,128)S(1)}, f32[128,8,128]{2,1,0:T(8,128)S(1)}, u32[]{:S(2)}, u32[]{:S(2)}) collective-permute-start(f32[128,8,128]{2,1,0:T(8,128)S(1)} %get-tuple-element.73), channel_id=1, source_target_pairs={{0,8},{1,2},{2,1},{3,4},{4,3},{5,6},{6,5},{7,15},{8,0},{9,10},{10,... | collective-permute-start | bytes 1572872 | tf_op jit(solution)/shard_map/ppermute | solution.py:739
  20.1 16.6 %collective-permute-start.10 = (f32[128,8,128]{2,1,0:T(8,128)S(1)}, f32[128,8,128]{2,1,0:T(8,128)S(1)}, u32[]{:S(2)}, u32[]{:S(2)}) collective-permute-start(f32[128,8,128]{2,1,0:T(8,128)S(1)} %get-tuple-element.74), channel_id=1, source_target_pairs={{0,1},{1,0},{2,3},{3,2},{4,5},{5,4},{6,7},{7,6},{8,9},{9,8},{10,11... | collective-permute-start | bytes 1572872 | tf_op jit(solution)/shard_map/ppermute | solution.py:742
  25.8 9.0 %collective-permute-start.6 = (f32[64,8,128]{2,1,0:T(8,128)S(1)}, f32[64,8,128]{2,1,0:T(8,128)S(1)}, u32[]{:S(2)}, u32[]{:S(2)}) collective-permute-start(f32[64,8,128]{2,1,0:T(8,128)S(1)} %get-tuple-element.69), channel_id=1, source_target_pairs={{0,96},{8,104},{16,48},{24,56},{32,0},{40,8},{48,80},{56,88},{64,3... | collective-permute-start | bytes 786440 | tf_op jit(solution)/shard_map/ppermute | solution.py:810
  27.8 7.9 %collective-permute-start.7 = (f32[64,8,128]{2,1,0:T(8,128)S(1)}, f32[64,8,128]{2,1,0:T(8,128)S(1)}, u32[]{:S(2)}, u32[]{:S(2)}) collective-permute-start(f32[64,8,128]{2,1,0:T(8,128)S(1)} %get-tuple-element.71), channel_id=1, source_target_pairs={{0,32},{1,33},{2,34},{3,35},{4,36},{5,37},{6,38},{7,39},{8,16},{9,... | collective-permute-start | bytes 786440 | tf_op jit(solution)/shard_map/ppermute | solution.py:821
  28.0 7.7 %collective-permute-start.8 = (f32[64,8,128]{2,1,0:T(8,128)S(1)}, f32[64,8,128]{2,1,0:T(8,128)S(1)}, u32[]{:S(2)}, u32[]{:S(2)}) collective-permute-start(f32[64,8,128]{2,1,0:T(8,128)S(1)} %get-tuple-element.72), channel_id=1, source_target_pairs={{0,8},{1,9},{2,10},{3,11},{4,12},{5,13},{6,14},{7,15},{8,0},{9,1},... | collective-permute-start | bytes 786440 | tf_op jit(solution)/shard_map/ppermute | solution.py:742

commit v7 on v6

--- a/solution.py
+++ b/solution.py
@@ -654,11 +654,8 @@
     wait_all(done, sem)
 
 
-def stage_two_ends(
-    q_in, rkx, aky, gx, gy, hold_ref, spec, kx_od, kx_ev, ky_od, ky_ev, out_in,
-    q_ref, out, done, ends, sems,
-):
-    kx_halo, ky_halo = Halo(kx_od, kx_ev, "kx", 2), Halo(ky_od, ky_ev, "ky", 1)
+def stage_two_kx(q_in, rkx, gx, kx_od, kx_ev, q_ref):
+    kx_halo = Halo(kx_od, kx_ev, "kx", 2)
 
     def kx_ends(j, carry):
         g = load(gx, 0)
@@ -672,6 +669,10 @@
         return carry
 
     loop(BY, kx_ends, 4)
+
+
+def stage_two_ky(q_ref, aky, gy, hold_ref, spec, ky_od, ky_ev, out_in, out, done, ends, sems):
+    ky_halo = Halo(ky_od, ky_ev, "ky", 1)
     hold = each(lambda m: m == 1, load(hold_ref, 0))
     for e, i in enumerate((0, 1, BX - 2, BX - 1)):
         for j in MIDDLE:
@@ -838,14 +839,23 @@
         alias={0: 0},
         us=2,
     )
-    _, out = call(
-        stage_two_ends,
-        (v(slabs), jax.ShapeDtypeStruct(action.shape, f32)),
-        (q, rkx, aky, gx, gy, hold, spec, kx2_od, kx2_ev, ky2_od, ky2_ev, out),
-        "v" * 11 + "h",
-        "vh",
+    (q,) = call(
+        stage_two_kx,
+        (v(slabs),),
+        (q, rkx, gx, kx2_od, kx2_ev),
+        "v" * 5,
+        "v",
+        alias={0: 0},
+        us=1,
+    )
+    (out,) = call(
+        stage_two_ky,
+        (jax.ShapeDtypeStruct(action.shape, f32),),
+        (q, aky, gy, hold, spec, ky2_od, ky2_ev, out),
+        "v" * 7 + "h",
+        "h",
         [v(BX, len(EDGES), T), v(4, len(MIDDLE), T), sem((2,))],
-        alias={0: 0, 11: 1},
+        alias={7: 0},
         us=0,
     )
     return out

time: 38.3 us -> 38.1 us (level)
    pallas_call x11 -> x12, Pallas kernels: 15.1 us -> 15.2 us  [call(): pl.pallas_call(kernel, out_shape=tuple(outs), in_specs=[whole[c] for c in...]
  transfers between devices with their start and end apart: 11 -> 11, of which waited for: 4 -> 4; matrix products, arithmetic and copies ran while one was open for 0% -> 0% of each run, Pallas kernels for 31% -> 32%
where the time goes in v7:
time: 38.1 us; the launch traced here: 37.9 us
  Pallas kernels  15.2 us (40%)
  waiting for transfers between devices  11.6 us (30%)
  starting transfers between devices  11 us (29%)
    pallas_call x12, Pallas kernels, call(): pl.pallas_call(kernel, out_shape=tuple(outs), in_specs=[whole[c] for c in...  15.2 us
    ppermute x4, starting transfers between devices, swap_odd(): lax.ppermute(message, AXES, swaps(sizes, AXES.index(axis), 1, AXES.index(...  7.47 us
    ppermute x5, waiting for transfers between devices, swap_even(): return lax.ppermute(message, AXES, swaps(sizes, AXES.index(axis), 0, 0))  7.25 us
    ppermute x1, waiting for transfers between devices, per_device(): x2 = lax.ppermute(x2, AXES[:2], ring(sizes))  3.69 us
    ppermute x1, starting transfers between devices, per_device(): x2 = lax.ppermute(x2, AXES[:2], ring(sizes))  1.98 us
    ppermute x5, starting transfers between devices, swap_even(): return lax.ppermute(message, AXES, swaps(sizes, AXES.index(axis), 0, 0))  1.39 us
  transfers between devices with their start and end apart: 11, of which 4 were waited for; matrix products, arithmetic and copies ran while one was open for 0% of the time, Pallas kernels for 32%

profile of v7, /device:TPU:8, one launch (start us, length us, event | category | flops | bytes accessed | tf_op | source)
XLA Modules:
  0.0 37.9 jit_solution(17841840031375021279)
XLA Ops:
  0.0 1.7 %first_messages.1 = (f32[20,8,4,8,128]{4,3,2,1,0:T(8,128)S(1)}, f32[2,8,4,8,128]{4,3,2,1,0:T(8,128)S(1)}, f32[2,8,4,8,128]{4,3,2,1,0:T(8,128)S(1)}, f32[16,2,4,8...) custom-call(f32[16,8,16,256]{3,2,1,0:T(8,128)} %a_ref.1, ...), custom_call_target="tpu_custom_call" | custom-call | tf_op jit(solution)/shard_map/first_messages/pallas_call | solution.py:718
  1.7 0.1 collective-permute-start
  1.8 1.6 %collective-permute-start.1 = (f32[2,8,4,8,128]{4,3,2,1,0:T(8,128)S(1)}, f32[2,8,4,8,128]{4,3,2,1,0:T(8,128)S(1)}, u32[]{:S(2)}, u32[]{:S(2)}) collective-permute-start(f32[2,8,4,8,128]{4,3,2,1,0:T(8,128)S(1)} %get-tuple-element.53), channel_id=1, source_target_pairs={{0,32},{1,33},{2,34},{3,35},{4,36},{5,37},{6,38},{7,39},{8,16},{9,... | collective-permute-start | bytes 786440 | tf_op jit(solution)/shard_map/ppermute | solution.py:740
  3.4 3.9 %collective-permute-start.4 = (f32[16,2,4,8,128]{4,3,2,1,0:T(8,128)S(1)}, f32[16,2,4,8,128]{4,3,2,1,0:T(8,128)S(1)}, u32[]{:S(2)}, u32[]{:S(2)}) collective-permute-start(f32[16,2,4,8,128]{4,3,2,1,0:T(8,128)S(1)} %get-tuple-element.63), channel_id=1, source_target_pairs={{0,8},{1,2},{2,1},{3,4},{4,3},{5,6},{6,5},{7,15},{8,0},{9,10},{10,... | collective-permute-start | bytes 1572872 | tf_op jit(solution)/shard_map/ppermute | solution.py:740
  7.3 0.0 collective-permute-done
  7.3 0.2 more_messages.1
  7.6 1.6 %collective-permute-start.2 = (f32[66,8,128]{2,1,0:T(8,128)S(1)}, f32[66,8,128]{2,1,0:T(8,128)S(1)}, u32[]{:S(2)}, u32[]{:S(2)}) collective-permute-start(f32[66,8,128]{2,1,0:T(8,128)S(1)} %get-tuple-element.54), channel_id=1, source_target_pairs={{0,8},{1,9},{2,10},{3,11},{4,12},{5,13},{6,14},{7,15},{8,0},{9,1},... | collective-permute-start | bytes 811016 | tf_op jit(solution)/shard_map/ppermute | solution.py:740
  9.2 1.1 %collective-permute-start.3 = (f32[66,8,128]{2,1,0:T(8,128)S(1)}, f32[66,8,128]{2,1,0:T(8,128)S(1)}, u32[]{:S(2)}, u32[]{:S(2)}) collective-permute-start(f32[66,8,128]{2,1,0:T(8,128)S(1)} %get-tuple-element.55), channel_id=1, source_target_pairs={{0,32},{1,33},{2,34},{3,35},{4,36},{5,37},{6,38},{7,39},{8,40},{9,... | collective-permute-start | bytes 811016 | tf_op jit(solution)/shard_map/ppermute | solution.py:743
  10.4 0.0 collective-permute-start.5
  10.4 2.9 %speeds.1 = (f32[512,8,128]{2,1,0:T(8,128)S(1)}, f32[512,8,128]{2,1,0:T(8,128)S(1)}, f32[544,8,128]{2,1,0:T(8,128)S(1)}, f32[576,8,128]{2,1,0:T(8,128)S(1)}, f32...) custom-call(s32[16,256]{1,0:T(8,128)S(1)} %get-tuple-element.41.depth, ...), custom_call_target="tpu_custom_call" | custom-call | flops 3000000000 | tf_op jit(solution)/shard_map/speeds/pallas_call | solution.py:718
  13.3 2.1 %stage_one_y.1.p_y = f32[512,8,128]{2,1,0:T(8,128)S(1)} custom-call(f32[640,8,128]{2,1,0:T(8,128)S(1)} %get-tuple-element.43.np_ref.np_in, f32[512,8,128]{2,1,0:T(8,128)S(1)} %get-tuple-element.46.ay), custom_call_target="tpu_custom_call" | custom-call | flops 1000000000 | tf_op jit(solution)/shard_map/stage_one_y/pallas_call | solution.py:718
  15.4 0.0 collective-permute-done.1
  15.4 0.0 collective-permute-done.2.x_od
  15.4 3.1 %collective-permute-done.3.x_ev = f32[66,8,128]{2,1,0:T(8,128)S(1)} collective-permute-done((f32[66,8,128]{2,1,0:T(8,128)S(1)}, f32[66,8,128]{2,1,0:T(8,128)S(1)}, u32[]{:S(2)}, u32[]{:S(2)}) %collective-permute-start.3) | collective-permute-done | bytes 270368 | tf_op jit(solution)/shard_map/ppermute | solution.py:743
  18.5 1.1 %stage_one_edges.1 = (f32[640,8,128]{2,1,0:T(8,128)S(1)}, f32[256,8,128]{2,1,0:T(8,128)S(1)}, f32[4,8,128]{2,1,0:T(8,128)S(1)}, f32[32,8,128]{2,1,0:T(8,128)S(1)...) custom-call(f32[640,8,128]{2,1,0:T(8,128)S(1)} %get-tuple-element.43, ...), custom_call_target="tpu_custom_call", output_to_operand_aliasing={{0}: (0, {})} | custom-call | tf_op jit(solution)/shard_map/stage_one_edges/pallas_call | solution.py:718
  19.7 0.4 collective-permute-start.9
  20.1 0.0 collective-permute-start.10
  20.1 0.6 %stage_one_middle.1.p_middle = f32[256,8,128]{2,1,0:T(8,128)S(1)} custom-call(f32[640,8,128]{2,1,0:T(8,128)S(1)} %get-tuple-element.56.np_ref, f32[512,8,128]{2,1,0:T(8,128)S(1)} %stage_one_y.1.p_y, f32[512,8,128]{2,1,0:T(8,128)S(1)} %get-tuple-element.47.ax, f32[544,8,128]{2,1,0:T(8,128)S(1)} %get-tuple-element.48.rkx, ...), custom_call_target="tpu_custom_call" | custom-call | flops 2000000000 | tf_op jit(solution)/shard_map/stage_one_middle/pallas_call | solution.py:718
  20.7 0.0 collective-permute-done.4
  20.7 4.1 %collective-permute-done.5 = f32[16,2,4,8,128]{4,3,2,1,0:T(8,128)S(1)} collective-permute-done((f32[16,2,4,8,128]{4,3,2,1,0:T(8,128)S(1)}, f32[16,2,4,8,128]{4,3,2,1,0:T(8,128)S(1)}, u32[]{:S(2)}, u32[]{:S(2)}) %collective-permute-start.5) | collective-permute-done | bytes 524320 | tf_op jit(solution)/shard_map/ppermute | solution.py:743
  24.8 0.9 %stage_one_rest.1 = (f32[640,8,128]{2,1,0:T(8,128)S(1)}, f32[64,8,128]{2,1,0:T(8,128)S(1)}) custom-call(f32[640,8,128]{2,1,0:T(8,128)S(1)} %get-tuple-element.56.np_ref, f32[256,8,128]{2,1,0:T(8,128)S(1)} %get-tuple-element.57.p_ref, f32[256,8,128]{2,1,0:T(8,128)S(1)} %stage_one_middle.1.p_middle, f32[576,8,128]{2,1,0:T(8,128)S(1)} %get-tuple-element.49.aky, ...), custom_call_target="tpu_custom_call" | custom-call | tf_op jit(solution)/shard_map/stage_one_rest/pallas_call | solution.py:718
  25.8 2.0 %collective-permute-start.6 = (f32[64,8,128]{2,1,0:T(8,128)S(1)}, f32[64,8,128]{2,1,0:T(8,128)S(1)}, u32[]{:S(2)}, u32[]{:S(2)}) collective-permute-start(f32[64,8,128]{2,1,0:T(8,128)S(1)} %get-tuple-element.68), channel_id=1, source_target_pairs={{0,96},{8,104},{16,48},{24,56},{32,0},{40,8},{48,80},{56,88},{64,3... | collective-permute-start | bytes 786440 | tf_op jit(solution)/shard_map/ppermute | solution.py:811
  27.7 0.1 kx_messages.1
  27.8 0.2 collective-permute-start.7
  28.0 0.1 collective-permute-start.8
  28.2 2.9 %stage_two_inner.1.q_in = f32[512,8,128]{2,1,0:T(8,128)S(1)} custom-call(f32[640,8,128]{2,1,0:T(8,128)S(1)} %get-tuple-element.56.np_ref, f32[640,8,128]{2,1,0:T(8,128)S(1)} %get-tuple-element.66.sp_ref, f32[512,8,128]{2,1,0:T(8,128)S(1)} %get-tuple-element.47.ax, f32[512,8,128]{2,1,0:T(8,128)S(1)} %get-tuple-element.46.ay, ...), custom_call_target="tpu_custom_call" | custom-call | flops 4000000000 | tf_op jit(solution)/shard_map/stage_two_inner/pallas_call | solution.py:718
  31.1 3.7 %collective-permute-done.6.x2 = f32[64,8,128]{2,1,0:T(8,128)S(1)} collective-permute-done((f32[64,8,128]{2,1,0:T(8,128)S(1)}, f32[64,8,128]{2,1,0:T(8,128)S(1)}, u32[]{:S(2)}, u32[]{:S(2)}) %collective-permute-start.6) | collective-permute-done | bytes 262176 | tf_op jit(solution)/shard_map/ppermute | solution.py:811
  34.8 1.0 %stage_two_x.1 = (f32[512,8,128]{2,1,0:T(8,128)S(1)}, f32[16,8,16,256]{3,2,1,0:T(8,128)}) custom-call(f32[512,8,128]{2,1,0:T(8,128)S(1)} %stage_two_inner.1.q_in, f32[512,8,128]{2,1,0:T(8,128)S(1)} %get-tuple-element.47.ax, f32[32,8,128]{2,1,0:T(8,128)S(1)} %get-tuple-element.67.halo_speed, ...), custom_call_target="tpu_custom_call", output_to_operand_aliasing={{0}: (0, {})} | custom-call | flops 2000000000 | tf_op jit(solution)/shard_map/stage_two_x/pallas_call | solution.py:718
  35.7 0.0 collective-permute-done.7.kx_od
  35.8 0.0 collective-permute-done.8.kx_ev
  35.8 0.2 stage_two_kx.1.q_ref
  36.0 0.7 %collective-permute-done.9.ky_od = f32[128,8,128]{2,1,0:T(8,128)S(1)} collective-permute-done((f32[128,8,128]{2,1,0:T(8,128)S(1)}, f32[128,8,128]{2,1,0:T(8,128)S(1)}, u32[]{:S(2)}, u32[]{:S(2)}) %collective-permute-start.9) | collective-permute-done | bytes 524320 | tf_op jit(solution)/shard_map/ppermute | solution.py:740
  36.7 0.0 collective-permute-done.10.ky_ev
  36.7 1.3 %stage_two_ky.1 = f32[16,8,16,256]{3,2,1,0:T(8,128)} custom-call(f32[512,8,128]{2,1,0:T(8,128)S(1)} %stage_two_kx.1.q_ref, f32[576,8,128]{2,1,0:T(8,128)S(1)} %get-tuple-element.49.aky, f32[4,8,128]{2,1,0:T(8,128)S(1)} %get-tuple-element.62.gy, s32[4,8,128]{2,1,0:T(8,128)S(1)} %get-tuple-element.51.hold_ref, ...), custom_call_target="tpu_custom_call", output_to_operand_aliasing={{}: (7, {})} | custom-call | tf_op jit(solution)/shard_map/stage_two_ky/pallas_call | solution.py:718
Async XLA Ops:
  1.7 5.6 %collective-permute-start = (f32[2,8,4,8,128]{4,3,2,1,0:T(8,128)S(1)}, f32[2,8,4,8,128]{4,3,2,1,0:T(8,128)S(1)}, u32[]{:S(2)}, u32[]{:S(2)}) collective-permute-start(f32[2,8,4,8,128]{4,3,2,1,0:T(8,128)S(1)} %get-tuple-element.42), channel_id=1, source_target_pairs={{0,8},{1,9},{2,10},{3,11},{4,12},{5,13},{6,14},{7,15},{8,0},{9,1},... | collective-permute-start | bytes 786440 | tf_op jit(solution)/shard_map/ppermute | solution.py:743
  1.8 13.6 %collective-permute-start.1 = (f32[2,8,4,8,128]{4,3,2,1,0:T(8,128)S(1)}, f32[2,8,4,8,128]{4,3,2,1,0:T(8,128)S(1)}, u32[]{:S(2)}, u32[]{:S(2)}) collective-permute-start(f32[2,8,4,8,128]{4,3,2,1,0:T(8,128)S(1)} %get-tuple-element.53), channel_id=1, source_target_pairs={{0,32},{1,33},{2,34},{3,35},{4,36},{5,37},{6,38},{7,39},{8,16},{9,... | collective-permute-start | bytes 786440 | tf_op jit(solution)/shard_map/ppermute | solution.py:740
  3.4 17.3 %collective-permute-start.4 = (f32[16,2,4,8,128]{4,3,2,1,0:T(8,128)S(1)}, f32[16,2,4,8,128]{4,3,2,1,0:T(8,128)S(1)}, u32[]{:S(2)}, u32[]{:S(2)}) collective-permute-start(f32[16,2,4,8,128]{4,3,2,1,0:T(8,128)S(1)} %get-tuple-element.63), channel_id=1, source_target_pairs={{0,8},{1,2},{2,1},{3,4},{4,3},{5,6},{6,5},{7,15},{8,0},{9,10},{10,... | collective-permute-start | bytes 1572872 | tf_op jit(solution)/shard_map/ppermute | solution.py:740
  7.6 7.8 %collective-permute-start.2 = (f32[66,8,128]{2,1,0:T(8,128)S(1)}, f32[66,8,128]{2,1,0:T(8,128)S(1)}, u32[]{:S(2)}, u32[]{:S(2)}) collective-permute-start(f32[66,8,128]{2,1,0:T(8,128)S(1)} %get-tuple-element.54), channel_id=1, source_target_pairs={{0,8},{1,9},{2,10},{3,11},{4,12},{5,13},{6,14},{7,15},{8,0},{9,1},... | collective-permute-start | bytes 811016 | tf_op jit(solution)/shard_map/ppermute | solution.py:740
  9.2 9.3 %collective-permute-start.3 = (f32[66,8,128]{2,1,0:T(8,128)S(1)}, f32[66,8,128]{2,1,0:T(8,128)S(1)}, u32[]{:S(2)}, u32[]{:S(2)}) collective-permute-start(f32[66,8,128]{2,1,0:T(8,128)S(1)} %get-tuple-element.55), channel_id=1, source_target_pairs={{0,32},{1,33},{2,34},{3,35},{4,36},{5,37},{6,38},{7,39},{8,40},{9,... | collective-permute-start | bytes 811016 | tf_op jit(solution)/shard_map/ppermute | solution.py:743
  10.4 14.5 %collective-permute-start.5 = (f32[16,2,4,8,128]{4,3,2,1,0:T(8,128)S(1)}, f32[16,2,4,8,128]{4,3,2,1,0:T(8,128)S(1)}, u32[]{:S(2)}, u32[]{:S(2)}) collective-permute-start(f32[16,2,4,8,128]{4,3,2,1,0:T(8,128)S(1)} %get-tuple-element.64), channel_id=1, source_target_pairs={{0,1},{1,0},{2,3},{3,2},{4,5},{5,4},{6,7},{7,6},{8,9},{9,8},{10,11... | collective-permute-start | bytes 1572872 | tf_op jit(solution)/shard_map/ppermute | solution.py:743
  19.7 17.0 %collective-permute-start.9 = (f32[128,8,128]{2,1,0:T(8,128)S(1)}, f32[128,8,128]{2,1,0:T(8,128)S(1)}, u32[]{:S(2)}, u32[]{:S(2)}) collective-permute-start(f32[128,8,128]{2,1,0:T(8,128)S(1)} %get-tuple-element.72), channel_id=1, source_target_pairs={{0,8},{1,2},{2,1},{3,4},{4,3},{5,6},{6,5},{7,15},{8,0},{9,10},{10,... | collective-permute-start | bytes 1572872 | tf_op jit(solution)/shard_map/ppermute | solution.py:740
  20.1 16.6 %collective-permute-start.10 = (f32[128,8,128]{2,1,0:T(8,128)S(1)}, f32[128,8,128]{2,1,0:T(8,128)S(1)}, u32[]{:S(2)}, u32[]{:S(2)}) collective-permute-start(f32[128,8,128]{2,1,0:T(8,128)S(1)} %get-tuple-element.73), channel_id=1, source_target_pairs={{0,1},{1,0},{2,3},{3,2},{4,5},{5,4},{6,7},{7,6},{8,9},{9,8},{10,11... | collective-permute-start | bytes 1572872 | tf_op jit(solution)/shard_map/ppermute | solution.py:743
  25.8 9.0 %collective-permute-start.6 = (f32[64,8,128]{2,1,0:T(8,128)S(1)}, f32[64,8,128]{2,1,0:T(8,128)S(1)}, u32[]{:S(2)}, u32[]{:S(2)}) collective-permute-start(f32[64,8,128]{2,1,0:T(8,128)S(1)} %get-tuple-element.68), channel_id=1, source_target_pairs={{0,96},{8,104},{16,48},{24,56},{32,0},{40,8},{48,80},{56,88},{64,3... | collective-permute-start | bytes 786440 | tf_op jit(solution)/shard_map/ppermute | solution.py:811
  27.8 7.9 %collective-permute-start.7 = (f32[64,8,128]{2,1,0:T(8,128)S(1)}, f32[64,8,128]{2,1,0:T(8,128)S(1)}, u32[]{:S(2)}, u32[]{:S(2)}) collective-permute-start(f32[64,8,128]{2,1,0:T(8,128)S(1)} %get-tuple-element.70), channel_id=1, source_target_pairs={{0,32},{1,33},{2,34},{3,35},{4,36},{5,37},{6,38},{7,39},{8,16},{9,... | collective-permute-start | bytes 786440 | tf_op jit(solution)/shard_map/ppermute | solution.py:822
  28.0 7.7 %collective-permute-start.8 = (f32[64,8,128]{2,1,0:T(8,128)S(1)}, f32[64,8,128]{2,1,0:T(8,128)S(1)}, u32[]{:S(2)}, u32[]{:S(2)}) collective-permute-start(f32[64,8,128]{2,1,0:T(8,128)S(1)} %get-tuple-element.71), channel_id=1, source_target_pairs={{0,8},{1,9},{2,10},{3,11},{4,12},{5,13},{6,14},{7,15},{8,0},{9,1},... | collective-permute-start | bytes 786440 | tf_op jit(solution)/shard_map/ppermute | solution.py:743

commit v8 on v7

--- a/solution.py
+++ b/solution.py
@@ -182,7 +182,7 @@
 
 def first_messages(
     a_ref, depth_ref, mask_ref, inflow_ref,
-    np_ref, kx_od, kx_ev, ky_od, depth, mask, inflow, sems,
+    np_ref, kx_od, kx_ev, ky_od, ky_ev, depth, mask, inflow, sems,
 ):
     s, i, j, x_up, y_up = place()
     flow = Flow()
@@ -204,6 +204,7 @@
         for n, (src, ref) in enumerate(
             (
                 (own.at[:, pl.ds(jnp.where(is_even(j), 0, BY - 2), 2)], ky_od),
+                (own.at[:, pl.ds(jnp.where(is_even(j), BY - 2, 0), 2)], ky_ev),
                 (own.at[pl.ds(low, 2)], kx_od),
                 (own.at[pl.ds(high, 2)], kx_ev),
             ),
@@ -216,12 +217,9 @@
         c.wait()
 
 
-def more_messages(np_in, depth, kx_ev, np_ref, ky_ev, x_od, x_ev, sem):
+def x_messages(np_in, depth, kx_ev, np_ref, x_od, x_ev):
     s, i, j, x_up, _ = place()
     flow = Flow()
-    own = np_ref.reshape(BX + 4, BY, T, 8, 128).at[pl.ds(2, BX)]
-    message = pltpu.make_async_copy(own.at[:, pl.ds(jnp.where(is_even(j), BY - 2, 0), 2)], ky_ev, sem)
-    message.start()
     for b in range(2):
         y = pl.ds(flow.y[b], 128)
         first = jnp.broadcast_to(depth[0:1, y].astype(f32), (8, 128))
@@ -240,7 +238,6 @@
     loop(BX, one_kx, 4)
     size = 2 * BY * T
     np_ref[pl.ds(jnp.where(is_even(i), (BX + 2) * BY * T, 0), size)] = kx_ev[...]
-    message.wait()
 
 
 def speeds(depth, mask, inflow, ax, ay, rkx, aky, gy, heights, hold, spec, geo):
@@ -743,27 +740,26 @@
         return lax.ppermute(message, AXES, swaps(sizes, AXES.index(axis), 0, 0))
 
     sem = pltpu.SemaphoreType.DMA
-    np5, kx_od, kx_ev, ky_od, depth, mask, spectrum = call(
+    np5, kx_od, kx_ev, ky_od, ky_ev, depth, mask, spectrum = call(
         first_messages,
-        (v(BX + 4, BY, T), v(2, BY, T), v(2, BY, T), v(BX, 2, T), pltpu.VMEM((BS, NY), jnp.int32),
+        (v(BX + 4, BY, T), v(2, BY, T), v(2, BY, T), v(BX, 2, T), v(BX, 2, T), pltpu.VMEM((BS, NY), jnp.int32),
          pltpu.VMEM((BS, NY), jnp.int32), pltpu.VMEM((NKX, NKY), f32)),
         (action, depth_cm, inflow_mask, inflow),
         "hhhh",
-        "v" * 7,
-        [sem((7,))],
+        "v" * 8,
+        [sem((8,))],
         us=0,
         limit=FIRST_LIMIT,
     )
     ky_od = swap_odd(ky_od, "ky", "kx").reshape(ky_tiles, 8, 128)
     kx_ev = swap_even(kx_ev, "kx").reshape(kx_tiles, 8, 128)
     kx_od = swap_odd(kx_od, "kx", "space").reshape(kx_tiles, 8, 128)
-    np3, ky_ev, x_od, x_ev = call(
-        more_messages,
-        (v(padded), v(BX, 2, T), v(4 * BX + 2), v(4 * BX + 2)),
+    np3, x_od, x_ev = call(
+        x_messages,
+        (v(padded), v(4 * BX + 2), v(4 * BX + 2)),
         (np5.reshape(padded, 8, 128), depth, kx_ev),
         "v" * 3,
-        "v" * 4,
-        [sem],
+        "v" * 3,
         alias={0: 0},
         us=0,
     )
@@ -827,7 +823,7 @@
         "v" * 9,
         "v",
         [v(BY * T)],
-        us=4,
+        us=0,
     )
     q, out = call(
         stage_two_x,

time: 38.1 us -> 44.3 us (1.16)
  the two profiles are of different devices: /device:TPU:8 before, /device:TPU:11 now
where the time goes in v8:
time: 44.3 us; the launch traced here: 44.2 us
  Pallas kernels  15.2 us (34%)
  waiting for transfers between devices  14.8 us (33%)
  starting transfers between devices  14.1 us (32%)
    pallas_call x12, Pallas kernels, call(): pl.pallas_call(kernel, out_shape=tuple(outs), in_specs=[whole[c] for c in...  15.2 us
    ppermute x1, waiting for transfers between devices, per_device(): lax.ppermute(kx2_od, AXES, swaps(sizes, 1, 1, 0, True))  10.1 us
    ppermute x4, starting transfers between devices, swap_odd(): lax.ppermute(message, AXES, swaps(sizes, AXES.index(axis), 1, AXES.index(...  8.69 us
    ppermute x1, starting transfers between devices, per_device(): lax.ppermute(kx2_od, AXES, swaps(sizes, 1, 1, 0, True))  3.32 us
    ppermute x4, waiting for transfers between devices, swap_odd(): lax.ppermute(message, AXES, swaps(sizes, AXES.index(axis), 1, AXES.index(...  2.73 us
    ppermute x5, waiting for transfers between devices, swap_even(): return lax.ppermute(message, AXES, swaps(sizes, AXES.index(axis), 0, 0))  2.03 us
    ppermute x1, starting transfers between devices, per_device(): x2 = lax.ppermute(x2, AXES[:2], ring(sizes))  1.28 us
  transfers between devices with their start and end apart: 11, of which 4 were waited for; matrix products, arithmetic and copies ran while one was open for 0% of the time, Pallas kernels for 25%

profile of v8, /device:TPU:11, one launch (start us, length us, event | category | flops | bytes accessed | tf_op | source)
XLA Modules:
  0.0 44.2 jit_solution(17230620794155113034)
XLA Ops:
  0.0 1.8 %first_messages.1 = (f32[20,8,4,8,128]{4,3,2,1,0:T(8,128)S(1)}, f32[2,8,4,8,128]{4,3,2,1,0:T(8,128)S(1)}, f32[2,8,4,8,128]{4,3,2,1,0:T(8,128)S(1)}, f32[16,2,4,8...) custom-call(f32[16,8,16,256]{3,2,1,0:T(8,128)} %a_ref.1, ...), custom_call_target="tpu_custom_call" | custom-call | tf_op jit(solution)/shard_map/first_messages/pallas_call | solution.py:715
  1.8 0.8 %collective-permute-start = (f32[2,8,4,8,128]{4,3,2,1,0:T(8,128)S(1)}, f32[2,8,4,8,128]{4,3,2,1,0:T(8,128)S(1)}, u32[]{:S(2)}, u32[]{:S(2)}) collective-permute-start(f32[2,8,4,8,128]{4,3,2,1,0:T(8,128)S(1)} %get-tuple-element.42), channel_id=1, source_target_pairs={{0,8},{1,9},{2,10},{3,11},{4,12},{5,13},{6,14},{7,15},{8,0},{9,1},... | collective-permute-start | bytes 786440 | tf_op jit(solution)/shard_map/ppermute | solution.py:740
  2.5 2.0 %collective-permute-start.1 = (f32[2,8,4,8,128]{4,3,2,1,0:T(8,128)S(1)}, f32[2,8,4,8,128]{4,3,2,1,0:T(8,128)S(1)}, u32[]{:S(2)}, u32[]{:S(2)}) collective-permute-start(f32[2,8,4,8,128]{4,3,2,1,0:T(8,128)S(1)} %get-tuple-element.53), channel_id=1, source_target_pairs={{0,32},{1,33},{2,34},{3,35},{4,36},{5,37},{6,38},{7,39},{8,16},{9,... | collective-permute-start | bytes 786440 | tf_op jit(solution)/shard_map/ppermute | solution.py:737
  4.5 4.5 %collective-permute-start.4 = (f32[16,2,4,8,128]{4,3,2,1,0:T(8,128)S(1)}, f32[16,2,4,8,128]{4,3,2,1,0:T(8,128)S(1)}, u32[]{:S(2)}, u32[]{:S(2)}) collective-permute-start(f32[16,2,4,8,128]{4,3,2,1,0:T(8,128)S(1)} %get-tuple-element.63), channel_id=1, source_target_pairs={{0,8},{1,2},{2,1},{3,4},{4,3},{5,6},{6,5},{7,15},{8,0},{9,10},{10,... | collective-permute-start | bytes 1572872 | tf_op jit(solution)/shard_map/ppermute | solution.py:737
  9.1 0.0 collective-permute-start.5
  9.1 0.0 collective-permute-done
  9.1 0.2 x_messages.1
  9.3 1.3 %collective-permute-start.2 = (f32[66,8,128]{2,1,0:T(8,128)S(1)}, f32[66,8,128]{2,1,0:T(8,128)S(1)}, u32[]{:S(2)}, u32[]{:S(2)}) collective-permute-start(f32[66,8,128]{2,1,0:T(8,128)S(1)} %get-tuple-element.54), channel_id=1, source_target_pairs={{0,8},{1,9},{2,10},{3,11},{4,12},{5,13},{6,14},{7,15},{8,0},{9,1},... | collective-permute-start | bytes 811016 | tf_op jit(solution)/shard_map/ppermute | solution.py:737
  10.6 0.0 collective-permute-start.3
  10.6 2.9 %speeds.1 = (f32[512,8,128]{2,1,0:T(8,128)S(1)}, f32[512,8,128]{2,1,0:T(8,128)S(1)}, f32[544,8,128]{2,1,0:T(8,128)S(1)}, f32[576,8,128]{2,1,0:T(8,128)S(1)}, f32...) custom-call(s32[16,256]{1,0:T(8,128)S(1)} %get-tuple-element.41.depth, ...), custom_call_target="tpu_custom_call" | custom-call | flops 3000000000 | tf_op jit(solution)/shard_map/speeds/pallas_call | solution.py:715
  13.5 2.1 %stage_one_y.1.p_y = f32[512,8,128]{2,1,0:T(8,128)S(1)} custom-call(f32[640,8,128]{2,1,0:T(8,128)S(1)} %get-tuple-element.43.np_ref.np_in, f32[512,8,128]{2,1,0:T(8,128)S(1)} %get-tuple-element.46.ay), custom_call_target="tpu_custom_call" | custom-call | flops 1000000000 | tf_op jit(solution)/shard_map/stage_one_y/pallas_call | solution.py:715
  15.6 0.0 collective-permute-done.1
  15.6 0.8 %collective-permute-done.2.x_od = f32[66,8,128]{2,1,0:T(8,128)S(1)} collective-permute-done((f32[66,8,128]{2,1,0:T(8,128)S(1)}, f32[66,8,128]{2,1,0:T(8,128)S(1)}, u32[]{:S(2)}, u32[]{:S(2)}) %collective-permute-start.2) | collective-permute-done | bytes 270368 | tf_op jit(solution)/shard_map/ppermute | solution.py:737
  16.5 2.0 %collective-permute-done.3.x_ev = f32[66,8,128]{2,1,0:T(8,128)S(1)} collective-permute-done((f32[66,8,128]{2,1,0:T(8,128)S(1)}, f32[66,8,128]{2,1,0:T(8,128)S(1)}, u32[]{:S(2)}, u32[]{:S(2)}) %collective-permute-start.3) | collective-permute-done | bytes 270368 | tf_op jit(solution)/shard_map/ppermute | solution.py:740
  18.5 1.1 %stage_one_edges.1 = (f32[640,8,128]{2,1,0:T(8,128)S(1)}, f32[256,8,128]{2,1,0:T(8,128)S(1)}, f32[4,8,128]{2,1,0:T(8,128)S(1)}, f32[32,8,128]{2,1,0:T(8,128)S(1)...) custom-call(f32[640,8,128]{2,1,0:T(8,128)S(1)} %get-tuple-element.43, ...), custom_call_target="tpu_custom_call", output_to_operand_aliasing={{0}: (0, {})} | custom-call | tf_op jit(solution)/shard_map/stage_one_edges/pallas_call | solution.py:715
  19.7 0.6 %stage_one_middle.1.p_middle = f32[256,8,128]{2,1,0:T(8,128)S(1)} custom-call(f32[640,8,128]{2,1,0:T(8,128)S(1)} %get-tuple-element.56.np_ref, f32[512,8,128]{2,1,0:T(8,128)S(1)} %stage_one_y.1.p_y, f32[512,8,128]{2,1,0:T(8,128)S(1)} %get-tuple-element.47.ax, f32[544,8,128]{2,1,0:T(8,128)S(1)} %get-tuple-element.48.rkx, ...), custom_call_target="tpu_custom_call" | custom-call | flops 2000000000 | tf_op jit(solution)/shard_map/stage_one_middle/pallas_call | solution.py:715
  20.3 1.9 %collective-permute-done.4 = f32[16,2,4,8,128]{4,3,2,1,0:T(8,128)S(1)} collective-permute-done((f32[16,2,4,8,128]{4,3,2,1,0:T(8,128)S(1)}, f32[16,2,4,8,128]{4,3,2,1,0:T(8,128)S(1)}, u32[]{:S(2)}, u32[]{:S(2)}) %collective-permute-start.4) | collective-permute-done | bytes 524320 | tf_op jit(solution)/shard_map/ppermute | solution.py:737
  22.2 0.0 collective-permute-done.5
  22.2 0.9 %stage_one_rest.1 = (f32[640,8,128]{2,1,0:T(8,128)S(1)}, f32[64,8,128]{2,1,0:T(8,128)S(1)}) custom-call(f32[640,8,128]{2,1,0:T(8,128)S(1)} %get-tuple-element.56.np_ref, f32[256,8,128]{2,1,0:T(8,128)S(1)} %get-tuple-element.57.p_ref, f32[256,8,128]{2,1,0:T(8,128)S(1)} %stage_one_middle.1.p_middle, f32[576,8,128]{2,1,0:T(8,128)S(1)} %get-tuple-element.49.aky, ...), custom_call_target="tpu_custom_call" | custom-call | tf_op jit(solution)/shard_map/stage_one_rest/pallas_call | solution.py:715
  23.1 1.3 %collective-permute-start.6 = (f32[64,8,128]{2,1,0:T(8,128)S(1)}, f32[64,8,128]{2,1,0:T(8,128)S(1)}, u32[]{:S(2)}, u32[]{:S(2)}) collective-permute-start(f32[64,8,128]{2,1,0:T(8,128)S(1)} %get-tuple-element.68), channel_id=1, source_target_pairs={{0,96},{8,104},{16,48},{24,56},{32,0},{40,8},{48,80},{56,88},{64,3... | collective-permute-start | bytes 786440 | tf_op jit(solution)/shard_map/ppermute | solution.py:807
  24.4 0.9 %collective-permute-start.9 = (f32[128,8,128]{2,1,0:T(8,128)S(1)}, f32[128,8,128]{2,1,0:T(8,128)S(1)}, u32[]{:S(2)}, u32[]{:S(2)}) collective-permute-start(f32[128,8,128]{2,1,0:T(8,128)S(1)} %get-tuple-element.72), channel_id=1, source_target_pairs={{0,8},{1,2},{2,1},{3,4},{4,3},{5,6},{6,5},{7,15},{8,0},{9,10},{10,... | collective-permute-start | bytes 1572872 | tf_op jit(solution)/shard_map/ppermute | solution.py:737
  25.3 0.0 collective-permute-start.10
  25.3 0.1 kx_messages.1
  25.4 3.3 %collective-permute-start.7 = (f32[64,8,128]{2,1,0:T(8,128)S(1)}, f32[64,8,128]{2,1,0:T(8,128)S(1)}, u32[]{:S(2)}, u32[]{:S(2)}) collective-permute-start(f32[64,8,128]{2,1,0:T(8,128)S(1)} %get-tuple-element.70), channel_id=1, source_target_pairs={{0,32},{1,33},{2,34},{3,35},{4,36},{5,37},{6,38},{7,39},{8,16},{9,... | collective-permute-start | bytes 786440 | tf_op jit(solution)/shard_map/ppermute | solution.py:818
  28.7 0.0 collective-permute-start.8
  28.7 2.9 %stage_two_inner.1.q_in = f32[512,8,128]{2,1,0:T(8,128)S(1)} custom-call(f32[640,8,128]{2,1,0:T(8,128)S(1)} %get-tuple-element.56.np_ref, f32[640,8,128]{2,1,0:T(8,128)S(1)} %get-tuple-element.66.sp_ref, f32[512,8,128]{2,1,0:T(8,128)S(1)} %get-tuple-element.47.ax, f32[512,8,128]{2,1,0:T(8,128)S(1)} %get-tuple-element.46.ay, ...), custom_call_target="tpu_custom_call" | custom-call | tf_op jit(solution)/shard_map/stage_two_inner/pallas_call | solution.py:715
  31.6 0.0 collective-permute-done.6.x2
  31.6 1.0 %stage_two_x.1 = (f32[512,8,128]{2,1,0:T(8,128)S(1)}, f32[16,8,16,256]{3,2,1,0:T(8,128)}) custom-call(f32[512,8,128]{2,1,0:T(8,128)S(1)} %stage_two_inner.1.q_in, f32[512,8,128]{2,1,0:T(8,128)S(1)} %get-tuple-element.47.ax, f32[32,8,128]{2,1,0:T(8,128)S(1)} %get-tuple-element.67.halo_speed, ...), custom_call_target="tpu_custom_call", output_to_operand_aliasing={{0}: (0, {})} | custom-call | flops 2000000000 | tf_op jit(solution)/shard_map/stage_two_x/pallas_call | solution.py:715
  32.6 10.1 %collective-permute-done.7.kx_od = f32[64,8,128]{2,1,0:T(8,128)S(1)} collective-permute-done((f32[64,8,128]{2,1,0:T(8,128)S(1)}, f32[64,8,128]{2,1,0:T(8,128)S(1)}, u32[]{:S(2)}, u32[]{:S(2)}) %collective-permute-start.7) | collective-permute-done | bytes 262176 | tf_op jit(solution)/shard_map/ppermute | solution.py:818
  42.7 0.0 collective-permute-done.8.kx_ev
  42.7 0.2 stage_two_kx.1.q_ref
  42.9 0.0 collective-permute-done.9.ky_od
  42.9 0.0 collective-permute-done.10.ky_ev
  42.9 1.3 %stage_two_ky.1 = f32[16,8,16,256]{3,2,1,0:T(8,128)} custom-call(f32[512,8,128]{2,1,0:T(8,128)S(1)} %stage_two_kx.1.q_ref, f32[576,8,128]{2,1,0:T(8,128)S(1)} %get-tuple-element.49.aky, f32[4,8,128]{2,1,0:T(8,128)S(1)} %get-tuple-element.62.gy, s32[4,8,128]{2,1,0:T(8,128)S(1)} %get-tuple-element.51.hold_ref, ...), custom_call_target="tpu_custom_call", output_to_operand_aliasing={{}: (7, {})} | custom-call | tf_op jit(solution)/shard_map/stage_two_ky/pallas_call | solution.py:715
Async XLA Ops:
  1.8 7.3 %collective-permute-start = (f32[2,8,4,8,128]{4,3,2,1,0:T(8,128)S(1)}, f32[2,8,4,8,128]{4,3,2,1,0:T(8,128)S(1)}, u32[]{:S(2)}, u32[]{:S(2)}) collective-permute-start(f32[2,8,4,8,128]{4,3,2,1,0:T(8,128)S(1)} %get-tuple-element.42), channel_id=1, source_target_pairs={{0,8},{1,9},{2,10},{3,11},{4,12},{5,13},{6,14},{7,15},{8,0},{9,1},... | collective-permute-start | bytes 786440 | tf_op jit(solution)/shard_map/ppermute | solution.py:740
  2.5 13.1 %collective-permute-start.1 = (f32[2,8,4,8,128]{4,3,2,1,0:T(8,128)S(1)}, f32[2,8,4,8,128]{4,3,2,1,0:T(8,128)S(1)}, u32[]{:S(2)}, u32[]{:S(2)}) collective-permute-start(f32[2,8,4,8,128]{4,3,2,1,0:T(8,128)S(1)} %get-tuple-element.53), channel_id=1, source_target_pairs={{0,32},{1,33},{2,34},{3,35},{4,36},{5,37},{6,38},{7,39},{8,16},{9,... | collective-permute-start | bytes 786440 | tf_op jit(solution)/shard_map/ppermute | solution.py:737
  4.5 17.7 %collective-permute-start.4 = (f32[16,2,4,8,128]{4,3,2,1,0:T(8,128)S(1)}, f32[16,2,4,8,128]{4,3,2,1,0:T(8,128)S(1)}, u32[]{:S(2)}, u32[]{:S(2)}) collective-permute-start(f32[16,2,4,8,128]{4,3,2,1,0:T(8,128)S(1)} %get-tuple-element.63), channel_id=1, source_target_pairs={{0,8},{1,2},{2,1},{3,4},{4,3},{5,6},{6,5},{7,15},{8,0},{9,10},{10,... | collective-permute-start | bytes 1572872 | tf_op jit(solution)/shard_map/ppermute | solution.py:737
  9.1 13.1 %collective-permute-start.5 = (f32[16,2,4,8,128]{4,3,2,1,0:T(8,128)S(1)}, f32[16,2,4,8,128]{4,3,2,1,0:T(8,128)S(1)}, u32[]{:S(2)}, u32[]{:S(2)}) collective-permute-start(f32[16,2,4,8,128]{4,3,2,1,0:T(8,128)S(1)} %get-tuple-element.64), channel_id=1, source_target_pairs={{0,1},{1,0},{2,3},{3,2},{4,5},{5,4},{6,7},{7,6},{8,9},{9,8},{10,11... | collective-permute-start | bytes 1572872 | tf_op jit(solution)/shard_map/ppermute | solution.py:740
  9.3 7.2 %collective-permute-start.2 = (f32[66,8,128]{2,1,0:T(8,128)S(1)}, f32[66,8,128]{2,1,0:T(8,128)S(1)}, u32[]{:S(2)}, u32[]{:S(2)}) collective-permute-start(f32[66,8,128]{2,1,0:T(8,128)S(1)} %get-tuple-element.54), channel_id=1, source_target_pairs={{0,8},{1,9},{2,10},{3,11},{4,12},{5,13},{6,14},{7,15},{8,0},{9,1},... | collective-permute-start | bytes 811016 | tf_op jit(solution)/shard_map/ppermute | solution.py:737
  10.6 7.9 %collective-permute-start.3 = (f32[66,8,128]{2,1,0:T(8,128)S(1)}, f32[66,8,128]{2,1,0:T(8,128)S(1)}, u32[]{:S(2)}, u32[]{:S(2)}) collective-permute-start(f32[66,8,128]{2,1,0:T(8,128)S(1)} %get-tuple-element.55), channel_id=1, source_target_pairs={{0,32},{1,33},{2,34},{3,35},{4,36},{5,37},{6,38},{7,39},{8,40},{9,... | collective-permute-start | bytes 811016 | tf_op jit(solution)/shard_map/ppermute | solution.py:740
  23.1 8.5 %collective-permute-start.6 = (f32[64,8,128]{2,1,0:T(8,128)S(1)}, f32[64,8,128]{2,1,0:T(8,128)S(1)}, u32[]{:S(2)}, u32[]{:S(2)}) collective-permute-start(f32[64,8,128]{2,1,0:T(8,128)S(1)} %get-tuple-element.68), channel_id=1, source_target_pairs={{0,96},{8,104},{16,48},{24,56},{32,0},{40,8},{48,80},{56,88},{64,3... | collective-permute-start | bytes 786440 | tf_op jit(solution)/shard_map/ppermute | solution.py:807
  24.4 18.5 %collective-permute-start.9 = (f32[128,8,128]{2,1,0:T(8,128)S(1)}, f32[128,8,128]{2,1,0:T(8,128)S(1)}, u32[]{:S(2)}, u32[]{:S(2)}) collective-permute-start(f32[128,8,128]{2,1,0:T(8,128)S(1)} %get-tuple-element.72), channel_id=1, source_target_pairs={{0,8},{1,2},{2,1},{3,4},{4,3},{5,6},{6,5},{7,15},{8,0},{9,10},{10,... | collective-permute-start | bytes 1572872 | tf_op jit(solution)/shard_map/ppermute | solution.py:737
  25.3 17.6 %collective-permute-start.10 = (f32[128,8,128]{2,1,0:T(8,128)S(1)}, f32[128,8,128]{2,1,0:T(8,128)S(1)}, u32[]{:S(2)}, u32[]{:S(2)}) collective-permute-start(f32[128,8,128]{2,1,0:T(8,128)S(1)} %get-tuple-element.73), channel_id=1, source_target_pairs={{0,1},{1,0},{2,3},{3,2},{4,5},{5,4},{6,7},{7,6},{8,9},{9,8},{10,11... | collective-permute-start | bytes 1572872 | tf_op jit(solution)/shard_map/ppermute | solution.py:740
  25.4 17.3 %collective-permute-start.7 = (f32[64,8,128]{2,1,0:T(8,128)S(1)}, f32[64,8,128]{2,1,0:T(8,128)S(1)}, u32[]{:S(2)}, u32[]{:S(2)}) collective-permute-start(f32[64,8,128]{2,1,0:T(8,128)S(1)} %get-tuple-element.70), channel_id=1, source_target_pairs={{0,32},{1,33},{2,34},{3,35},{4,36},{5,37},{6,38},{7,39},{8,16},{9,... | collective-permute-start | bytes 786440 | tf_op jit(solution)/shard_map/ppermute | solution.py:818
  28.7 14.0 %collective-permute-start.8 = (f32[64,8,128]{2,1,0:T(8,128)S(1)}, f32[64,8,128]{2,1,0:T(8,128)S(1)}, u32[]{:S(2)}, u32[]{:S(2)}) collective-permute-start(f32[64,8,128]{2,1,0:T(8,128)S(1)} %get-tuple-element.71), channel_id=1, source_target_pairs={{0,8},{1,9},{2,10},{3,11},{4,12},{5,13},{6,14},{7,15},{8,0},{9,1},... | collective-permute-start | bytes 786440 | tf_op jit(solution)/shard_map/ppermute | solution.py:740
